TPU v7x, 32 devices: a whole 2x2x4 slice. The times are simulated.
32 devices in a mesh: ref: 8 (over z, x), win: 4 (over y, core).
Axes of the slice: x: 2, y: 2, z: 4, core: 2. Of those that a mesh axis runs over, the one named last changes fastest.
Arguments:
- queries: bfloat16 [256, 8192], P('ref', 'win'), may hold values from -1 to 1, as said below
- references: bfloat16 [8192, 8192], P('ref', 'win'), may hold values from -1 to 1, as said below
- labels: int32 [64], P('ref'), may hold values from 0 to 7, as said below
- kernel: float32 [9, 8], replicated, may hold values from 0.02 to 0.3
- class_bias: float32 [8], replicated, may hold values from -4 to 4
Outputs:
- ancestry_logprob: float32 [16, 8, 256], P('win', None, 'ref')
Inputs may be any that keep to these rules, and one draw needn't show every extreme that they name: `queries`: every entry is -1 or +1. `references`: every entry is -1 or +1. Every ancestry labels at least one block.
All inputs are finite; a program needn't handle non-finite values.
Results may differ from a plain program's by a relative error of at most 0.0003.
Values may be sent and summed in bfloat16 or wider, within the bound.
No kernel may reach another device: no remote copies, remote signals or barrier semaphores. Data moves between devices by JAX's collectives and lax.ppermute only.
A program may use at most 64 MiB of HBM per device.

v0:
```python
import jax
import jax.numpy as jnp
from jax import lax
from jax.sharding import PartitionSpec as P

S = 512
A = 8
BLOCK = 128
TAPS = 9


neg_floor = -1e30


def with_halo(block, sides, width):
    for axis, dim in sides:
        count = lax.axis_size(axis)
        forward = [(i, i + 1) for i in range(count - 1)]
        backward = [(target, source) for source, target in forward]
        low = lax.ppermute(
            lax.slice_in_dim(block, block.shape[dim] - width, None, axis=dim), axis, forward
        )
        high = lax.ppermute(lax.slice_in_dim(block, 0, width, axis=dim), axis, backward)
        block = jnp.concatenate([low, block, high], axis=dim)
    return block


def pool_rows(query_piece, references, member, windows):
    score_scale = 256.0 / S
    row_count = query_piece.shape[0]
    block_count = references.shape[0] // BLOCK
    results = []
    for window in range(windows):
        query_part = query_piece[:, window * S : (window + 1) * S]
        ref_part = references[:, window * S : (window + 1) * S]
        scores = (
            jnp.einsum("qs,rs->qr", query_part, ref_part, preferred_element_type=jnp.float32)
            * score_scale
        )
        blocks = scores.reshape(row_count, block_count, BLOCK)
        block_peak = jnp.max(blocks, axis=2)
        block_total = jnp.sum(jnp.exp(blocks - block_peak[:, :, None]), axis=2)
        group_peak = jnp.max(jnp.where(member[None], block_peak[:, :, None], neg_floor), axis=1)
        weights = jnp.where(
            member[None],
            block_total[:, :, None] * jnp.exp(block_peak[:, :, None] - group_peak[:, None, :]),
            0.0,
        )
        group_total = jnp.sum(weights, axis=1)
        group_lse = jnp.where(group_total > 0, group_peak + jnp.log(group_total), neg_floor)
        results.append(group_lse.T)
    return jnp.stack(results)


def per_device(queries, references, labels, kernel, class_bias):
    member = labels[:, None] == jnp.arange(A, dtype=jnp.int32)[None, :]
    windows = references.shape[1] // S
    query_count = queries.shape[0]
    partial_value = pool_rows(
        lax.all_gather(queries, "ref", axis=0, tiled=True), references, member, windows
    )
    received = lax.all_to_all(partial_value, "ref", split_axis=2, concat_axis=0, tiled=True)
    stacked = received.reshape(lax.axis_size("ref"), windows, A, query_count)
    highest = jnp.max(stacked, axis=0)
    pooled = highest + jnp.log(jnp.sum(jnp.exp(stacked - highest[None]), axis=0))
    centered = pooled - jnp.mean(pooled, axis=1, keepdims=True)
    padded = with_halo(centered, (("win", 0),), TAPS // 2)
    smoothed = jnp.zeros_like(centered)
    for offset in range(TAPS):
        smoothed = smoothed + kernel[offset][None, :, None] * padded[offset : offset + windows]
    logits = smoothed + class_bias[None, :, None]
    return jax.nn.log_softmax(logits, axis=1)


def solution(mesh):
    in_specs = (P("ref", "win"), P("ref", "win"), P("ref"), P(), P())
    out_specs = P("win", None, "ref")
    return jax.shard_map(
        per_device, mesh=mesh, in_specs=in_specs, out_specs=out_specs, check_vma=False
    )
```

profile of v0, /device:TPU:0, one launch (start us, length us, event | category | flops | bytes accessed | tf_op | source)
XLA Modules:
  0.0 91.1 jit_solution(7309044293743512215)
XLA Ops:
  6.5 0.7 all-gather.2.cloned.1.call-update
  7.3 0.7 iota_compare_fusion
  8.0 44.4 %all-gather.2.cloned.1.call-done = bf16[256,2048]{1,0:T(8,128)(2,1)} async-done(((bf16[32,2048]{1,0:T(8,128)(2,1)}), bf16[256,2048]{1,0:T(8,128)(2,1)}) %all-gather.2.cloned.1.call-update) | async-done | bytes 1048592 | tf_op jit(solution)/shard_map/all_gather | solution.py:60
  52.4 1.9 %fusion.2 = f32[32,8,8,128]{3,1,2,0:T(8,128)S(1)} fusion(bf16[1024,2048]{1,0:T(8,128)(2,1)} %param.6, bf16[256,2048]{1,0:T(8,128)(2,1)} %all-gather.2.cloned.1.call-done), kind=kOutput, calls=%fused_computation.3 | convolution fusion | flops 268697600 | bytes 2359296 | tf_op jit(solution)/shard_map/qs,rs->qr/dot_general | solution.py:37
  54.5 0.3 reduce_max.97
  54.8 0.7 exponential_reduce_fusion
  55.6 1.7 %fusion.3 = f32[32,8,8,128]{3,1,2,0:T(8,128)S(1)} fusion(bf16[1024,2048]{1,0:T(8,128)(2,1)} %param.6, bf16[256,2048]{1,0:T(8,128)(2,1)S(1)} %copy-done), kind=kOutput, calls=%fused_computation.5 | convolution fusion | flops 268697600 | bytes 2359296 | tf_op jit(solution)/shard_map/qs,rs->qr/dot_general | solution.py:37
  57.5 0.3 reduce_max.95
  57.8 0.7 exponential_reduce_fusion.1
  58.6 1.7 %fusion.4 = f32[32,8,8,128]{3,1,2,0:T(8,128)S(1)} fusion(bf16[1024,2048]{1,0:T(8,128)(2,1)} %param.6, bf16[256,2048]{1,0:T(8,128)(2,1)S(1)} %copy-done), kind=kOutput, calls=%fused_computation.7 | convolution fusion | flops 268697600 | bytes 2359296 | tf_op jit(solution)/shard_map/qs,rs->qr/dot_general | solution.py:37
  60.5 0.3 reduce_max.93
  60.8 0.7 exponential_reduce_fusion.2
  61.6 1.7 %fusion.5 = f32[32,8,8,128]{3,1,2,0:T(8,128)S(1)} fusion(bf16[1024,2048]{1,0:T(8,128)(2,1)} %param.6, bf16[256,2048]{1,0:T(8,128)(2,1)S(1)} %copy-done), kind=kOutput, calls=%fused_computation.9 | convolution fusion | flops 268697600 | bytes 2359296 | tf_op jit(solution)/shard_map/qs,rs->qr/dot_general | solution.py:37
  63.5 0.3 reduce_max.91
  63.9 0.7 exponential_reduce_fusion.3
  65.5 0.5 reshape.77
  66.0 9.8 %all_to_all.15 = f32[8,1,1024]{2,1,0:T(1,128)S(1)} all-to-all(f32[8,1,1024]{2,1,0:T(1,128)S(1)} %reshape.77), channel_id=1, replica_groups=mesh['ref'=8,'win'=4] {'ref'}, dimensions={0} | all-to-all | bytes 65536 | tf_op jit(solution)/shard_map/all_to_all | solution.py:62
  75.9 0.5 broadcast.75
  76.4 0.7 reduce.18
  77.1 0.6 reshape.78
  78.3 1.3 %collective-permute-start.1 = (f32[4,8,32]{2,1,0:T(8,128)S(1)}, f32[4,8,32]{2,1,0:T(8,128)S(1)}, u32[]{:S(2)}, u32[]{:S(2)}) collective-permute-start(f32[4,8,32]{2,1,0:T(8,128)S(1)} %broadcast_subtract_fusion), channel_id=1, source_target_pairs={{1,0},{2,1},{3,2},{5,4},{6,5},{7,6},{9,8},{10,9},{11,10},{13,12},{... | collective-permute-start | bytes 12296 | tf_op jit(solution)/shard_map/ppermute | solution.py:23
  79.6 3.0 %collective-permute-start = (f32[4,8,32]{2,1,0:T(8,128)S(1)}, f32[4,8,32]{2,1,0:T(8,128)S(1)}, u32[]{:S(2)}, u32[]{:S(2)}) collective-permute-start(f32[4,8,32]{2,1,0:T(8,128)S(1)} %broadcast_subtract_fusion), channel_id=1, source_target_pairs={{0,1},{1,2},{2,3},{4,5},{5,6},{6,7},{8,9},{9,10},{10,11},{12,13},{... | collective-permute-start | bytes 12296 | tf_op jit(solution)/shard_map/ppermute | solution.py:20
  83.0 0.5 collective-permute-done
  83.6 0.6 fusion.8
  (36 shorter events, 2.8 us)
Async XLA Ops:
  6.5 45.8 %all-gather.2.cloned.1.call-start = ((), (), s32[]{:S(2)}) async-start(), calls=%async_computation.1 | async-start | bytes 1179648 | tf_op jit(solution)/shard_map/all_gather | solution.py:60
  52.4 3.2 %copy-start = (bf16[256,2048]{1,0:T(8,128)(2,1)S(1)}, bf16[256,2048]{1,0:T(8,128)(2,1)}, u32[]{:S(2)}) copy-start(bf16[256,2048]{1,0:T(8,128)(2,1)} %all-gather.2.cloned.1.call-done) | copy-start | bytes 3145732
  63.3 19.4 %copy-start.1 = (f32[9,8]{0,1:T(8,128)S(1)}, f32[9,8]{0,1:T(8,128)}, u32[]{:S(2)}) copy-start(f32[9,8]{0,1:T(8,128)} %param.8) | copy-start | bytes 868
  63.3 20.2 %copy-start.2 = (f32[8]{0:T(128)S(1)}, f32[8]{0:T(128)}, u32[]{:S(2)}) copy-start(f32[8]{0:T(128)} %param.9) | copy-start | bytes 100
  78.3 4.6 %collective-permute-start.1 = (f32[4,8,32]{2,1,0:T(8,128)S(1)}, f32[4,8,32]{2,1,0:T(8,128)S(1)}, u32[]{:S(2)}, u32[]{:S(2)}) collective-permute-start(f32[4,8,32]{2,1,0:T(8,128)S(1)} %broadcast_subtract_fusion), channel_id=1, source_target_pairs={{1,0},{2,1},{3,2},{5,4},{6,5},{7,6},{9,8},{10,9},{11,10},{13,12},{... | collective-permute-start | bytes 12296 | tf_op jit(solution)/shard_map/ppermute | solution.py:23
  79.6 3.9 %collective-permute-start = (f32[4,8,32]{2,1,0:T(8,128)S(1)}, f32[4,8,32]{2,1,0:T(8,128)S(1)}, u32[]{:S(2)}, u32[]{:S(2)}) collective-permute-start(f32[4,8,32]{2,1,0:T(8,128)S(1)} %broadcast_subtract_fusion), channel_id=1, source_target_pairs={{0,1},{1,2},{2,3},{4,5},{5,6},{6,7},{8,9},{9,10},{10,11},{12,13},{... | collective-permute-start | bytes 12296 | tf_op jit(solution)/shard_map/ppermute | solution.py:20
Sparse Core Ops, SparseCore 0:
  9.5 42.8 all-gather.1
where the time goes:
time: 92.1 us; the launch traced here: 91.1 us
  waiting for transfers between devices  45.6 us (50%)
  between operations  13.7 us (15%)
  blocking collectives  9.84 us (11%)
  other arithmetic  6.98 us (8%)
  matrix products  6.97 us (8%)
  starting transfers between devices  4.33 us (5%)
  local copies, waits for them, and re-layouts  3.69 us (4%)
    all_gather x1, waiting for transfers between devices, per_device(): lax.all_gather(queries, 'ref', axis=0, tiled=True)  44.4 us
    all_to_all x1, blocking collectives, per_device(): lax.all_to_all(partial_value, 'ref', split_axis=2, concat_axis=0, tiled=T...  9.84 us
    dot_general x4, matrix products, pool_rows(): jnp.einsum('qs,rs->qr', query_part, ref_part, preferred_element_type=jnp....  6.97 us
    ppermute x1, starting transfers between devices, with_halo(): lax.ppermute(lax.slice_in_dim(block, block.shape[dim] - width, None, axis...  3.03 us
    reduce_sum x4, other arithmetic, pool_rows(): block_total = jnp.sum(jnp.exp(blocks - block_peak[:, :, None]), axis=2)  2.76 us
    unnamed x12, local copies, waits for them, and re-layouts  1.99 us
  transfers between devices with their start and end apart: 3, of which 2 were waited for; matrix products, arithmetic and copies ran while one was open for 1% of the time, Pallas kernels for 0%

commit v1 on v0

v1 whole, which is shorter than its diff:
```python
import functools

import jax
import jax.numpy as jnp
from jax import lax
from jax.experimental import pallas as pl
from jax.experimental.pallas import tpu as pltpu
from jax.sharding import PartitionSpec as P

S = 512
A = 8
BLOCK = 128
TAPS = 9
HALF = TAPS // 2

LOG2E = 1.4426950408889634
SCALE = 256.0 / S

neg_floor = -1e30


def pool_window(scores, labels_ref):
    count = scores.shape[1]
    blocks = scores.shape[0] // BLOCK
    ancestry = lax.broadcasted_iota(jnp.int32, (A, count), 0)
    peaks, totals = [], []
    for b in range(blocks):
        part = scores[b * BLOCK : (b + 1) * BLOCK]
        peak = jnp.max(part, axis=0, keepdims=True)
        totals.append(jnp.sum(jnp.exp2((part - peak) * (SCALE * LOG2E)), axis=0, keepdims=True))
        peaks.append(peak)
    members = [ancestry == labels_ref[b] for b in range(blocks)]
    group_peak = jnp.full((A, count), neg_floor, jnp.float32)
    for b in range(blocks):
        group_peak = jnp.where(members[b], jnp.maximum(group_peak, peaks[b]), group_peak)
    group_total = jnp.zeros((A, count), jnp.float32)
    for b in range(blocks):
        weight = totals[b] * jnp.exp2((peaks[b] - group_peak) * (SCALE * LOG2E))
        group_total = group_total + jnp.where(members[b], weight, 0.0)
    return jnp.where(group_total > 0, SCALE * group_peak + jnp.log(group_total), neg_floor)


def pool_body(labels_ref, refs_ref, *rest):
    query_refs, out_ref = rest[:-1], rest[-1]
    windows = refs_ref.shape[1] // S
    rows = query_refs[0].shape[0]
    pooled = []
    for window in range(windows):
        cols = slice(window * S, (window + 1) * S)
        queries = jnp.concatenate([q[:, cols] for q in query_refs], axis=0)
        scores = lax.dot_general(
            refs_ref[:, cols],
            queries,
            (((1,), (1,)), ((), ())),
            preferred_element_type=jnp.float32,
        )
        pooled.append(pool_window(scores, labels_ref))
    for j in range(len(query_refs)):
        out_ref[j] = jnp.concatenate([p[:, j * rows : (j + 1) * rows] for p in pooled], axis=1)


def pool(labels, refs, queries):
    windows = refs.shape[1] // S
    rows = queries[0].shape[0]
    count = rows * len(queries)
    return pl.pallas_call(
        pool_body,
        out_shape=jax.ShapeDtypeStruct((len(queries), A, windows * rows), jnp.float32),
        in_specs=[pl.BlockSpec(memory_space=pltpu.SMEM)]
        + [pl.BlockSpec(memory_space=pltpu.VMEM)] * (1 + len(queries)),
        out_specs=pl.BlockSpec(memory_space=pltpu.VMEM),
        cost_estimate=pl.CostEstimate(
            flops=2 * refs.size * count, bytes_accessed=2 * refs.size, transcendentals=0
        ),
        compiler_params=pltpu.CompilerParams(vmem_limit_bytes=40 << 20),
        name="pool",
    )(labels, refs, *queries)


def finish_body(win, refs, windows, place_ref, taps_ref, bias_ref, in_ref, out_ref):
    here = place_ref[0]
    rows = out_ref.shape[2]

    def centered(block):
        parts = in_ref[pl.ds(block * refs, refs)]
        highest = jnp.max(parts, axis=0)
        pooled = highest + jnp.log(jnp.sum(jnp.exp(parts - highest[None]), axis=0))
        return pooled - jnp.mean(pooled, axis=0, keepdims=True)

    before = jnp.where(here > 0, centered(jnp.maximum(here - 1, 0)), 0.0)
    after = jnp.where(here < win - 1, centered(jnp.minimum(here + 1, win - 1)), 0.0)
    padded = jnp.concatenate([before, centered(here), after], axis=1)
    width = windows * rows
    total = jnp.zeros((A, width), jnp.float32)
    for tap in range(TAPS):
        start = width + (tap - HALF) * rows
        total = total + taps_ref[:, tap : tap + 1] * padded[:, start : start + width]
    logits = total + bias_ref[...]
    shifted = logits - jnp.max(logits, axis=0, keepdims=True)
    result = shifted - jnp.log(jnp.sum(jnp.exp(shifted), axis=0, keepdims=True))
    for window in range(windows):
        out_ref[window] = result[:, window * rows : (window + 1) * rows]


def finish(received, kernel, class_bias, win, refs, windows, rows):
    place = lax.axis_index("win").astype(jnp.int32).reshape(1)
    return pl.pallas_call(
        functools.partial(finish_body, win, refs, windows),
        out_shape=jax.ShapeDtypeStruct((windows, A, rows), jnp.float32),
        in_specs=[pl.BlockSpec(memory_space=pltpu.SMEM)]
        + [pl.BlockSpec(memory_space=pltpu.VMEM)] * 3,
        out_specs=pl.BlockSpec(memory_space=pltpu.VMEM),
        name="finish",
    )(place, kernel.T, class_bias[:, None], received)


def exchange(block, offset, size):
    return lax.ppermute(block, "ref", [(i, i ^ offset) for i in range(size)])


def gather_queries(queries, size):
    blocks = {0: queries}
    far = [k for k in range(size - 2, 0, -2)]
    for k in far + [1]:
        blocks[k] = exchange(queries, k, size)
    for k in far[::-1]:
        if k == 2:
            blocks[k ^ 1] = exchange(queries, k ^ 1, size)
        else:
            blocks[k ^ 1] = exchange(blocks[k], 1, size)
    return blocks


def per_device(queries, references, labels, kernel, class_bias):
    refs, win = lax.axis_size("ref"), lax.axis_size("win")
    windows = references.shape[1] // S
    rows = queries.shape[0]
    blocks = gather_queries(queries, refs)
    early = [0, 1, 2, 3]
    late = [k for k in range(4, refs)]
    tiles = jnp.concatenate(
        [pool(labels, references, [blocks[k] for k in part]) for part in (early, late)], axis=0
    )
    owner = lax.axis_index("ref") ^ jnp.arange(refs)
    tiles = jnp.take(tiles, owner, axis=0)
    sent = jnp.broadcast_to(tiles[None], (win,) + tiles.shape).reshape((win * refs,) + tiles.shape[1:])
    received = lax.all_to_all(sent, ("win", "ref"), split_axis=0, concat_axis=0, tiled=True)
    return finish(received, kernel, class_bias, win, refs, windows, rows)


def solution(mesh):
    in_specs = (P("ref", "win"), P("ref", "win"), P("ref"), P(), P())
    out_specs = P("win", None, "ref")
    return jax.shard_map(
        per_device, mesh=mesh, in_specs=in_specs, out_specs=out_specs, check_vma=False
    )
```

time: 92.1 us -> 43.5 us (0.47)
  waiting for transfers between devices: 45.6 us -> 15 us
  between operations: 13.7 us -> 0.07 us
  starting transfers between devices: 4.33 us -> 16.2 us
  blocking collectives: 9.84 us -> 0 us
  matrix products: 6.97 us -> 0 us
  other arithmetic: 6.98 us -> 0.1 us
  Pallas kernels: 0 us -> 5.66 us
  local copies, waits for them, and re-layouts: 3.69 us -> 6.29 us
    all_gather x1 -> x0, waiting for transfers between devices: 44.4 us -> none  [per_device(): lax.all_gather(queries, 'ref', axis=0, tiled=True)]
    all_to_all x1 -> x0, blocking collectives: 9.84 us -> none  [per_device(): lax.all_to_all(partial_value, 'ref', split_axis=2, concat_axis=0, tiled=T...]
    ppermute x2 -> x7, waiting for transfers between devices: 0.51 us -> 7.94 us  [exchange(): return lax.ppermute(block, 'ref', [(i, i ^ offset) for i in range(size)])]
    all_to_all x0 -> x1, waiting for transfers between devices: none -> 7.06 us  [per_device(): lax.all_to_all(sent, ('win', 'ref'), split_axis=0, concat_axis=0, tiled=T...]
    dot_general x4 -> x0, matrix products: 6.97 us -> none  [pool_rows(): jnp.einsum('qs,rs->qr', query_part, ref_part, preferred_element_type=jnp....]
    ppermute x2 -> x7, starting transfers between devices: 4.32 us -> 10.9 us  [exchange(): return lax.ppermute(block, 'ref', [(i, i ^ offset) for i in range(size)])]
    pallas_call x0 -> x3, Pallas kernels: none -> 5.66 us  [the longest x2 3.88 us: pool(): pl.pallas_call(pool_body, out_shape=jax.ShapeDtypeStruct((len(queries), A...]
    all_to_all x0 -> x1, starting transfers between devices: none -> 5.28 us  [per_device(): lax.all_to_all(sent, ('win', 'ref'), split_axis=0, concat_axis=0, tiled=T...]
  transfers between devices with their start and end apart: 3 -> 8, of which waited for: 2 -> 3; matrix products, arithmetic and copies ran while one was open for 1% -> 2% of each run, Pallas kernels for 0% -> 4%
where the time goes in v1:
time: 43.5 us; the launch traced here: 43.3 us
  starting transfers between devices  16.2 us (37%)
  waiting for transfers between devices  15 us (34%)
  local copies, waits for them, and re-layouts  6.29 us (14%)
  Pallas kernels  5.66 us (13%)
    ppermute x7, starting transfers between devices, exchange(): return lax.ppermute(block, 'ref', [(i, i ^ offset) for i in range(size)])  10.9 us
    ppermute x7, waiting for transfers between devices, exchange(): return lax.ppermute(block, 'ref', [(i, i ^ offset) for i in range(size)])  7.94 us
    all_to_all x1, waiting for transfers between devices, per_device(): lax.all_to_all(sent, ('win', 'ref'), split_axis=0, concat_axis=0, tiled=T...  7.06 us
    all_to_all x1, starting transfers between devices, per_device(): lax.all_to_all(sent, ('win', 'ref'), split_axis=0, concat_axis=0, tiled=T...  5.28 us
    unnamed x10, local copies, waits for them, and re-layouts  4.4 us
    pallas_call x2, Pallas kernels, pool(): pl.pallas_call(pool_body, out_shape=jax.ShapeDtypeStruct((len(queries), A...  3.88 us
    pallas_call x1, Pallas kernels, finish(): pl.pallas_call(functools.partial(finish_body, win, refs, windows), out_sh...  1.78 us
  transfers between devices with their start and end apart: 8, of which 3 were waited for; matrix products, arithmetic and copies ran while one was open for 2% of the time, Pallas kernels for 4%

profile of v1, /device:TPU:0, one launch (start us, length us, event | category | flops | bytes accessed | tf_op | source)
XLA Modules:
  0.0 43.3 jit_solution(3882278787859075035)
XLA Ops:
  0.0 4.0 %collective-permute-start.3 = (bf16[32,2048]{1,0:T(8,128)(2,1)}, bf16[32,2048]{1,0:T(8,128)(2,1)S(1)}, u32[]{:S(2)}, u32[]{:S(2)}) collective-permute-start(bf16[32,2048]{1,0:T(8,128)(2,1)} %rest_0_.1), channel_id=1, source_target_pairs={{0,16},{4,20},{8,24},{12,28},{16,0},{20,4},{24,8},{28,12},{1,17},{... | collective-permute-start | bytes 393224 | tf_op jit(solution)/shard_map/ppermute | solution.py:118
  4.0 1.3 %collective-permute-start.5 = (bf16[32,2048]{1,0:T(8,128)(2,1)}, bf16[32,2048]{1,0:T(8,128)(2,1)S(1)}, u32[]{:S(2)}, u32[]{:S(2)}) collective-permute-start(bf16[32,2048]{1,0:T(8,128)(2,1)} %rest_0_.1), channel_id=1, source_target_pairs={{0,24},{4,28},{8,16},{12,20},{16,8},{20,12},{24,0},{28,4},{1,25},{... | collective-permute-start | bytes 393224 | tf_op jit(solution)/shard_map/ppermute | solution.py:118
  5.4 1.5 %collective-permute-start = (bf16[32,2048]{1,0:T(8,128)(2,1)}, bf16[32,2048]{1,0:T(8,128)(2,1)S(1)}, u32[]{:S(2)}, u32[]{:S(2)}) collective-permute-start(bf16[32,2048]{1,0:T(8,128)(2,1)} %rest_0_.1), channel_id=1, source_target_pairs={{0,4},{4,0},{8,12},{12,8},{16,20},{20,16},{24,28},{28,24},{1,5},{5... | collective-permute-start | bytes 393224 | tf_op jit(solution)/shard_map/ppermute | solution.py:118
  6.9 0.2 collective-permute-start.1
  7.1 1.8 %collective-permute-start.2 = (bf16[32,2048]{1,0:T(8,128)(2,1)}, bf16[32,2048]{1,0:T(8,128)(2,1)S(1)}, u32[]{:S(2)}, u32[]{:S(2)}) collective-permute-start(bf16[32,2048]{1,0:T(8,128)(2,1)} %rest_0_.1), channel_id=1, source_target_pairs={{0,12},{4,8},{8,4},{12,0},{16,28},{20,24},{24,20},{28,16},{1,13},{... | collective-permute-start | bytes 393224 | tf_op jit(solution)/shard_map/ppermute | solution.py:118
  8.9 5.3 %collective-permute-done.3.rest_0_ = bf16[32,2048]{1,0:T(8,128)(2,1)S(1)} collective-permute-done((bf16[32,2048]{1,0:T(8,128)(2,1)}, bf16[32,2048]{1,0:T(8,128)(2,1)S(1)}, u32[]{:S(2)}, u32[]{:S(2)}) %collective-permute-start.3) | collective-permute-done | bytes 131104 | tf_op jit(solution)/shard_map/ppermute | solution.py:118
  14.2 1.8 %collective-permute-start.4 = (bf16[32,2048]{1,0:T(8,128)(2,1)S(1)}, bf16[32,2048]{1,0:T(8,128)(2,1)S(1)}, u32[]{:S(2)}, u32[]{:S(2)}) collective-permute-start(bf16[32,2048]{1,0:T(8,128)(2,1)S(1)} %collective-permute-done.3.rest_0_), channel_id=1, source_target_pairs={{0,4},{4,0},{8,12},{12,8},{16,20},{20,16},{24,28},{28,24},{1,5},{5... | collective-permute-start | bytes 393224 | tf_op jit(solution)/shard_map/ppermute | solution.py:118
  16.1 0.0 collective-permute-done.5.rest_2_
  16.1 0.2 collective-permute-start.6
  16.3 0.0 collective-permute-done.1.rest_2_
  16.3 2.5 %collective-permute-done.2.rest_3_ = bf16[32,2048]{1,0:T(8,128)(2,1)S(1)} collective-permute-done((bf16[32,2048]{1,0:T(8,128)(2,1)}, bf16[32,2048]{1,0:T(8,128)(2,1)S(1)}, u32[]{:S(2)}, u32[]{:S(2)}) %collective-permute-start.2) | collective-permute-done | bytes 131104 | tf_op jit(solution)/shard_map/ppermute | solution.py:118
  18.9 2.2 %copy-done = bf16[1024,2048]{1,0:T(8,128)(2,1)S(1)} copy-done((bf16[1024,2048]{1,0:T(8,128)(2,1)S(1)}, bf16[1024,2048]{1,0:T(8,128)(2,1)}, u32[]{:S(2)}) %copy-start) | copy-done | bytes 4194328
  21.1 0.9 %copy-done.1 = bf16[32,2048]{1,0:T(8,128)(2,1)S(1)} copy-done((bf16[32,2048]{1,0:T(8,128)(2,1)S(1)}, bf16[32,2048]{1,0:T(8,128)(2,1)}, u32[]{:S(2)}) %copy-start.1) | copy-done | bytes 131096
  22.0 0.7 %copy-done.2 = s32[8]{0:T(128)S(1)} copy-done((s32[8]{0:T(128)S(1)}, s32[8]{0:T(128)}, u32[]{:S(2)}) %copy-start.2) | copy-done | bytes 56
  22.6 1.9 %pool.2 = f32[4,8,128]{2,1,0:T(8,128)S(1)} custom-call(s32[8]{0:T(128)S(1)} %copy-done.2, bf16[1024,2048]{1,0:T(8,128)(2,1)S(1)} %copy-done, bf16[32,2048]{1,0:T(8,128)(2,1)S(1)} %copy-done.1, bf16[32,2048]{1,0:T(8,128)(2,1)S(1)} %collective-permute-done.rest_1_, bf16[32,2048]{1,0:T(8,128)(2,1)S(1)} %collective-permute-done.1.rest_2_, ...), custom_call_target="tpu_custom_call" | custom-call | flops 536870912 | bytes 4194304 | tf_op jit(solution)/shard_map/pool/pallas_call | solution.py:66
  24.6 1.9 %pool.3 = f32[4,8,128]{2,1,0:T(8,128)S(1)} custom-call(s32[8]{0:T(128)S(1)} %copy-done.2, bf16[1024,2048]{1,0:T(8,128)(2,1)S(1)} %copy-done, bf16[32,2048]{1,0:T(8,128)(2,1)S(1)} %collective-permute-done.3.rest_0_, bf16[32,2048]{1,0:T(8,128)(2,1)S(1)} %collective-permute-done.4.rest_1_, bf16[32,2048]{1,0:T(8,128)(2,1)S(1)} %collective-permute-done.5.rest_2_, ...), custom_call_target="tpu_custom_call" | custom-call | flops 536870912 | bytes 4194304 | tf_op jit(solution)/shard_map/pool/pallas_call | solution.py:66
  26.5 0.6 %gather_fusion = f32[8,8,128]{2,1,0:T(8,128)S(1)} fusion(f32[8,8,128]{2,1,0:T(8,128)S(1)} %pad_maximum_fusion, s32[1024]{0:T(1024)S(1)} %pad_clamp_fusion), kind=kCustom, calls=%fused_computation | custom fusion | bytes 65568 | tf_op jit(solution)/shard_map/jit(_take)/gather | solution.py:145
  27.1 0.1 broadcast_select_fusion
  27.2 0.7 %broadcast_in_dim.22 = f32[4,8,8,128]{3,2,1,0:T(8,128)} broadcast(f32[8,8,128]{2,1,0:T(8,128)S(1)} %broadcast_select_fusion), dimensions={1,2,3} | broadcast | bytes 163840 | tf_op jit(solution)/shard_map/broadcast_in_dim | solution.py:146
  27.8 5.3 %all-to-all-start = ((f32[32,8,128]{2,1,0:T(8,128)}), f32[32,8,128]{2,1,0:T(8,128)S(1)}, u32[]{:S(2)}, u32[]{:S(2)}) async-start(f32[32,8,128]{2,1,0:T(8,128)} %bitcast.4), calls=%async_computation | async-start | bytes 262144 | tf_op jit(solution)/shard_map/all_to_all | solution.py:147
  33.1 0.7 %copy.6.bias_ref = f32[8,1]{1,0:T(8,128)} copy(f32[8,1]{0,1:T(1,128)S(1)} %bitcast.7) | data formatting | bytes 64 | tf_op jit(solution)/shard_map/broadcast_in_dim | solution.py:114
  33.8 7.1 %all-to-all-done.in_ref = f32[32,8,128]{2,1,0:T(8,128)S(1)} async-done(((f32[32,8,128]{2,1,0:T(8,128)}), f32[32,8,128]{2,1,0:T(8,128)S(1)}, u32[]{:S(2)}, u32[]{:S(2)}) %all-to-all-start) | async-done | bytes 131104 | tf_op jit(solution)/shard_map/all_to_all | solution.py:147
  40.9 0.6 %copy-done.3 = f32[32,8,128]{2,1,0:T(8,128)} copy-done((f32[32,8,128]{2,1,0:T(8,128)}, f32[32,8,128]{2,1,0:T(8,128)S(1)}, u32[]{:S(2)}) %copy-start.3) | copy-done | bytes 131096
  41.5 1.8 %finish.1 = f32[4,8,32]{2,1,0:T(8,128)} custom-call(s32[1]{0:T(128)} %bitcast.place_ref, f32[8,9]{1,0:T(8,128)} %bitcast.6, f32[8,1]{1,0:T(8,128)} %copy.6.bias_ref, f32[32,8,128]{2,1,0:T(8,128)} %copy-done.3), custom_call_target="tpu_custom_call" | custom-call | tf_op jit(solution)/shard_map/finish/pallas_call | solution.py:107
  (13 shorter events, 0.0 us)
Async XLA Ops:
  0.0 14.2 %collective-permute-start.3 = (bf16[32,2048]{1,0:T(8,128)(2,1)}, bf16[32,2048]{1,0:T(8,128)(2,1)S(1)}, u32[]{:S(2)}, u32[]{:S(2)}) collective-permute-start(bf16[32,2048]{1,0:T(8,128)(2,1)} %rest_0_.1), channel_id=1, source_target_pairs={{0,16},{4,20},{8,24},{12,28},{16,0},{20,4},{24,8},{28,12},{1,17},{... | collective-permute-start | bytes 393224 | tf_op jit(solution)/shard_map/ppermute | solution.py:118
  4.0 12.0 %collective-permute-start.5 = (bf16[32,2048]{1,0:T(8,128)(2,1)}, bf16[32,2048]{1,0:T(8,128)(2,1)S(1)}, u32[]{:S(2)}, u32[]{:S(2)}) collective-permute-start(bf16[32,2048]{1,0:T(8,128)(2,1)} %rest_0_.1), channel_id=1, source_target_pairs={{0,24},{4,28},{8,16},{12,20},{16,8},{20,12},{24,0},{28,4},{1,25},{... | collective-permute-start | bytes 393224 | tf_op jit(solution)/shard_map/ppermute | solution.py:118
  5.4 10.9 %collective-permute-start = (bf16[32,2048]{1,0:T(8,128)(2,1)}, bf16[32,2048]{1,0:T(8,128)(2,1)S(1)}, u32[]{:S(2)}, u32[]{:S(2)}) collective-permute-start(bf16[32,2048]{1,0:T(8,128)(2,1)} %rest_0_.1), channel_id=1, source_target_pairs={{0,4},{4,0},{8,12},{12,8},{16,20},{20,16},{24,28},{28,24},{1,5},{5... | collective-permute-start | bytes 393224 | tf_op jit(solution)/shard_map/ppermute | solution.py:118
  6.9 9.4 %collective-permute-start.1 = (bf16[32,2048]{1,0:T(8,128)(2,1)}, bf16[32,2048]{1,0:T(8,128)(2,1)S(1)}, u32[]{:S(2)}, u32[]{:S(2)}) collective-permute-start(bf16[32,2048]{1,0:T(8,128)(2,1)} %rest_0_.1), channel_id=1, source_target_pairs={{0,8},{4,12},{8,0},{12,4},{16,24},{20,28},{24,16},{28,20},{1,9},{5... | collective-permute-start | bytes 393224 | tf_op jit(solution)/shard_map/ppermute | solution.py:118
  7.1 11.8 %collective-permute-start.2 = (bf16[32,2048]{1,0:T(8,128)(2,1)}, bf16[32,2048]{1,0:T(8,128)(2,1)S(1)}, u32[]{:S(2)}, u32[]{:S(2)}) collective-permute-start(bf16[32,2048]{1,0:T(8,128)(2,1)} %rest_0_.1), channel_id=1, source_target_pairs={{0,12},{4,8},{8,4},{12,0},{16,28},{20,24},{24,20},{28,16},{1,13},{... | collective-permute-start | bytes 393224 | tf_op jit(solution)/shard_map/ppermute | solution.py:118
  14.2 10.3 %collective-permute-start.4 = (bf16[32,2048]{1,0:T(8,128)(2,1)S(1)}, bf16[32,2048]{1,0:T(8,128)(2,1)S(1)}, u32[]{:S(2)}, u32[]{:S(2)}) collective-permute-start(bf16[32,2048]{1,0:T(8,128)(2,1)S(1)} %collective-permute-done.3.rest_0_), channel_id=1, source_target_pairs={{0,4},{4,0},{8,12},{12,8},{16,20},{20,16},{24,28},{28,24},{1,5},{5... | collective-permute-start | bytes 393224 | tf_op jit(solution)/shard_map/ppermute | solution.py:118
  16.1 8.5 %collective-permute-start.6 = (bf16[32,2048]{1,0:T(8,128)(2,1)S(1)}, bf16[32,2048]{1,0:T(8,128)(2,1)S(1)}, u32[]{:S(2)}, u32[]{:S(2)}) collective-permute-start(bf16[32,2048]{1,0:T(8,128)(2,1)S(1)} %collective-permute-done.5.rest_2_), channel_id=1, source_target_pairs={{0,4},{4,0},{8,12},{12,8},{16,20},{20,16},{24,28},{28,24},{1,5},{5... | collective-permute-start | bytes 393224 | tf_op jit(solution)/shard_map/ppermute | solution.py:118
  16.3 16.9 %copy-start.4 = (f32[8]{0:T(128)S(1)}, f32[8]{0:T(128)}, u32[]{:S(2)}) copy-start(f32[8]{0:T(128)} %param.9) | copy-start | bytes 100
  18.9 2.2 %copy-start = (bf16[1024,2048]{1,0:T(8,128)(2,1)S(1)}, bf16[1024,2048]{1,0:T(8,128)(2,1)}, u32[]{:S(2)}) copy-start(bf16[1024,2048]{1,0:T(8,128)(2,1)} %refs_ref.3) | copy-start | bytes 12582916
  21.1 0.9 %copy-start.1 = (bf16[32,2048]{1,0:T(8,128)(2,1)S(1)}, bf16[32,2048]{1,0:T(8,128)(2,1)}, u32[]{:S(2)}) copy-start(bf16[32,2048]{1,0:T(8,128)(2,1)} %rest_0_.1) | copy-start | bytes 393220
  22.0 0.7 %copy-start.2 = (s32[8]{0:T(128)S(1)}, s32[8]{0:T(128)}, u32[]{:S(2)}) copy-start(s32[8]{0:T(128)} %labels_ref.3) | copy-start | bytes 100
  27.8 13.0 %all-to-all-start = ((f32[32,8,128]{2,1,0:T(8,128)}), f32[32,8,128]{2,1,0:T(8,128)S(1)}, u32[]{:S(2)}, u32[]{:S(2)}) async-start(f32[32,8,128]{2,1,0:T(8,128)} %bitcast.4), calls=%async_computation | async-start | bytes 262144 | tf_op jit(solution)/shard_map/all_to_all | solution.py:147
  40.9 0.7 %copy-start.3 = (f32[32,8,128]{2,1,0:T(8,128)}, f32[32,8,128]{2,1,0:T(8,128)S(1)}, u32[]{:S(2)}) copy-start(f32[32,8,128]{2,1,0:T(8,128)S(1)} %all-to-all-done.in_ref) | copy-start | bytes 393220

commit v2 on v1

--- a/solution.py
+++ b/solution.py
@@ -17,6 +17,9 @@
 SCALE = 256.0 / S
 
 neg_floor = -1e30
+narrow = jnp.float8_e4m3fn
+vmem = pl.BlockSpec(memory_space=pltpu.VMEM)
+smem = pl.BlockSpec(memory_space=pltpu.SMEM)
 
 
 def pool_window(scores, labels_ref):
@@ -40,8 +43,45 @@
     return jnp.where(group_total > 0, SCALE * group_peak + jnp.log(group_total), neg_floor)
 
 
-def pool_body(labels_ref, refs_ref, *rest):
-    query_refs, out_ref = rest[:-1], rest[-1]
+def stage_body(refs_ref, queries_ref, out_ref, mine_ref, chunks, sems):
+    count, step = chunks.shape[0], chunks.shape[1]
+    copies = [
+        pltpu.make_async_copy(refs_ref.at[pl.ds(c * step, step)], chunks.at[c], sems.at[c])
+        for c in range(count)
+    ]
+    copies.append(pltpu.make_async_copy(queries_ref, mine_ref, sems.at[count]))
+    for copy in copies:
+        copy.start()
+    for c in range(count):
+        copies[c].wait()
+        out_ref[c * step : (c + 1) * step] = chunks[c].astype(narrow)
+    copies[count].wait()
+
+
+def stage(references, queries):
+    step = 128
+    count = references.shape[0] // step
+    return pl.pallas_call(
+        stage_body,
+        out_shape=(
+            pltpu.VMEM(references.shape, narrow),
+            pltpu.VMEM(queries.shape, queries.dtype),
+        ),
+        in_specs=[pl.BlockSpec(memory_space=pl.ANY)] * 2,
+        out_specs=(vmem, vmem),
+        scratch_shapes=[
+            pltpu.VMEM((count, step, references.shape[1]), references.dtype),
+            pltpu.SemaphoreType.DMA((count + 1,)),
+        ],
+        cost_estimate=pl.CostEstimate(
+            flops=references.size, bytes_accessed=3 * references.size, transcendentals=0
+        ),
+        compiler_params=pltpu.CompilerParams(vmem_limit_bytes=40 << 20),
+        name="stage",
+    )(*(pltpu.with_memory_space_constraint(x, pltpu.HBM) for x in (references, queries)))
+
+
+def pool_tiles(labels_ref, refs_ref, query_refs):
     windows = refs_ref.shape[1] // S
     rows = query_refs[0].shape[0]
     pooled = []
@@ -50,31 +90,74 @@
         queries = jnp.concatenate([q[:, cols] for q in query_refs], axis=0)
         scores = lax.dot_general(
             refs_ref[:, cols],
-            queries,
+            queries.astype(narrow),
             (((1,), (1,)), ((), ())),
             preferred_element_type=jnp.float32,
         )
         pooled.append(pool_window(scores, labels_ref))
-    for j in range(len(query_refs)):
-        out_ref[j] = jnp.concatenate([p[:, j * rows : (j + 1) * rows] for p in pooled], axis=1)
+    return [
+        jnp.concatenate([p[:, j * rows : (j + 1) * rows] for p in pooled], axis=1)
+        for j in range(len(query_refs))
+    ]
+
+
+def pool_body(labels_ref, refs_ref, *rest):
+    out_ref = rest[-1]
+    for j, tile in enumerate(pool_tiles(labels_ref, refs_ref, rest[:-1])):
+        out_ref[j] = tile
+
+
+def last_body(late, groups, here_ref, labels_ref, refs_ref, *rest):
+    out_ref = rest[-1]
+    here = here_ref[0]
+
+    def place(offset, tile):
+        for v in range(out_ref.shape[0]):
+            out_ref[v, here ^ offset] = tile
+
+    for ref, offsets in zip(rest[len(late) : -1], groups, strict=True):
+        for j, offset in enumerate(offsets):
+            place(offset, ref[j])
+    for offset, tile in zip(late, pool_tiles(labels_ref, refs_ref, rest[: len(late)]), strict=True):
+        place(offset, tile)
+
+
+def pool_cost(refs, queries):
+    count = sum(q.shape[0] for q in queries)
+    return pl.CostEstimate(
+        flops=2 * refs.size * count,
+        bytes_accessed=refs.size,
+        transcendentals=refs.size // S * count,
+    )
 
 
 def pool(labels, refs, queries):
     windows = refs.shape[1] // S
     rows = queries[0].shape[0]
-    count = rows * len(queries)
     return pl.pallas_call(
         pool_body,
-        out_shape=jax.ShapeDtypeStruct((len(queries), A, windows * rows), jnp.float32),
-        in_specs=[pl.BlockSpec(memory_space=pltpu.SMEM)]
-        + [pl.BlockSpec(memory_space=pltpu.VMEM)] * (1 + len(queries)),
-        out_specs=pl.BlockSpec(memory_space=pltpu.VMEM),
-        cost_estimate=pl.CostEstimate(
-            flops=2 * refs.size * count, bytes_accessed=2 * refs.size, transcendentals=0
-        ),
+        out_shape=pltpu.VMEM((len(queries), A, windows * rows), jnp.float32),
+        in_specs=[smem] + [vmem] * (1 + len(queries)),
+        out_specs=vmem,
+        cost_estimate=pool_cost(refs, queries),
         compiler_params=pltpu.CompilerParams(vmem_limit_bytes=40 << 20),
         name="pool",
     )(labels, refs, *queries)
+
+
+def pool_last(labels, refs, queries, late, tiles, groups, win, count):
+    windows = refs.shape[1] // S
+    rows = queries[0].shape[0]
+    here = lax.axis_index("ref").astype(jnp.int32).reshape(1)
+    return pl.pallas_call(
+        functools.partial(last_body, late, groups),
+        out_shape=pltpu.VMEM((win, count, A, windows * rows), jnp.float32),
+        in_specs=[smem, smem] + [vmem] * (1 + len(queries) + len(tiles)),
+        out_specs=vmem,
+        cost_estimate=pool_cost(refs, queries),
+        compiler_params=pltpu.CompilerParams(vmem_limit_bytes=40 << 20),
+        name="pool_last",
+    )(here, labels, refs, *queries, *tiles)
 
 
 def finish_body(win, refs, windows, place_ref, taps_ref, bias_ref, in_ref, out_ref):
@@ -95,7 +178,8 @@
     for tap in range(TAPS):
         start = width + (tap - HALF) * rows
         total = total + taps_ref[:, tap : tap + 1] * padded[:, start : start + width]
-    logits = total + bias_ref[...]
+    same = lax.broadcasted_iota(jnp.int32, (A, A), 0) == lax.broadcasted_iota(jnp.int32, (A, A), 1)
+    logits = total + jnp.sum(jnp.where(same, bias_ref[...], 0.0), axis=1, keepdims=True)
     shifted = logits - jnp.max(logits, axis=0, keepdims=True)
     result = shifted - jnp.log(jnp.sum(jnp.exp(shifted), axis=0, keepdims=True))
     for window in range(windows):
@@ -104,30 +188,59 @@
 
 def finish(received, kernel, class_bias, win, refs, windows, rows):
     place = lax.axis_index("win").astype(jnp.int32).reshape(1)
+    operands = [
+        pltpu.with_memory_space_constraint(x, pltpu.VMEM)
+        for x in (kernel.T, class_bias[None, :], received)
+    ]
     return pl.pallas_call(
         functools.partial(finish_body, win, refs, windows),
         out_shape=jax.ShapeDtypeStruct((windows, A, rows), jnp.float32),
-        in_specs=[pl.BlockSpec(memory_space=pltpu.SMEM)]
-        + [pl.BlockSpec(memory_space=pltpu.VMEM)] * 3,
-        out_specs=pl.BlockSpec(memory_space=pltpu.VMEM),
+        in_specs=[smem] + [vmem] * 3,
+        out_specs=vmem,
         name="finish",
-    )(place, kernel.T, class_bias[:, None], received)
+    )(place, *operands)
 
 
 def exchange(block, offset, size):
     return lax.ppermute(block, "ref", [(i, i ^ offset) for i in range(size)])
 
 
-def gather_queries(queries, size):
-    blocks = {0: queries}
-    far = [k for k in range(size - 2, 0, -2)]
-    for k in far + [1]:
-        blocks[k] = exchange(queries, k, size)
-    for k in far[::-1]:
+def tie_body(*refs):
+    pass
+
+
+def tie(value, *others):
+    return pl.pallas_call(
+        tie_body,
+        out_shape=pltpu.VMEM(value.shape, value.dtype),
+        in_specs=[vmem] * (1 + len(others)),
+        out_specs=vmem,
+        input_output_aliases={0: 0},
+        compiler_params=pltpu.CompilerParams(vmem_limit_bytes=40 << 20),
+        name="tie",
+    )(value, *others)
+
+
+def gather_queries(queries, mine, size, early):
+    bits = [1 << b for b in range(1, size.bit_length() - 1)][::-1]
+    blocks = {0: mine}
+    for bit in bits[:-1] + [1]:
+        blocks[bit] = exchange(mine if bit <= 2 else queries, bit, size)
+    blocks[2] = exchange(tie(mine, blocks[1]), 2, size)
+    pooled = early(blocks)
+    even = [0]
+    for bit in bits:
+        for k in list(even):
+            if k:
+                blocks[k | bit] = exchange(blocks[k], bit, size)
+            even.append(k | bit)
+    for k in even[1:]:
         if k == 2:
-            blocks[k ^ 1] = exchange(queries, k ^ 1, size)
+            blocks[k | 1] = exchange(blocks[1], k, size)
         else:
-            blocks[k ^ 1] = exchange(blocks[k], 1, size)
+            blocks[k | 1] = exchange(blocks[k], 1, size)
+        if (k // 2) % 4 == 0:
+            early(blocks)
     return blocks
 
 
@@ -135,15 +248,18 @@
     refs, win = lax.axis_size("ref"), lax.axis_size("win")
     windows = references.shape[1] // S
     rows = queries.shape[0]
-    blocks = gather_queries(queries, refs)
-    early = [0, 1, 2, 3]
-    late = [k for k in range(4, refs)]
-    tiles = jnp.concatenate(
-        [pool(labels, references, [blocks[k] for k in part]) for part in (early, late)], axis=0
-    )
-    owner = lax.axis_index("ref") ^ jnp.arange(refs)
-    tiles = jnp.take(tiles, owner, axis=0)
-    sent = jnp.broadcast_to(tiles[None], (win,) + tiles.shape).reshape((win * refs,) + tiles.shape[1:])
+    staged, mine = stage(references, queries)
+    tiles, groups = [], []
+
+    def early(blocks):
+        groups.append([k for k in blocks if k not in sum(groups, [])])
+        tiles.append(pool(labels, staged, [blocks[k] for k in groups[-1]]))
+        return tiles[-1]
+
+    blocks = gather_queries(queries, mine, refs, early)
+    late = [k for k in blocks if k not in sum(groups, [])]
+    sent = pool_last(labels, staged, [blocks[k] for k in late], late, tiles, groups, win, refs)
+    sent = sent.reshape((win * refs,) + sent.shape[2:])
     received = lax.all_to_all(sent, ("win", "ref"), split_axis=0, concat_axis=0, tiled=True)
     return finish(received, kernel, class_bias, win, refs, windows, rows)
 

time: 43.5 us -> 38.6 us (0.89)
  local copies, waits for them, and re-layouts: 6.29 us -> 0.03 us
  Pallas kernels: 5.66 us -> 6.68 us
  starting transfers between devices: 16.2 us -> 17.1 us
  waiting for transfers between devices: 15 us -> 14.5 us
    unnamed x10 -> x7, local copies, waits for them, and re-layouts: 4.4 us -> 0.03 us
    pallas_call x2 -> x4, Pallas kernels: 3.88 us -> 5.81 us  [the longest x1 2.25 us: stage(): pl.pallas_call(stage_body, out_shape=(pltpu.VMEM(references.shape, narrow...]
    broadcast_in_dim x2 -> x0, local copies, waits for them, and re-layouts: 1.33 us -> none  [the longest x1 0.67 us: finish(): class_bias[:, None]]
    ppermute x7, waiting for transfers between devices: 7.94 us -> 6.77 us  [exchange(): return lax.ppermute(block, 'ref', [(i, i ^ offset) for i in range(size)])]
    pallas_call x1, Pallas kernels: 1.78 us -> 0.88 us  [finish(): pl.pallas_call(functools.partial(finish_body, win, refs, windows), out_sh...]
    all_to_all x1, waiting for transfers between devices: 7.06 us -> 7.74 us  [per_device(): lax.all_to_all(sent, ('win', 'ref'), split_axis=0, concat_axis=0, tiled=T...]
    gather x1 -> x0, local copies, waits for them, and re-layouts: 0.56 us -> none  [per_device(): tiles = jnp.take(tiles, owner, axis=0)]
    ppermute x7, starting transfers between devices: 10.9 us -> 11.4 us  [exchange(): return lax.ppermute(block, 'ref', [(i, i ^ offset) for i in range(size)])]
  transfers between devices with their start and end apart: 8 -> 8, of which waited for: 3 -> 5; matrix products, arithmetic and copies ran while one was open for 2% -> 0% of each run, Pallas kernels for 4% -> 10%
where the time goes in v2:
time: 38.6 us; the launch traced here: 38.4 us
  starting transfers between devices  17.1 us (44%)
  waiting for transfers between devices  14.5 us (38%)
  Pallas kernels  6.68 us (17%)
    ppermute x7, starting transfers between devices, exchange(): return lax.ppermute(block, 'ref', [(i, i ^ offset) for i in range(size)])  11.4 us
    all_to_all x1, waiting for transfers between devices, per_device(): lax.all_to_all(sent, ('win', 'ref'), split_axis=0, concat_axis=0, tiled=T...  7.74 us
    ppermute x7, waiting for transfers between devices, exchange(): return lax.ppermute(block, 'ref', [(i, i ^ offset) for i in range(size)])  6.77 us
    all_to_all x1, starting transfers between devices, per_device(): lax.all_to_all(sent, ('win', 'ref'), split_axis=0, concat_axis=0, tiled=T...  5.71 us
    pallas_call x1, Pallas kernels, stage(): pl.pallas_call(stage_body, out_shape=(pltpu.VMEM(references.shape, narrow...  2.25 us
    pallas_call x1, Pallas kernels, pool_last(): pl.pallas_call(functools.partial(last_body, late, groups), out_shape=pltp...  2.11 us
    pallas_call x1, Pallas kernels, pool(): pl.pallas_call(pool_body, out_shape=pltpu.VMEM((len(queries), A, windows...  1.45 us
    pallas_call x1, Pallas kernels, finish(): pl.pallas_call(functools.partial(finish_body, win, refs, windows), out_sh...  0.88 us
  transfers between devices with their start and end apart: 8, of which 5 were waited for; matrix products, arithmetic and copies ran while one was open for 0% of the time, Pallas kernels for 10%

profile of v2, /device:TPU:0, one launch (start us, length us, event | category | flops | bytes accessed | tf_op | source)
XLA Modules:
  0.0 38.4 jit_solution(15864880500055522615)
XLA Ops:
  0.0 4.0 %collective-permute-start = (bf16[32,2048]{1,0:T(8,128)(2,1)}, bf16[32,2048]{1,0:T(8,128)(2,1)S(1)}, u32[]{:S(2)}, u32[]{:S(2)}) collective-permute-start(bf16[32,2048]{1,0:T(8,128)(2,1)} %queries_ref.1), channel_id=1, source_target_pairs={{0,16},{4,20},{8,24},{12,28},{16,0},{20,4},{24,8},{28,12},{1,17},{... | collective-permute-start | bytes 393224 | tf_op jit(solution)/shard_map/ppermute | solution.py:205
  4.0 2.3 %stage.1 = (f8e4m3fn[1024,2048]{1,0:T(32,128)(4,1)S(1)}, bf16[32,2048]{1,0:T(8,128)(2,1)S(1)}) custom-call(bf16[1024,2048]{1,0:T(8,128)(2,1)} %refs_ref.1, bf16[32,2048]{1,0:T(8,128)(2,1)} %queries_ref.1), custom_call_target="tpu_custom_call" | custom-call | flops 2097152 | bytes 6291456 | tf_op jit(solution)/shard_map/stage/pallas_call | solution.py:64
  6.3 0.0 copy-start
  6.3 0.0 copy-start.2
  6.3 1.6 %collective-permute-start.3 = (bf16[32,2048]{1,0:T(8,128)(2,1)S(1)}, bf16[32,2048]{1,0:T(8,128)(2,1)S(1)}, u32[]{:S(2)}, u32[]{:S(2)}) collective-permute-start(bf16[32,2048]{1,0:T(8,128)(2,1)S(1)} %get-tuple-element.8.rest_0_), channel_id=1, source_target_pairs={{0,4},{4,0},{8,12},{12,8},{16,20},{20,16},{24,28},{28,24},{1,5},{5... | collective-permute-start | bytes 393224 | tf_op jit(solution)/shard_map/ppermute | solution.py:205
  7.9 2.7 %collective-permute-done.rest_1_ = bf16[32,2048]{1,0:T(8,128)(2,1)S(1)} collective-permute-done((bf16[32,2048]{1,0:T(8,128)(2,1)}, bf16[32,2048]{1,0:T(8,128)(2,1)S(1)}, u32[]{:S(2)}, u32[]{:S(2)}) %collective-permute-start) | collective-permute-done | bytes 131104 | tf_op jit(solution)/shard_map/ppermute | solution.py:205
  10.6 0.8 %collective-permute-start.1 = (bf16[32,2048]{1,0:T(8,128)(2,1)S(1)}, bf16[32,2048]{1,0:T(8,128)(2,1)S(1)}, u32[]{:S(2)}, u32[]{:S(2)}) collective-permute-start(bf16[32,2048]{1,0:T(8,128)(2,1)S(1)} %collective-permute-done.rest_1_), channel_id=1, source_target_pairs={{0,8},{4,12},{8,0},{12,4},{16,24},{20,28},{24,16},{28,20},{1,9},{5... | collective-permute-start | bytes 393224 | tf_op jit(solution)/shard_map/ppermute | solution.py:205
  11.4 0.0 collective-permute-done.3.refs_1_.rest_2_
  11.4 1.5 %collective-permute-start.6 = (bf16[32,2048]{1,0:T(8,128)(2,1)S(1)}, bf16[32,2048]{1,0:T(8,128)(2,1)S(1)}, u32[]{:S(2)}, u32[]{:S(2)}) collective-permute-start(bf16[32,2048]{1,0:T(8,128)(2,1)S(1)} %tie.1), channel_id=1, source_target_pairs={{0,8},{4,12},{8,0},{12,4},{16,24},{20,28},{24,16},{28,20},{1,9},{5... | collective-permute-start | bytes 393224 | tf_op jit(solution)/shard_map/ppermute | solution.py:205
  12.9 0.6 %collective-permute-start.4 = (bf16[32,2048]{1,0:T(8,128)(2,1)S(1)}, bf16[32,2048]{1,0:T(8,128)(2,1)S(1)}, u32[]{:S(2)}, u32[]{:S(2)}) collective-permute-start(bf16[32,2048]{1,0:T(8,128)(2,1)S(1)} %collective-permute-done.3.refs_1_.rest_2_), channel_id=1, source_target_pairs={{0,8},{4,12},{8,0},{12,4},{16,24},{20,28},{24,16},{28,20},{1,9},{5... | collective-permute-start | bytes 393224 | tf_op jit(solution)/shard_map/ppermute | solution.py:205
  13.5 1.5 %collective-permute-start.2 = (bf16[32,2048]{1,0:T(8,128)(2,1)S(1)}, bf16[32,2048]{1,0:T(8,128)(2,1)S(1)}, u32[]{:S(2)}, u32[]{:S(2)}) collective-permute-start(bf16[32,2048]{1,0:T(8,128)(2,1)S(1)} %collective-permute-done.rest_1_), channel_id=1, source_target_pairs={{0,4},{4,0},{8,12},{12,8},{16,20},{20,16},{24,28},{28,24},{1,5},{5... | collective-permute-start | bytes 393224 | tf_op jit(solution)/shard_map/ppermute | solution.py:205
  15.0 2.0 %collective-permute-done.1.rest_0_ = bf16[32,2048]{1,0:T(8,128)(2,1)S(1)} collective-permute-done((bf16[32,2048]{1,0:T(8,128)(2,1)S(1)}, bf16[32,2048]{1,0:T(8,128)(2,1)S(1)}, u32[]{:S(2)}, u32[]{:S(2)}) %collective-permute-start.1) | collective-permute-done | bytes 131104 | tf_op jit(solution)/shard_map/ppermute | solution.py:205
  17.0 1.4 %collective-permute-start.5 = (bf16[32,2048]{1,0:T(8,128)(2,1)S(1)}, bf16[32,2048]{1,0:T(8,128)(2,1)S(1)}, u32[]{:S(2)}, u32[]{:S(2)}) collective-permute-start(bf16[32,2048]{1,0:T(8,128)(2,1)S(1)} %collective-permute-done.1.rest_0_), channel_id=1, source_target_pairs={{0,4},{4,0},{8,12},{12,8},{16,20},{20,16},{24,28},{28,24},{1,5},{5... | collective-permute-start | bytes 393224 | tf_op jit(solution)/shard_map/ppermute | solution.py:205
  18.4 1.1 %collective-permute-done.6.rest_3_ = bf16[32,2048]{1,0:T(8,128)(2,1)S(1)} collective-permute-done((bf16[32,2048]{1,0:T(8,128)(2,1)S(1)}, bf16[32,2048]{1,0:T(8,128)(2,1)S(1)}, u32[]{:S(2)}, u32[]{:S(2)}) %collective-permute-start.6) | collective-permute-done | bytes 131104 | tf_op jit(solution)/shard_map/ppermute | solution.py:205
  19.5 0.0 copy-done.1
  19.5 1.4 %pool.1.rest_4_ = f32[4,8,128]{2,1,0:T(8,128)S(1)} custom-call(s32[8]{0:T(128)S(1)} %copy-done.1, f8e4m3fn[1024,2048]{1,0:T(32,128)(4,1)S(1)} %get-tuple-element.7.refs_ref, bf16[32,2048]{1,0:T(8,128)(2,1)S(1)} %get-tuple-element.8.rest_0_, bf16[32,2048]{1,0:T(8,128)(2,1)S(1)} %collective-permute-done.rest_1_, ...), custom_call_target="tpu_custom_call" | custom-call | flops 536870912 | bytes 2097152 | tf_op jit(solution)/shard_map/pool/pallas_call | solution.py:137
  20.9 0.0 collective-permute-done.4.rest_2_
  20.9 0.0 collective-permute-done.2.rest_1_
  20.9 1.0 %collective-permute-done.5.rest_3_ = bf16[32,2048]{1,0:T(8,128)(2,1)S(1)} collective-permute-done((bf16[32,2048]{1,0:T(8,128)(2,1)S(1)}, bf16[32,2048]{1,0:T(8,128)(2,1)S(1)}, u32[]{:S(2)}, u32[]{:S(2)}) %collective-permute-start.5) | collective-permute-done | bytes 131104 | tf_op jit(solution)/shard_map/ppermute | solution.py:205
  22.0 2.1 %pool_last.1 = f32[4,8,8,128]{3,2,1,0:T(8,128)} custom-call(s32[1]{0:T(128)} %bitcast.3.here_ref, s32[8]{0:T(128)S(1)} %copy-done.1, f8e4m3fn[1024,2048]{1,0:T(32,128)(4,1)S(1)} %get-tuple-element.7.refs_ref, bf16[32,2048]{1,0:T(8,128)(2,1)S(1)} %collective-permute-done.1.rest_0_, bf16[32,2048]{1,0:T(8,128)(2,1)S(1)} %collective-permute-done.2.rest_1_, ...), custom_call_target="tpu_custom_call" | custom-call | flops 536870912 | bytes 2097152 | tf_op jit(solution)/shard_map/pool_last/pallas_call | solution.py:152
  24.1 5.7 %all-to-all-start = ((f32[32,8,128]{2,1,0:T(8,128)}), f32[32,8,128]{2,1,0:T(8,128)S(1)}, u32[]{:S(2)}, u32[]{:S(2)}) async-start(f32[32,8,128]{2,1,0:T(8,128)} %bitcast.4), calls=%async_computation | async-start | bytes 262144 | tf_op jit(solution)/shard_map/all_to_all | solution.py:263
  29.8 7.7 %all-to-all-done.in_ref = f32[32,8,128]{2,1,0:T(8,128)S(1)} async-done(((f32[32,8,128]{2,1,0:T(8,128)}), f32[32,8,128]{2,1,0:T(8,128)S(1)}, u32[]{:S(2)}, u32[]{:S(2)}) %all-to-all-start) | async-done | bytes 131104 | tf_op jit(solution)/shard_map/all_to_all | solution.py:263
  37.5 0.0 copy-done
  37.5 0.9 %finish.1 = f32[4,8,32]{2,1,0:T(8,128)} custom-call(s32[1]{0:T(128)} %bitcast.place_ref, f32[8,9]{1,0:T(8,128)S(1)} %bitcast.5, f32[1,8]{1,0:T(1,128)S(1)} %bitcast.6, f32[32,8,128]{2,1,0:T(8,128)S(1)} %all-to-all-done.in_ref), custom_call_target="tpu_custom_call" | custom-call | tf_op jit(solution)/shard_map/finish/pallas_call | solution.py:195
  (4 shorter events, 0.0 us)
Async XLA Ops:
  0.0 19.5 %copy-start.1 = (s32[8]{0:T(128)S(1)}, s32[8]{0:T(128)}, u32[]{:S(2)}) copy-start(s32[8]{0:T(128)} %labels_ref.3) | copy-start | bytes 100
  0.0 10.5 %collective-permute-start = (bf16[32,2048]{1,0:T(8,128)(2,1)}, bf16[32,2048]{1,0:T(8,128)(2,1)S(1)}, u32[]{:S(2)}, u32[]{:S(2)}) collective-permute-start(bf16[32,2048]{1,0:T(8,128)(2,1)} %queries_ref.1), channel_id=1, source_target_pairs={{0,16},{4,20},{8,24},{12,28},{16,0},{20,4},{24,8},{28,12},{1,17},{... | collective-permute-start | bytes 393224 | tf_op jit(solution)/shard_map/ppermute | solution.py:205
  6.3 31.2 %copy-start = (f32[9,8]{0,1:T(8,128)S(1)}, f32[9,8]{0,1:T(8,128)}, u32[]{:S(2)}) copy-start(f32[9,8]{0,1:T(8,128)} %param.8) | copy-start | bytes 868
  6.3 31.2 %copy-start.2 = (f32[8]{0:T(128)S(1)}, f32[8]{0:T(128)}, u32[]{:S(2)}) copy-start(f32[8]{0:T(128)} %param.9) | copy-start | bytes 100
  6.3 5.1 %collective-permute-start.3 = (bf16[32,2048]{1,0:T(8,128)(2,1)S(1)}, bf16[32,2048]{1,0:T(8,128)(2,1)S(1)}, u32[]{:S(2)}, u32[]{:S(2)}) collective-permute-start(bf16[32,2048]{1,0:T(8,128)(2,1)S(1)} %get-tuple-element.8.rest_0_), channel_id=1, source_target_pairs={{0,4},{4,0},{8,12},{12,8},{16,20},{20,16},{24,28},{28,24},{1,5},{5... | collective-permute-start | bytes 393224 | tf_op jit(solution)/shard_map/ppermute | solution.py:205
  10.6 6.4 %collective-permute-start.1 = (bf16[32,2048]{1,0:T(8,128)(2,1)S(1)}, bf16[32,2048]{1,0:T(8,128)(2,1)S(1)}, u32[]{:S(2)}, u32[]{:S(2)}) collective-permute-start(bf16[32,2048]{1,0:T(8,128)(2,1)S(1)} %collective-permute-done.rest_1_), channel_id=1, source_target_pairs={{0,8},{4,12},{8,0},{12,4},{16,24},{20,28},{24,16},{28,20},{1,9},{5... | collective-permute-start | bytes 393224 | tf_op jit(solution)/shard_map/ppermute | solution.py:205
  11.4 8.0 %collective-permute-start.6 = (bf16[32,2048]{1,0:T(8,128)(2,1)S(1)}, bf16[32,2048]{1,0:T(8,128)(2,1)S(1)}, u32[]{:S(2)}, u32[]{:S(2)}) collective-permute-start(bf16[32,2048]{1,0:T(8,128)(2,1)S(1)} %tie.1), channel_id=1, source_target_pairs={{0,8},{4,12},{8,0},{12,4},{16,24},{20,28},{24,16},{28,20},{1,9},{5... | collective-permute-start | bytes 393224 | tf_op jit(solution)/shard_map/ppermute | solution.py:205
  12.9 8.0 %collective-permute-start.4 = (bf16[32,2048]{1,0:T(8,128)(2,1)S(1)}, bf16[32,2048]{1,0:T(8,128)(2,1)S(1)}, u32[]{:S(2)}, u32[]{:S(2)}) collective-permute-start(bf16[32,2048]{1,0:T(8,128)(2,1)S(1)} %collective-permute-done.3.refs_1_.rest_2_), channel_id=1, source_target_pairs={{0,8},{4,12},{8,0},{12,4},{16,24},{20,28},{24,16},{28,20},{1,9},{5... | collective-permute-start | bytes 393224 | tf_op jit(solution)/shard_map/ppermute | solution.py:205
  13.5 7.4 %collective-permute-start.2 = (bf16[32,2048]{1,0:T(8,128)(2,1)S(1)}, bf16[32,2048]{1,0:T(8,128)(2,1)S(1)}, u32[]{:S(2)}, u32[]{:S(2)}) collective-permute-start(bf16[32,2048]{1,0:T(8,128)(2,1)S(1)} %collective-permute-done.rest_1_), channel_id=1, source_target_pairs={{0,4},{4,0},{8,12},{12,8},{16,20},{20,16},{24,28},{28,24},{1,5},{5... | collective-permute-start | bytes 393224 | tf_op jit(solution)/shard_map/ppermute | solution.py:205
  17.0 5.0 %collective-permute-start.5 = (bf16[32,2048]{1,0:T(8,128)(2,1)S(1)}, bf16[32,2048]{1,0:T(8,128)(2,1)S(1)}, u32[]{:S(2)}, u32[]{:S(2)}) collective-permute-start(bf16[32,2048]{1,0:T(8,128)(2,1)S(1)} %collective-permute-done.1.rest_0_), channel_id=1, source_target_pairs={{0,4},{4,0},{8,12},{12,8},{16,20},{20,16},{24,28},{28,24},{1,5},{5... | collective-permute-start | bytes 393224 | tf_op jit(solution)/shard_map/ppermute | solution.py:205
  24.1 13.5 %all-to-all-start = ((f32[32,8,128]{2,1,0:T(8,128)}), f32[32,8,128]{2,1,0:T(8,128)S(1)}, u32[]{:S(2)}, u32[]{:S(2)}) async-start(f32[32,8,128]{2,1,0:T(8,128)} %bitcast.4), calls=%async_computation | async-start | bytes 262144 | tf_op jit(solution)/shard_map/all_to_all | solution.py:263

commit v3 on v2

--- a/solution.py
+++ b/solution.py
@@ -12,6 +12,7 @@
 BLOCK = 128
 TAPS = 9
 HALF = TAPS // 2
+LAST = 4
 
 LOG2E = 1.4426950408889634
 SCALE = 256.0 / S
@@ -20,6 +21,7 @@
 narrow = jnp.float8_e4m3fn
 vmem = pl.BlockSpec(memory_space=pltpu.VMEM)
 smem = pl.BlockSpec(memory_space=pltpu.SMEM)
+anywhere = pl.BlockSpec(memory_space=pl.ANY)
 
 
 def pool_window(scores, labels_ref):
@@ -67,7 +69,7 @@
             pltpu.VMEM(references.shape, narrow),
             pltpu.VMEM(queries.shape, queries.dtype),
         ),
-        in_specs=[pl.BlockSpec(memory_space=pl.ANY)] * 2,
+        in_specs=[anywhere] * 2,
         out_specs=(vmem, vmem),
         scratch_shapes=[
             pltpu.VMEM((count, step, references.shape[1]), references.dtype),
@@ -213,34 +215,31 @@
     return pl.pallas_call(
         tie_body,
         out_shape=pltpu.VMEM(value.shape, value.dtype),
-        in_specs=[vmem] * (1 + len(others)),
-        out_specs=vmem,
+        in_specs=[anywhere] * (1 + len(others)),
+        out_specs=anywhere,
         input_output_aliases={0: 0},
-        compiler_params=pltpu.CompilerParams(vmem_limit_bytes=40 << 20),
         name="tie",
-    )(value, *others)
+    )(value, *(pltpu.with_memory_space_constraint(x, pltpu.VMEM) for x in others))
 
 
 def gather_queries(queries, mine, size, early):
-    bits = [1 << b for b in range(1, size.bit_length() - 1)][::-1]
+    far = [k for k in range(4, size, 2)]
     blocks = {0: mine}
-    for bit in bits[:-1] + [1]:
-        blocks[bit] = exchange(mine if bit <= 2 else queries, bit, size)
-    blocks[2] = exchange(tie(mine, blocks[1]), 2, size)
-    pooled = early(blocks)
-    even = [0]
-    for bit in bits:
-        for k in list(even):
-            if k:
-                blocks[k | bit] = exchange(blocks[k], bit, size)
-            even.append(k | bit)
-    for k in even[1:]:
-        if k == 2:
-            blocks[k | 1] = exchange(blocks[1], k, size)
-        else:
-            blocks[k | 1] = exchange(blocks[k], 1, size)
-        if (k // 2) % 4 == 0:
-            early(blocks)
+    for k in [k for k in far if k & 2]:
+        blocks[k] = exchange(queries, k, size)
+    blocks[1] = exchange(mine, 1, size)
+    blocks[2] = exchange(mine, 2, size)
+    first = [0, 1, 2, far[-1]]
+    pooled = early({k: blocks[k] for k in first})
+    for k in [k for k in far if not k & 2]:
+        blocks[k] = exchange(blocks[k | 2], 2, size)
+    for k in far:
+        source = tie(blocks[k], pooled) if k == 4 else blocks[k]
+        blocks[k | 1] = exchange(source, 1, size)
+    blocks[3] = exchange(blocks[1], 2, size)
+    rest = [k for k in blocks if k not in first]
+    for k in range(0, len(rest) - LAST, LAST):
+        early({j: blocks[j] for j in rest[k : k + LAST]})
     return blocks
 
 
@@ -252,8 +251,8 @@
     tiles, groups = [], []
 
     def early(blocks):
-        groups.append([k for k in blocks if k not in sum(groups, [])])
-        tiles.append(pool(labels, staged, [blocks[k] for k in groups[-1]]))
+        groups.append(list(blocks))
+        tiles.append(pool(labels, staged, list(blocks.values())))
         return tiles[-1]
 
     blocks = gather_queries(queries, mine, refs, early)

time: 38.6 us -> 37.4 us (0.969)
  starting transfers between devices: 17.1 us -> 14.8 us
  waiting for transfers between devices: 14.5 us -> 15.6 us
    all_to_all x1, starting transfers between devices: 5.71 us -> 3.66 us  [per_device(): lax.all_to_all(sent, ('win', 'ref'), split_axis=0, concat_axis=0, tiled=T...]
    ppermute x7, waiting for transfers between devices: 6.77 us -> 7.91 us  [exchange(): return lax.ppermute(block, 'ref', [(i, i ^ offset) for i in range(size)])]
where the time goes in v3:
time: 37.4 us; the launch traced here: 37.2 us
  waiting for transfers between devices  15.6 us (42%)
  starting transfers between devices  14.8 us (40%)
  Pallas kernels  6.69 us (18%)
    ppermute x7, starting transfers between devices, exchange(): return lax.ppermute(block, 'ref', [(i, i ^ offset) for i in range(size)])  11.2 us
    ppermute x7, waiting for transfers between devices, exchange(): return lax.ppermute(block, 'ref', [(i, i ^ offset) for i in range(size)])  7.91 us
    all_to_all x1, waiting for transfers between devices, per_device(): lax.all_to_all(sent, ('win', 'ref'), split_axis=0, concat_axis=0, tiled=T...  7.74 us
    all_to_all x1, starting transfers between devices, per_device(): lax.all_to_all(sent, ('win', 'ref'), split_axis=0, concat_axis=0, tiled=T...  3.66 us
    pallas_call x1, Pallas kernels, stage(): pl.pallas_call(stage_body, out_shape=(pltpu.VMEM(references.shape, narrow...  2.25 us
    pallas_call x1, Pallas kernels, pool_last(): pl.pallas_call(functools.partial(last_body, late, groups), out_shape=pltp...  2.11 us
    pallas_call x1, Pallas kernels, pool(): pl.pallas_call(pool_body, out_shape=pltpu.VMEM((len(queries), A, windows...  1.45 us
    pallas_call x1, Pallas kernels, finish(): pl.pallas_call(functools.partial(finish_body, win, refs, windows), out_sh...  0.88 us
  transfers between devices with their start and end apart: 8, of which 5 were waited for; matrix products, arithmetic and copies ran while one was open for 0% of the time, Pallas kernels for 10%

profile of v3, /device:TPU:0, one launch (start us, length us, event | category | flops | bytes accessed | tf_op | source)
XLA Modules:
  0.0 37.2 jit_solution(18058334687683638708)
XLA Ops:
  0.0 5.0 %collective-permute-start = (bf16[32,2048]{1,0:T(8,128)(2,1)}, bf16[32,2048]{1,0:T(8,128)(2,1)S(1)}, u32[]{:S(2)}, u32[]{:S(2)}) collective-permute-start(bf16[32,2048]{1,0:T(8,128)(2,1)} %queries_ref.1), channel_id=1, source_target_pairs={{0,24},{4,28},{8,16},{12,20},{16,8},{20,12},{24,0},{28,4},{1,25},{... | collective-permute-start | bytes 393224 | tf_op jit(solution)/shard_map/ppermute | solution.py:207
  5.1 2.3 %stage.1 = (f8e4m3fn[1024,2048]{1,0:T(32,128)(4,1)S(1)}, bf16[32,2048]{1,0:T(8,128)(2,1)S(1)}) custom-call(bf16[1024,2048]{1,0:T(8,128)(2,1)} %refs_ref.1, bf16[32,2048]{1,0:T(8,128)(2,1)} %queries_ref.1), custom_call_target="tpu_custom_call" | custom-call | flops 2097152 | bytes 6291456 | tf_op jit(solution)/shard_map/stage/pallas_call | solution.py:66
  7.3 0.0 copy-start
  7.3 0.0 copy-start.2
  7.3 1.6 %collective-permute-start.2 = (bf16[32,2048]{1,0:T(8,128)(2,1)S(1)}, bf16[32,2048]{1,0:T(8,128)(2,1)S(1)}, u32[]{:S(2)}, u32[]{:S(2)}) collective-permute-start(bf16[32,2048]{1,0:T(8,128)(2,1)S(1)} %get-tuple-element.8.rest_0_), channel_id=1, source_target_pairs={{0,4},{4,0},{8,12},{12,8},{16,20},{20,16},{24,28},{28,24},{1,5},{5... | collective-permute-start | bytes 393224 | tf_op jit(solution)/shard_map/ppermute | solution.py:207
  8.9 0.0 collective-permute-start.3
  8.9 0.0 collective-permute-done.rest_3_
  8.9 2.4 %collective-permute-start.1 = (bf16[32,2048]{1,0:T(8,128)(2,1)S(1)}, bf16[32,2048]{1,0:T(8,128)(2,1)S(1)}, u32[]{:S(2)}, u32[]{:S(2)}) collective-permute-start(bf16[32,2048]{1,0:T(8,128)(2,1)S(1)} %collective-permute-done.rest_3_), channel_id=1, source_target_pairs={{0,8},{4,12},{8,0},{12,4},{16,24},{20,28},{24,16},{28,20},{1,9},{5... | collective-permute-start | bytes 393224 | tf_op jit(solution)/shard_map/ppermute | solution.py:207
  11.3 1.5 %collective-permute-start.5 = (bf16[32,2048]{1,0:T(8,128)(2,1)S(1)}, bf16[32,2048]{1,0:T(8,128)(2,1)S(1)}, u32[]{:S(2)}, u32[]{:S(2)}) collective-permute-start(bf16[32,2048]{1,0:T(8,128)(2,1)S(1)} %collective-permute-done.rest_3_), channel_id=1, source_target_pairs={{0,4},{4,0},{8,12},{12,8},{16,20},{20,16},{24,28},{28,24},{1,5},{5... | collective-permute-start | bytes 393224 | tf_op jit(solution)/shard_map/ppermute | solution.py:207
  12.8 0.0 collective-permute-done.2.rest_1_
  12.8 0.0 collective-permute-start.6
  12.8 2.6 %collective-permute-done.3.rest_2_ = bf16[32,2048]{1,0:T(8,128)(2,1)S(1)} collective-permute-done((bf16[32,2048]{1,0:T(8,128)(2,1)S(1)}, bf16[32,2048]{1,0:T(8,128)(2,1)S(1)}, u32[]{:S(2)}, u32[]{:S(2)}) %collective-permute-start.3) | collective-permute-done | bytes 131104 | tf_op jit(solution)/shard_map/ppermute | solution.py:207
  15.3 0.0 copy-done.1
  15.3 1.5 %pool.1.refs_1_.rest_4_ = f32[4,8,128]{2,1,0:T(8,128)S(1)} custom-call(s32[8]{0:T(128)S(1)} %copy-done.1, f8e4m3fn[1024,2048]{1,0:T(32,128)(4,1)S(1)} %get-tuple-element.7.refs_ref, bf16[32,2048]{1,0:T(8,128)(2,1)S(1)} %get-tuple-element.8.rest_0_, bf16[32,2048]{1,0:T(8,128)(2,1)S(1)} %collective-permute-done.2.rest_1_, ...), custom_call_target="tpu_custom_call" | custom-call | flops 536870912 | bytes 2097152 | tf_op jit(solution)/shard_map/pool/pallas_call | solution.py:139
  16.8 1.0 %collective-permute-done.1.rest_0_ = bf16[32,2048]{1,0:T(8,128)(2,1)S(1)} collective-permute-done((bf16[32,2048]{1,0:T(8,128)(2,1)S(1)}, bf16[32,2048]{1,0:T(8,128)(2,1)S(1)}, u32[]{:S(2)}, u32[]{:S(2)}) %collective-permute-start.1) | collective-permute-done | bytes 131104 | tf_op jit(solution)/shard_map/ppermute | solution.py:207
  17.8 0.7 %collective-permute-start.4 = (bf16[32,2048]{1,0:T(8,128)(2,1)S(1)}, bf16[32,2048]{1,0:T(8,128)(2,1)S(1)}, u32[]{:S(2)}, u32[]{:S(2)}) collective-permute-start(bf16[32,2048]{1,0:T(8,128)(2,1)S(1)} %tie.1), channel_id=1, source_target_pairs={{0,4},{4,0},{8,12},{12,8},{16,20},{20,16},{24,28},{28,24},{1,5},{5... | collective-permute-start | bytes 393224 | tf_op jit(solution)/shard_map/ppermute | solution.py:207
  18.5 0.7 %collective-permute-done.6.rest_3_ = bf16[32,2048]{1,0:T(8,128)(2,1)S(1)} collective-permute-done((bf16[32,2048]{1,0:T(8,128)(2,1)S(1)}, bf16[32,2048]{1,0:T(8,128)(2,1)S(1)}, u32[]{:S(2)}, u32[]{:S(2)}) %collective-permute-start.6) | collective-permute-done | bytes 131104 | tf_op jit(solution)/shard_map/ppermute | solution.py:207
  19.2 0.0 collective-permute-done.5.rest_2_
  19.2 3.6 %collective-permute-done.4.rest_1_ = bf16[32,2048]{1,0:T(8,128)(2,1)S(1)} collective-permute-done((bf16[32,2048]{1,0:T(8,128)(2,1)S(1)}, bf16[32,2048]{1,0:T(8,128)(2,1)S(1)}, u32[]{:S(2)}, u32[]{:S(2)}) %collective-permute-start.4) | collective-permute-done | bytes 131104 | tf_op jit(solution)/shard_map/ppermute | solution.py:207
  22.8 2.1 %pool_last.1 = f32[4,8,8,128]{3,2,1,0:T(8,128)} custom-call(s32[1]{0:T(128)} %bitcast.3.here_ref, s32[8]{0:T(128)S(1)} %copy-done.1, f8e4m3fn[1024,2048]{1,0:T(32,128)(4,1)S(1)} %get-tuple-element.7.refs_ref, bf16[32,2048]{1,0:T(8,128)(2,1)S(1)} %collective-permute-done.1.rest_0_, bf16[32,2048]{1,0:T(8,128)(2,1)S(1)} %collective-permute-done.4.rest_1_, ...), custom_call_target="tpu_custom_call" | custom-call | flops 536870912 | bytes 2097152 | tf_op jit(solution)/shard_map/pool_last/pallas_call | solution.py:154
  24.9 3.7 %all-to-all-start = ((f32[32,8,128]{2,1,0:T(8,128)}), f32[32,8,128]{2,1,0:T(8,128)S(1)}, u32[]{:S(2)}, u32[]{:S(2)}) async-start(f32[32,8,128]{2,1,0:T(8,128)} %bitcast.4), calls=%async_computation | async-start | bytes 262144 | tf_op jit(solution)/shard_map/all_to_all | solution.py:262
  28.6 7.7 %all-to-all-done.in_ref = f32[32,8,128]{2,1,0:T(8,128)S(1)} async-done(((f32[32,8,128]{2,1,0:T(8,128)}), f32[32,8,128]{2,1,0:T(8,128)S(1)}, u32[]{:S(2)}, u32[]{:S(2)}) %all-to-all-start) | async-done | bytes 131104 | tf_op jit(solution)/shard_map/all_to_all | solution.py:262
  36.4 0.0 copy-done.2
  36.4 0.9 %finish.1 = f32[4,8,32]{2,1,0:T(8,128)} custom-call(s32[1]{0:T(128)} %bitcast.place_ref, f32[8,9]{1,0:T(8,128)S(1)} %bitcast.5, f32[1,8]{1,0:T(1,128)S(1)} %bitcast.6, f32[32,8,128]{2,1,0:T(8,128)S(1)} %all-to-all-done.in_ref), custom_call_target="tpu_custom_call" | custom-call | tf_op jit(solution)/shard_map/finish/pallas_call | solution.py:197
  (4 shorter events, 0.0 us)
Async XLA Ops:
  0.0 15.3 %copy-start.1 = (s32[8]{0:T(128)S(1)}, s32[8]{0:T(128)}, u32[]{:S(2)}) copy-start(s32[8]{0:T(128)} %labels_ref.3) | copy-start | bytes 100
  0.0 8.9 %collective-permute-start = (bf16[32,2048]{1,0:T(8,128)(2,1)}, bf16[32,2048]{1,0:T(8,128)(2,1)S(1)}, u32[]{:S(2)}, u32[]{:S(2)}) collective-permute-start(bf16[32,2048]{1,0:T(8,128)(2,1)} %queries_ref.1), channel_id=1, source_target_pairs={{0,24},{4,28},{8,16},{12,20},{16,8},{20,12},{24,0},{28,4},{1,25},{... | collective-permute-start | bytes 393224 | tf_op jit(solution)/shard_map/ppermute | solution.py:207
  7.3 29.0 %copy-start = (f32[9,8]{0,1:T(8,128)S(1)}, f32[9,8]{0,1:T(8,128)}, u32[]{:S(2)}) copy-start(f32[9,8]{0,1:T(8,128)} %param.8) | copy-start | bytes 868
  7.3 29.0 %copy-start.2 = (f32[8]{0:T(128)S(1)}, f32[8]{0:T(128)}, u32[]{:S(2)}) copy-start(f32[8]{0:T(128)} %param.9) | copy-start | bytes 100
  7.3 5.4 %collective-permute-start.2 = (bf16[32,2048]{1,0:T(8,128)(2,1)S(1)}, bf16[32,2048]{1,0:T(8,128)(2,1)S(1)}, u32[]{:S(2)}, u32[]{:S(2)}) collective-permute-start(bf16[32,2048]{1,0:T(8,128)(2,1)S(1)} %get-tuple-element.8.rest_0_), channel_id=1, source_target_pairs={{0,4},{4,0},{8,12},{12,8},{16,20},{20,16},{24,28},{28,24},{1,5},{5... | collective-permute-start | bytes 393224 | tf_op jit(solution)/shard_map/ppermute | solution.py:207
  8.9 6.4 %collective-permute-start.3 = (bf16[32,2048]{1,0:T(8,128)(2,1)S(1)}, bf16[32,2048]{1,0:T(8,128)(2,1)S(1)}, u32[]{:S(2)}, u32[]{:S(2)}) collective-permute-start(bf16[32,2048]{1,0:T(8,128)(2,1)S(1)} %get-tuple-element.8.rest_0_), channel_id=1, source_target_pairs={{0,8},{4,12},{8,0},{12,4},{16,24},{20,28},{24,16},{28,20},{1,9},{5... | collective-permute-start | bytes 393224 | tf_op jit(solution)/shard_map/ppermute | solution.py:207
  8.9 8.9 %collective-permute-start.1 = (bf16[32,2048]{1,0:T(8,128)(2,1)S(1)}, bf16[32,2048]{1,0:T(8,128)(2,1)S(1)}, u32[]{:S(2)}, u32[]{:S(2)}) collective-permute-start(bf16[32,2048]{1,0:T(8,128)(2,1)S(1)} %collective-permute-done.rest_3_), channel_id=1, source_target_pairs={{0,8},{4,12},{8,0},{12,4},{16,24},{20,28},{24,16},{28,20},{1,9},{5... | collective-permute-start | bytes 393224 | tf_op jit(solution)/shard_map/ppermute | solution.py:207
  11.3 7.9 %collective-permute-start.5 = (bf16[32,2048]{1,0:T(8,128)(2,1)S(1)}, bf16[32,2048]{1,0:T(8,128)(2,1)S(1)}, u32[]{:S(2)}, u32[]{:S(2)}) collective-permute-start(bf16[32,2048]{1,0:T(8,128)(2,1)S(1)} %collective-permute-done.rest_3_), channel_id=1, source_target_pairs={{0,4},{4,0},{8,12},{12,8},{16,20},{20,16},{24,28},{28,24},{1,5},{5... | collective-permute-start | bytes 393224 | tf_op jit(solution)/shard_map/ppermute | solution.py:207
  12.8 6.4 %collective-permute-start.6 = (bf16[32,2048]{1,0:T(8,128)(2,1)S(1)}, bf16[32,2048]{1,0:T(8,128)(2,1)S(1)}, u32[]{:S(2)}, u32[]{:S(2)}) collective-permute-start(bf16[32,2048]{1,0:T(8,128)(2,1)S(1)} %collective-permute-done.2.rest_1_), channel_id=1, source_target_pairs={{0,8},{4,12},{8,0},{12,4},{16,24},{20,28},{24,16},{28,20},{1,9},{5... | collective-permute-start | bytes 393224 | tf_op jit(solution)/shard_map/ppermute | solution.py:207
  17.8 5.0 %collective-permute-start.4 = (bf16[32,2048]{1,0:T(8,128)(2,1)S(1)}, bf16[32,2048]{1,0:T(8,128)(2,1)S(1)}, u32[]{:S(2)}, u32[]{:S(2)}) collective-permute-start(bf16[32,2048]{1,0:T(8,128)(2,1)S(1)} %tie.1), channel_id=1, source_target_pairs={{0,4},{4,0},{8,12},{12,8},{16,20},{20,16},{24,28},{28,24},{1,5},{5... | collective-permute-start | bytes 393224 | tf_op jit(solution)/shard_map/ppermute | solution.py:207
  24.9 11.4 %all-to-all-start = ((f32[32,8,128]{2,1,0:T(8,128)}), f32[32,8,128]{2,1,0:T(8,128)S(1)}, u32[]{:S(2)}, u32[]{:S(2)}) async-start(f32[32,8,128]{2,1,0:T(8,128)} %bitcast.4), calls=%async_computation | async-start | bytes 262144 | tf_op jit(solution)/shard_map/all_to_all | solution.py:262

commit v4 on v3

--- a/solution.py
+++ b/solution.py
@@ -20,21 +20,18 @@
 neg_floor = -1e30
 narrow = jnp.float8_e4m3fn
 vmem = pl.BlockSpec(memory_space=pltpu.VMEM)
-smem = pl.BlockSpec(memory_space=pltpu.SMEM)
 anywhere = pl.BlockSpec(memory_space=pl.ANY)
 
 
-def pool_window(scores, labels_ref):
+def pool_window(scores, members):
     count = scores.shape[1]
     blocks = scores.shape[0] // BLOCK
-    ancestry = lax.broadcasted_iota(jnp.int32, (A, count), 0)
     peaks, totals = [], []
     for b in range(blocks):
         part = scores[b * BLOCK : (b + 1) * BLOCK]
         peak = jnp.max(part, axis=0, keepdims=True)
         totals.append(jnp.sum(jnp.exp2((part - peak) * (SCALE * LOG2E)), axis=0, keepdims=True))
         peaks.append(peak)
-    members = [ancestry == labels_ref[b] for b in range(blocks)]
     group_peak = jnp.full((A, count), neg_floor, jnp.float32)
     for b in range(blocks):
         group_peak = jnp.where(members[b], jnp.maximum(group_peak, peaks[b]), group_peak)
@@ -45,47 +42,75 @@
     return jnp.where(group_total > 0, SCALE * group_peak + jnp.log(group_total), neg_floor)
 
 
-def stage_body(refs_ref, queries_ref, out_ref, mine_ref, chunks, sems):
+def stage_body(
+    refs_ref, queries_ref, labels_in, taps_in, bias_in,
+    out_ref, mine_ref, members_ref, consts_ref,
+    chunks, labels_ref, taps_ref, bias_ref, sems,
+):
     count, step = chunks.shape[0], chunks.shape[1]
     copies = [
         pltpu.make_async_copy(refs_ref.at[pl.ds(c * step, step)], chunks.at[c], sems.at[c])
         for c in range(count)
     ]
-    copies.append(pltpu.make_async_copy(queries_ref, mine_ref, sems.at[count]))
-    for copy in copies:
+    small = [(labels_in, labels_ref), (taps_in, taps_ref), (bias_in, bias_ref)]
+    small.append((queries_ref, mine_ref))
+    for source, target in small:
+        copies.append(pltpu.make_async_copy(source, target, sems.at[len(copies)]))
+    for copy in copies[count:] + copies[:count]:
         copy.start()
+    for copy in copies[count:]:
+        copy.wait()
+    ancestry = lax.broadcasted_iota(jnp.int32, (A, BLOCK), 0)
+    for b in range(members_ref.shape[0]):
+        members_ref[b] = (ancestry == labels_ref[b]).astype(jnp.float32)
+    same = lax.broadcasted_iota(jnp.int32, (A, A), 0) == lax.broadcasted_iota(jnp.int32, (A, A), 1)
+    bias = jnp.sum(jnp.where(same, bias_ref[...], 0.0), axis=1, keepdims=True)
+    for tap in range(TAPS):
+        consts_ref[tap] = jnp.broadcast_to(taps_ref[:, tap : tap + 1], (A, BLOCK))
+    consts_ref[TAPS] = jnp.broadcast_to(bias, (A, BLOCK))
     for c in range(count):
         copies[c].wait()
         out_ref[c * step : (c + 1) * step] = chunks[c].astype(narrow)
-    copies[count].wait()
-
-
-def stage(references, queries):
+
+
+def stage(references, queries, labels, kernel, class_bias):
     step = 128
     count = references.shape[0] // step
+    operands = (references, queries, labels, kernel.T, class_bias[None, :])
     return pl.pallas_call(
         stage_body,
         out_shape=(
             pltpu.VMEM(references.shape, narrow),
             pltpu.VMEM(queries.shape, queries.dtype),
+            pltpu.VMEM((references.shape[0] // BLOCK, A, BLOCK), jnp.float32),
+            pltpu.VMEM((TAPS + 1, A, BLOCK), jnp.float32),
         ),
-        in_specs=[anywhere] * 2,
-        out_specs=(vmem, vmem),
+        in_specs=[anywhere] * len(operands),
+        out_specs=(vmem,) * 4,
         scratch_shapes=[
             pltpu.VMEM((count, step, references.shape[1]), references.dtype),
-            pltpu.SemaphoreType.DMA((count + 1,)),
+            pltpu.SMEM(labels.shape, labels.dtype),
+            pltpu.VMEM((A, TAPS), kernel.dtype),
+            pltpu.VMEM((1, A), class_bias.dtype),
+            pltpu.SemaphoreType.DMA((count + 4,)),
         ],
         cost_estimate=pl.CostEstimate(
             flops=references.size, bytes_accessed=3 * references.size, transcendentals=0
         ),
         compiler_params=pltpu.CompilerParams(vmem_limit_bytes=40 << 20),
         name="stage",
-    )(*(pltpu.with_memory_space_constraint(x, pltpu.HBM) for x in (references, queries)))
-
-
-def pool_tiles(labels_ref, refs_ref, query_refs):
+    )(*(pltpu.with_memory_space_constraint(x, pltpu.HBM) for x in operands))
+
+
+def pool_tiles(members_ref, refs_ref, query_refs):
     windows = refs_ref.shape[1] // S
     rows = query_refs[0].shape[0]
+    count = rows * len(query_refs)
+    members = [members_ref[b] > 0.5 for b in range(members_ref.shape[0])]
+    if count != BLOCK:
+        members = [
+            jnp.broadcast_to(members_ref[b][:, :1], (A, count)) > 0.5 for b in range(len(members))
+        ]
     pooled = []
     for window in range(windows):
         cols = slice(window * S, (window + 1) * S)
@@ -96,22 +121,22 @@
             (((1,), (1,)), ((), ())),
             preferred_element_type=jnp.float32,
         )
-        pooled.append(pool_window(scores, labels_ref))
+        pooled.append(pool_window(scores, members))
     return [
         jnp.concatenate([p[:, j * rows : (j + 1) * rows] for p in pooled], axis=1)
         for j in range(len(query_refs))
     ]
 
 
-def pool_body(labels_ref, refs_ref, *rest):
+def pool_body(members_ref, refs_ref, *rest):
     out_ref = rest[-1]
-    for j, tile in enumerate(pool_tiles(labels_ref, refs_ref, rest[:-1])):
+    for j, tile in enumerate(pool_tiles(members_ref, refs_ref, rest[:-1])):
         out_ref[j] = tile
 
 
-def last_body(late, groups, here_ref, labels_ref, refs_ref, *rest):
+def last_body(late, groups, members_ref, refs_ref, *rest):
     out_ref = rest[-1]
-    here = here_ref[0]
+    here = lax.axis_index("ref")
 
     def place(offset, tile):
         for v in range(out_ref.shape[0]):
@@ -120,7 +145,7 @@
     for ref, offsets in zip(rest[len(late) : -1], groups, strict=True):
         for j, offset in enumerate(offsets):
             place(offset, ref[j])
-    for offset, tile in zip(late, pool_tiles(labels_ref, refs_ref, rest[: len(late)]), strict=True):
+    for offset, tile in zip(late, pool_tiles(members_ref, refs_ref, rest[: len(late)]), strict=True):
         place(offset, tile)
 
 
@@ -133,37 +158,36 @@
     )
 
 
-def pool(labels, refs, queries):
+def pool(members, refs, queries):
     windows = refs.shape[1] // S
     rows = queries[0].shape[0]
     return pl.pallas_call(
         pool_body,
         out_shape=pltpu.VMEM((len(queries), A, windows * rows), jnp.float32),
-        in_specs=[smem] + [vmem] * (1 + len(queries)),
+        in_specs=[vmem] * (2 + len(queries)),
         out_specs=vmem,
         cost_estimate=pool_cost(refs, queries),
         compiler_params=pltpu.CompilerParams(vmem_limit_bytes=40 << 20),
         name="pool",
-    )(labels, refs, *queries)
-
-
-def pool_last(labels, refs, queries, late, tiles, groups, win, count):
+    )(members, refs, *queries)
+
+
+def pool_last(members, refs, queries, late, tiles, groups, win, count):
     windows = refs.shape[1] // S
     rows = queries[0].shape[0]
-    here = lax.axis_index("ref").astype(jnp.int32).reshape(1)
     return pl.pallas_call(
         functools.partial(last_body, late, groups),
         out_shape=pltpu.VMEM((win, count, A, windows * rows), jnp.float32),
-        in_specs=[smem, smem] + [vmem] * (1 + len(queries) + len(tiles)),
+        in_specs=[vmem] * (2 + len(queries) + len(tiles)),
         out_specs=vmem,
         cost_estimate=pool_cost(refs, queries),
         compiler_params=pltpu.CompilerParams(vmem_limit_bytes=40 << 20),
         name="pool_last",
-    )(here, labels, refs, *queries, *tiles)
-
-
-def finish_body(win, refs, windows, place_ref, taps_ref, bias_ref, in_ref, out_ref):
-    here = place_ref[0]
+    )(members, refs, *queries, *tiles)
+
+
+def finish_body(win, refs, windows, consts_ref, in_ref, out_ref):
+    here = lax.axis_index("win")
     rows = out_ref.shape[2]
 
     def centered(block):
@@ -179,28 +203,22 @@
     total = jnp.zeros((A, width), jnp.float32)
     for tap in range(TAPS):
         start = width + (tap - HALF) * rows
-        total = total + taps_ref[:, tap : tap + 1] * padded[:, start : start + width]
-    same = lax.broadcasted_iota(jnp.int32, (A, A), 0) == lax.broadcasted_iota(jnp.int32, (A, A), 1)
-    logits = total + jnp.sum(jnp.where(same, bias_ref[...], 0.0), axis=1, keepdims=True)
+        total = total + consts_ref[tap][:, :width] * padded[:, start : start + width]
+    logits = total + consts_ref[TAPS][:, :width]
     shifted = logits - jnp.max(logits, axis=0, keepdims=True)
     result = shifted - jnp.log(jnp.sum(jnp.exp(shifted), axis=0, keepdims=True))
     for window in range(windows):
         out_ref[window] = result[:, window * rows : (window + 1) * rows]
 
 
-def finish(received, kernel, class_bias, win, refs, windows, rows):
-    place = lax.axis_index("win").astype(jnp.int32).reshape(1)
-    operands = [
-        pltpu.with_memory_space_constraint(x, pltpu.VMEM)
-        for x in (kernel.T, class_bias[None, :], received)
-    ]
+def finish(received, consts, win, refs, windows, rows):
     return pl.pallas_call(
         functools.partial(finish_body, win, refs, windows),
         out_shape=jax.ShapeDtypeStruct((windows, A, rows), jnp.float32),
-        in_specs=[smem] + [vmem] * 3,
+        in_specs=[vmem] * 2,
         out_specs=vmem,
         name="finish",
-    )(place, *operands)
+    )(*(pltpu.with_memory_space_constraint(x, pltpu.VMEM) for x in (consts, received)))
 
 
 def exchange(block, offset, size):
@@ -247,20 +265,20 @@
     refs, win = lax.axis_size("ref"), lax.axis_size("win")
     windows = references.shape[1] // S
     rows = queries.shape[0]
-    staged, mine = stage(references, queries)
+    staged, mine, members, consts = stage(references, queries, labels, kernel, class_bias)
     tiles, groups = [], []
 
     def early(blocks):
         groups.append(list(blocks))
-        tiles.append(pool(labels, staged, list(blocks.values())))
+        tiles.append(pool(members, staged, list(blocks.values())))
         return tiles[-1]
 
     blocks = gather_queries(queries, mine, refs, early)
     late = [k for k in blocks if k not in sum(groups, [])]
-    sent = pool_last(labels, staged, [blocks[k] for k in late], late, tiles, groups, win, refs)
+    sent = pool_last(members, staged, [blocks[k] for k in late], late, tiles, groups, win, refs)
     sent = sent.reshape((win * refs,) + sent.shape[2:])
     received = lax.all_to_all(sent, ("win", "ref"), split_axis=0, concat_axis=0, tiled=True)
-    return finish(received, kernel, class_bias, win, refs, windows, rows)
+    return finish(received, consts, win, refs, windows, rows)
 
 
 def solution(mesh):

time: 37.4 us -> 35.8 us (0.957)
  blocking collectives: 0 us -> 11 us
  waiting for transfers between devices: 15.6 us -> 8.63 us
  starting transfers between devices: 14.8 us -> 11 us
  Pallas kernels: 6.69 us -> 5.02 us
    all_to_all x0 -> x1, blocking collectives: none -> 11 us  [per_device(): lax.all_to_all(sent, ('win', 'ref'), split_axis=0, concat_axis=0, tiled=T...]
    all_to_all x1 -> x0, waiting for transfers between devices: 7.74 us -> none  [per_device(): lax.all_to_all(sent, ('win', 'ref'), split_axis=0, concat_axis=0, tiled=T...]
    all_to_all x1 -> x0, starting transfers between devices: 3.66 us -> none  [per_device(): lax.all_to_all(sent, ('win', 'ref'), split_axis=0, concat_axis=0, tiled=T...]
    pallas_call x1, Pallas kernels: 2.11 us -> 0.91 us  [pool_last(): pl.pallas_call(functools.partial(last_body, late, groups), out_shape=pltp...]
    ppermute x7, waiting for transfers between devices: 7.91 us -> 8.63 us  [exchange(): return lax.ppermute(block, 'ref', [(i, i ^ offset) for i in range(size)])]
    pallas_call x1, Pallas kernels: 1.45 us -> 0.91 us  [pool(): pl.pallas_call(pool_body, out_shape=pltpu.VMEM((len(queries), A, windows...]
  transfers between devices with their start and end apart: 8 -> 7, of which waited for: 5 -> 4; matrix products, arithmetic and copies ran while one was open for 0% -> 0% of each run, Pallas kernels for 10% -> 9%
where the time goes in v4:
time: 35.8 us; the launch traced here: 35.7 us
  starting transfers between devices  11 us (31%)
  blocking collectives  11 us (31%)
  waiting for transfers between devices  8.63 us (24%)
  Pallas kernels  5.02 us (14%)
    all_to_all x1, blocking collectives, per_device(): lax.all_to_all(sent, ('win', 'ref'), split_axis=0, concat_axis=0, tiled=T...  11 us
    ppermute x7, starting transfers between devices, exchange(): return lax.ppermute(block, 'ref', [(i, i ^ offset) for i in range(size)])  11 us
    ppermute x7, waiting for transfers between devices, exchange(): return lax.ppermute(block, 'ref', [(i, i ^ offset) for i in range(size)])  8.63 us
    pallas_call x1, Pallas kernels, stage(): pl.pallas_call(stage_body, out_shape=(pltpu.VMEM(references.shape, narrow...  2.38 us
    pallas_call x1, Pallas kernels, pool_last(): pl.pallas_call(functools.partial(last_body, late, groups), out_shape=pltp...  0.91 us
    pallas_call x1, Pallas kernels, pool(): pl.pallas_call(pool_body, out_shape=pltpu.VMEM((len(queries), A, windows...  0.91 us
    pallas_call x1, Pallas kernels, finish(): pl.pallas_call(functools.partial(finish_body, win, refs, windows), out_sh...  0.82 us
  transfers between devices with their start and end apart: 7, of which 4 were waited for; matrix products, arithmetic and copies ran while one was open for 0% of the time, Pallas kernels for 9%

profile of v4, /device:TPU:0, one launch (start us, length us, event | category | flops | bytes accessed | tf_op | source)
XLA Modules:
  0.0 35.7 jit_solution(5712256071732143816)
XLA Ops:
  0.0 5.0 %collective-permute-start = (bf16[32,2048]{1,0:T(8,128)(2,1)}, bf16[32,2048]{1,0:T(8,128)(2,1)S(1)}, u32[]{:S(2)}, u32[]{:S(2)}) collective-permute-start(bf16[32,2048]{1,0:T(8,128)(2,1)} %queries_ref.1), channel_id=1, source_target_pairs={{0,24},{4,28},{8,16},{12,20},{16,8},{20,12},{24,0},{28,4},{1,25},{... | collective-permute-start | bytes 393224 | tf_op jit(solution)/shard_map/ppermute | solution.py:225
  5.0 2.4 %stage.1 = (f8e4m3fn[1024,2048]{1,0:T(32,128)(4,1)S(1)}, bf16[32,2048]{1,0:T(8,128)(2,1)S(1)}, f32[8,8,128]{2,1,0:T(8,128)S(1)}, f32[10,8,128]{2,1,0:T(8,128)S(1)}) custom-call(bf16[1024,2048]{1,0:T(8,128)(2,1)} %refs_ref.1, bf16[32,2048]{1,0:T(8,128)(2,1)} %queries_ref.1, s32[8]{0:T(128)} %labels_in.1, f32[8,9]{1,0:T(8,128)} %bitcast.4, f32[1,8]{1,0:T(1,128)} %bitcast.5), custom_call_target="tpu_custom_call" | custom-call | flops 2097152 | bytes 6291456 | tf_op jit(solution)/shard_map/stage/pallas_call | solution.py:80
  7.4 1.6 %collective-permute-start.2 = (bf16[32,2048]{1,0:T(8,128)(2,1)S(1)}, bf16[32,2048]{1,0:T(8,128)(2,1)S(1)}, u32[]{:S(2)}, u32[]{:S(2)}) collective-permute-start(bf16[32,2048]{1,0:T(8,128)(2,1)S(1)} %get-tuple-element.12.rest_0_), channel_id=1, source_target_pairs={{0,4},{4,0},{8,12},{12,8},{16,20},{20,16},{24,28},{28,24},{1,5},{5... | collective-permute-start | bytes 393224 | tf_op jit(solution)/shard_map/ppermute | solution.py:225
  9.0 0.0 collective-permute-start.3
  9.0 0.0 collective-permute-done.rest_3_
  9.0 2.3 %collective-permute-start.1 = (bf16[32,2048]{1,0:T(8,128)(2,1)S(1)}, bf16[32,2048]{1,0:T(8,128)(2,1)S(1)}, u32[]{:S(2)}, u32[]{:S(2)}) collective-permute-start(bf16[32,2048]{1,0:T(8,128)(2,1)S(1)} %collective-permute-done.rest_3_), channel_id=1, source_target_pairs={{0,8},{4,12},{8,0},{12,4},{16,24},{20,28},{24,16},{28,20},{1,9},{5... | collective-permute-start | bytes 393224 | tf_op jit(solution)/shard_map/ppermute | solution.py:225
  11.3 1.5 %collective-permute-start.5 = (bf16[32,2048]{1,0:T(8,128)(2,1)S(1)}, bf16[32,2048]{1,0:T(8,128)(2,1)S(1)}, u32[]{:S(2)}, u32[]{:S(2)}) collective-permute-start(bf16[32,2048]{1,0:T(8,128)(2,1)S(1)} %collective-permute-done.rest_3_), channel_id=1, source_target_pairs={{0,4},{4,0},{8,12},{12,8},{16,20},{20,16},{24,28},{28,24},{1,5},{5... | collective-permute-start | bytes 393224 | tf_op jit(solution)/shard_map/ppermute | solution.py:225
  12.8 0.0 collective-permute-done.2.rest_1_
  12.8 0.0 collective-permute-start.6
  12.8 2.6 %collective-permute-done.3.rest_2_ = bf16[32,2048]{1,0:T(8,128)(2,1)S(1)} collective-permute-done((bf16[32,2048]{1,0:T(8,128)(2,1)S(1)}, bf16[32,2048]{1,0:T(8,128)(2,1)S(1)}, u32[]{:S(2)}, u32[]{:S(2)}) %collective-permute-start.3) | collective-permute-done | bytes 131104 | tf_op jit(solution)/shard_map/ppermute | solution.py:225
  15.4 0.9 %pool.1.refs_1_.rest_4_ = f32[4,8,128]{2,1,0:T(8,128)S(1)} custom-call(f32[8,8,128]{2,1,0:T(8,128)S(1)} %get-tuple-element.10.members_ref, f8e4m3fn[1024,2048]{1,0:T(32,128)(4,1)S(1)} %get-tuple-element.11.refs_ref, bf16[32,2048]{1,0:T(8,128)(2,1)S(1)} %get-tuple-element.12.rest_0_, bf16[32,2048]{1,0:T(8,128)(2,1)S(1)} %collective-permute-done.2.rest_1_, ...), custom_call_target="tpu_custom_call" | custom-call | flops 536870912 | bytes 2097152 | tf_op jit(solution)/shard_map/pool/pallas_call | solution.py:164
  16.3 1.5 %collective-permute-done.1.rest_0_ = bf16[32,2048]{1,0:T(8,128)(2,1)S(1)} collective-permute-done((bf16[32,2048]{1,0:T(8,128)(2,1)S(1)}, bf16[32,2048]{1,0:T(8,128)(2,1)S(1)}, u32[]{:S(2)}, u32[]{:S(2)}) %collective-permute-start.1) | collective-permute-done | bytes 131104 | tf_op jit(solution)/shard_map/ppermute | solution.py:225
  17.9 0.6 %collective-permute-start.4 = (bf16[32,2048]{1,0:T(8,128)(2,1)S(1)}, bf16[32,2048]{1,0:T(8,128)(2,1)S(1)}, u32[]{:S(2)}, u32[]{:S(2)}) collective-permute-start(bf16[32,2048]{1,0:T(8,128)(2,1)S(1)} %tie.1), channel_id=1, source_target_pairs={{0,4},{4,0},{8,12},{12,8},{16,20},{20,16},{24,28},{28,24},{1,5},{5... | collective-permute-start | bytes 393224 | tf_op jit(solution)/shard_map/ppermute | solution.py:225
  18.5 0.8 %collective-permute-done.6.rest_3_ = bf16[32,2048]{1,0:T(8,128)(2,1)S(1)} collective-permute-done((bf16[32,2048]{1,0:T(8,128)(2,1)S(1)}, bf16[32,2048]{1,0:T(8,128)(2,1)S(1)}, u32[]{:S(2)}, u32[]{:S(2)}) %collective-permute-start.6) | collective-permute-done | bytes 131104 | tf_op jit(solution)/shard_map/ppermute | solution.py:225
  19.3 0.0 collective-permute-done.5.rest_2_
  19.3 3.6 %collective-permute-done.4.rest_1_ = bf16[32,2048]{1,0:T(8,128)(2,1)S(1)} collective-permute-done((bf16[32,2048]{1,0:T(8,128)(2,1)S(1)}, bf16[32,2048]{1,0:T(8,128)(2,1)S(1)}, u32[]{:S(2)}, u32[]{:S(2)}) %collective-permute-start.4) | collective-permute-done | bytes 131104 | tf_op jit(solution)/shard_map/ppermute | solution.py:225
  22.9 0.9 %pool_last.1 = f32[4,8,8,128]{3,2,1,0:T(8,128)S(1)} custom-call(f32[8,8,128]{2,1,0:T(8,128)S(1)} %get-tuple-element.10.members_ref, f8e4m3fn[1024,2048]{1,0:T(32,128)(4,1)S(1)} %get-tuple-element.11.refs_ref, bf16[32,2048]{1,0:T(8,128)(2,1)S(1)} %collective-permute-done.1.rest_0_, bf16[32,2048]{1,0:T(8,128)(2,1)S(1)} %collective-permute-done.4.rest_1_, ...), custom_call_target="tpu_custom_call" | custom-call | flops 536870912 | bytes 2097152 | tf_op jit(solution)/shard_map/pool_last/pallas_call | solution.py:178
  23.8 11.0 %all_to_all.5.in_ref = f32[32,8,128]{2,1,0:T(8,128)S(1)} all-to-all(f32[32,8,128]{2,1,0:T(8,128)S(1)} %bitcast.3), channel_id=1, replica_groups=mesh['ref'=8,'win'=4] {'win','ref'}, dimensions={0} | all-to-all | bytes 262144 | tf_op jit(solution)/shard_map/all_to_all | solution.py:280
  34.8 0.8 %finish.1 = f32[4,8,32]{2,1,0:T(8,128)} custom-call(f32[10,8,128]{2,1,0:T(8,128)S(1)} %get-tuple-element.9.consts_ref, f32[32,8,128]{2,1,0:T(8,128)S(1)} %all_to_all.5.in_ref), custom_call_target="tpu_custom_call" | custom-call | tf_op jit(solution)/shard_map/finish/pallas_call | solution.py:215
  (2 shorter events, 0.0 us)
Async XLA Ops:
  0.0 9.0 %collective-permute-start = (bf16[32,2048]{1,0:T(8,128)(2,1)}, bf16[32,2048]{1,0:T(8,128)(2,1)S(1)}, u32[]{:S(2)}, u32[]{:S(2)}) collective-permute-start(bf16[32,2048]{1,0:T(8,128)(2,1)} %queries_ref.1), channel_id=1, source_target_pairs={{0,24},{4,28},{8,16},{12,20},{16,8},{20,12},{24,0},{28,4},{1,25},{... | collective-permute-start | bytes 393224 | tf_op jit(solution)/shard_map/ppermute | solution.py:225
  7.4 5.3 %collective-permute-start.2 = (bf16[32,2048]{1,0:T(8,128)(2,1)S(1)}, bf16[32,2048]{1,0:T(8,128)(2,1)S(1)}, u32[]{:S(2)}, u32[]{:S(2)}) collective-permute-start(bf16[32,2048]{1,0:T(8,128)(2,1)S(1)} %get-tuple-element.12.rest_0_), channel_id=1, source_target_pairs={{0,4},{4,0},{8,12},{12,8},{16,20},{20,16},{24,28},{28,24},{1,5},{5... | collective-permute-start | bytes 393224 | tf_op jit(solution)/shard_map/ppermute | solution.py:225
  9.0 6.4 %collective-permute-start.3 = (bf16[32,2048]{1,0:T(8,128)(2,1)S(1)}, bf16[32,2048]{1,0:T(8,128)(2,1)S(1)}, u32[]{:S(2)}, u32[]{:S(2)}) collective-permute-start(bf16[32,2048]{1,0:T(8,128)(2,1)S(1)} %get-tuple-element.12.rest_0_), channel_id=1, source_target_pairs={{0,8},{4,12},{8,0},{12,4},{16,24},{20,28},{24,16},{28,20},{1,9},{5... | collective-permute-start | bytes 393224 | tf_op jit(solution)/shard_map/ppermute | solution.py:225
  9.0 8.9 %collective-permute-start.1 = (bf16[32,2048]{1,0:T(8,128)(2,1)S(1)}, bf16[32,2048]{1,0:T(8,128)(2,1)S(1)}, u32[]{:S(2)}, u32[]{:S(2)}) collective-permute-start(bf16[32,2048]{1,0:T(8,128)(2,1)S(1)} %collective-permute-done.rest_3_), channel_id=1, source_target_pairs={{0,8},{4,12},{8,0},{12,4},{16,24},{20,28},{24,16},{28,20},{1,9},{5... | collective-permute-start | bytes 393224 | tf_op jit(solution)/shard_map/ppermute | solution.py:225
  11.3 8.0 %collective-permute-start.5 = (bf16[32,2048]{1,0:T(8,128)(2,1)S(1)}, bf16[32,2048]{1,0:T(8,128)(2,1)S(1)}, u32[]{:S(2)}, u32[]{:S(2)}) collective-permute-start(bf16[32,2048]{1,0:T(8,128)(2,1)S(1)} %collective-permute-done.rest_3_), channel_id=1, source_target_pairs={{0,4},{4,0},{8,12},{12,8},{16,20},{20,16},{24,28},{28,24},{1,5},{5... | collective-permute-start | bytes 393224 | tf_op jit(solution)/shard_map/ppermute | solution.py:225
  12.8 6.5 %collective-permute-start.6 = (bf16[32,2048]{1,0:T(8,128)(2,1)S(1)}, bf16[32,2048]{1,0:T(8,128)(2,1)S(1)}, u32[]{:S(2)}, u32[]{:S(2)}) collective-permute-start(bf16[32,2048]{1,0:T(8,128)(2,1)S(1)} %collective-permute-done.2.rest_1_), channel_id=1, source_target_pairs={{0,8},{4,12},{8,0},{12,4},{16,24},{20,28},{24,16},{28,20},{1,9},{5... | collective-permute-start | bytes 393224 | tf_op jit(solution)/shard_map/ppermute | solution.py:225
  17.9 5.0 %collective-permute-start.4 = (bf16[32,2048]{1,0:T(8,128)(2,1)S(1)}, bf16[32,2048]{1,0:T(8,128)(2,1)S(1)}, u32[]{:S(2)}, u32[]{:S(2)}) collective-permute-start(bf16[32,2048]{1,0:T(8,128)(2,1)S(1)} %tie.1), channel_id=1, source_target_pairs={{0,4},{4,0},{8,12},{12,8},{16,20},{20,16},{24,28},{28,24},{1,5},{5... | collective-permute-start | bytes 393224 | tf_op jit(solution)/shard_map/ppermute | solution.py:225

commit v5 on v4

--- a/solution.py
+++ b/solution.py
@@ -225,36 +225,20 @@
     return lax.ppermute(block, "ref", [(i, i ^ offset) for i in range(size)])
 
 
-def tie_body(*refs):
-    pass
-
-
-def tie(value, *others):
-    return pl.pallas_call(
-        tie_body,
-        out_shape=pltpu.VMEM(value.shape, value.dtype),
-        in_specs=[anywhere] * (1 + len(others)),
-        out_specs=anywhere,
-        input_output_aliases={0: 0},
-        name="tie",
-    )(value, *(pltpu.with_memory_space_constraint(x, pltpu.VMEM) for x in others))
-
-
 def gather_queries(queries, mine, size, early):
-    far = [k for k in range(4, size, 2)]
+    near = [k for k in range(4, size, 2) if k & 2]
     blocks = {0: mine}
-    for k in [k for k in far if k & 2]:
+    for k in near + [2, 1]:
         blocks[k] = exchange(queries, k, size)
-    blocks[1] = exchange(mine, 1, size)
-    blocks[2] = exchange(mine, 2, size)
-    first = [0, 1, 2, far[-1]]
-    pooled = early({k: blocks[k] for k in first})
-    for k in [k for k in far if not k & 2]:
-        blocks[k] = exchange(blocks[k | 2], 2, size)
-    for k in far:
-        source = tie(blocks[k], pooled) if k == 4 else blocks[k]
-        blocks[k | 1] = exchange(source, 1, size)
-    blocks[3] = exchange(blocks[1], 2, size)
+    first = [0, 1, 2, near[-1]]
+    early({k: blocks[k] for k in first})
+    for k in near:
+        blocks[k ^ 3] = exchange(mine, k ^ 3, size)
+    for k in near:
+        blocks[k | 1] = exchange(blocks[k], 1, size)
+    for k in near:
+        blocks[k ^ 2] = exchange(blocks[k], 2, size)
+    blocks[3] = exchange(blocks[2], 1, size)
     rest = [k for k in blocks if k not in first]
     for k in range(0, len(rest) - LAST, LAST):
         early({j: blocks[j] for j in rest[k : k + LAST]})

time: 35.8 us -> 33.7 us (0.941)
  waiting for transfers between devices: 8.63 us -> 5.41 us
  blocking collectives: 11 us -> 12.1 us
    ppermute x7, waiting for transfers between devices: 8.63 us -> 5.41 us  [exchange(): return lax.ppermute(block, 'ref', [(i, i ^ offset) for i in range(size)])]
    all_to_all x1, blocking collectives: 11 us -> 12.1 us  [per_device(): lax.all_to_all(sent, ('win', 'ref'), split_axis=0, concat_axis=0, tiled=T...]
  transfers between devices with their start and end apart: 7 -> 7, of which waited for: 4 -> 3; matrix products, arithmetic and copies ran while one was open for 0% -> 0% of each run, Pallas kernels for 9% -> 10%
where the time goes in v5:
time: 33.7 us; the launch traced here: 33.6 us
  blocking collectives  12.1 us (36%)
  starting transfers between devices  11.1 us (33%)
  waiting for transfers between devices  5.41 us (16%)
  Pallas kernels  5.01 us (15%)
    all_to_all x1, blocking collectives, per_device(): lax.all_to_all(sent, ('win', 'ref'), split_axis=0, concat_axis=0, tiled=T...  12.1 us
    ppermute x7, starting transfers between devices, exchange(): return lax.ppermute(block, 'ref', [(i, i ^ offset) for i in range(size)])  11.1 us
    ppermute x7, waiting for transfers between devices, exchange(): return lax.ppermute(block, 'ref', [(i, i ^ offset) for i in range(size)])  5.41 us
    pallas_call x1, Pallas kernels, stage(): pl.pallas_call(stage_body, out_shape=(pltpu.VMEM(references.shape, narrow...  2.38 us
    pallas_call x1, Pallas kernels, pool(): pl.pallas_call(pool_body, out_shape=pltpu.VMEM((len(queries), A, windows...  0.91 us
    pallas_call x1, Pallas kernels, pool_last(): pl.pallas_call(functools.partial(last_body, late, groups), out_shape=pltp...  0.91 us
    pallas_call x1, Pallas kernels, finish(): pl.pallas_call(functools.partial(finish_body, win, refs, windows), out_sh...  0.82 us
  transfers between devices with their start and end apart: 7, of which 3 were waited for; matrix products, arithmetic and copies ran while one was open for 0% of the time, Pallas kernels for 10%

profile of v5, /device:TPU:0, one launch (start us, length us, event | category | flops | bytes accessed | tf_op | source)
XLA Modules:
  0.0 33.6 jit_solution(3569298787389783578)
XLA Ops:
  0.0 5.0 %collective-permute-start.1 = (bf16[32,2048]{1,0:T(8,128)(2,1)}, bf16[32,2048]{1,0:T(8,128)(2,1)S(1)}, u32[]{:S(2)}, u32[]{:S(2)}) collective-permute-start(bf16[32,2048]{1,0:T(8,128)(2,1)} %queries_ref.1), channel_id=1, source_target_pairs={{0,24},{4,28},{8,16},{12,20},{16,8},{20,12},{24,0},{28,4},{1,25},{... | collective-permute-start | bytes 393224 | tf_op jit(solution)/shard_map/ppermute | solution.py:225
  5.0 0.0 collective-permute-start.4
  5.1 1.5 %collective-permute-start.6 = (bf16[32,2048]{1,0:T(8,128)(2,1)}, bf16[32,2048]{1,0:T(8,128)(2,1)S(1)}, u32[]{:S(2)}, u32[]{:S(2)}) collective-permute-start(bf16[32,2048]{1,0:T(8,128)(2,1)} %queries_ref.1), channel_id=1, source_target_pairs={{0,4},{4,0},{8,12},{12,8},{16,20},{20,16},{24,28},{28,24},{1,5},{5... | collective-permute-start | bytes 393224 | tf_op jit(solution)/shard_map/ppermute | solution.py:225
  6.5 2.4 %stage.1 = (f8e4m3fn[1024,2048]{1,0:T(32,128)(4,1)S(1)}, bf16[32,2048]{1,0:T(8,128)(2,1)S(1)}, f32[8,8,128]{2,1,0:T(8,128)S(1)}, f32[10,8,128]{2,1,0:T(8,128)S(1)}) custom-call(bf16[1024,2048]{1,0:T(8,128)(2,1)} %refs_ref.1, bf16[32,2048]{1,0:T(8,128)(2,1)} %queries_ref.1, s32[8]{0:T(128)} %labels_in.1, f32[8,9]{1,0:T(8,128)} %bitcast.4, f32[1,8]{1,0:T(1,128)} %bitcast.5), custom_call_target="tpu_custom_call" | custom-call | flops 2097152 | bytes 6291456 | tf_op jit(solution)/shard_map/stage/pallas_call | solution.py:80
  8.9 0.6 %collective-permute-start = (bf16[32,2048]{1,0:T(8,128)(2,1)S(1)}, bf16[32,2048]{1,0:T(8,128)(2,1)S(1)}, u32[]{:S(2)}, u32[]{:S(2)}) collective-permute-start(bf16[32,2048]{1,0:T(8,128)(2,1)S(1)} %get-tuple-element.12.rest_0_), channel_id=1, source_target_pairs={{0,20},{4,16},{8,28},{12,24},{16,4},{20,0},{24,12},{28,8},{1,21},{... | collective-permute-start | bytes 393224 | tf_op jit(solution)/shard_map/ppermute | solution.py:225
  9.5 0.1 collective-permute-done.1.rest_3_
  9.6 1.7 %collective-permute-start.2 = (bf16[32,2048]{1,0:T(8,128)(2,1)S(1)}, bf16[32,2048]{1,0:T(8,128)(2,1)S(1)}, u32[]{:S(2)}, u32[]{:S(2)}) collective-permute-start(bf16[32,2048]{1,0:T(8,128)(2,1)S(1)} %collective-permute-done.1.rest_3_), channel_id=1, source_target_pairs={{0,4},{4,0},{8,12},{12,8},{16,20},{20,16},{24,28},{28,24},{1,5},{5... | collective-permute-start | bytes 393224 | tf_op jit(solution)/shard_map/ppermute | solution.py:225
  11.3 1.4 %collective-permute-start.3 = (bf16[32,2048]{1,0:T(8,128)(2,1)S(1)}, bf16[32,2048]{1,0:T(8,128)(2,1)S(1)}, u32[]{:S(2)}, u32[]{:S(2)}) collective-permute-start(bf16[32,2048]{1,0:T(8,128)(2,1)S(1)} %collective-permute-done.1.rest_3_), channel_id=1, source_target_pairs={{0,8},{4,12},{8,0},{12,4},{16,24},{20,28},{24,16},{28,20},{1,9},{5... | collective-permute-start | bytes 393224 | tf_op jit(solution)/shard_map/ppermute | solution.py:225
  12.8 0.0 collective-permute-done.4.rest_2_
  12.8 0.8 %collective-permute-start.5 = (bf16[32,2048]{1,0:T(8,128)(2,1)S(1)}, bf16[32,2048]{1,0:T(8,128)(2,1)S(1)}, u32[]{:S(2)}, u32[]{:S(2)}) collective-permute-start(bf16[32,2048]{1,0:T(8,128)(2,1)S(1)} %collective-permute-done.4.rest_2_), channel_id=1, source_target_pairs={{0,4},{4,0},{8,12},{12,8},{16,20},{20,16},{24,28},{28,24},{1,5},{5... | collective-permute-start | bytes 393224 | tf_op jit(solution)/shard_map/ppermute | solution.py:225
  13.6 0.0 collective-permute-done.6.rest_1_
  13.6 0.9 %pool.1.rest_4_ = f32[4,8,128]{2,1,0:T(8,128)S(1)} custom-call(f32[8,8,128]{2,1,0:T(8,128)S(1)} %get-tuple-element.10.members_ref, f8e4m3fn[1024,2048]{1,0:T(32,128)(4,1)S(1)} %get-tuple-element.11.refs_ref, bf16[32,2048]{1,0:T(8,128)(2,1)S(1)} %get-tuple-element.12.rest_0_, bf16[32,2048]{1,0:T(8,128)(2,1)S(1)} %collective-permute-done.6.rest_1_, ...), custom_call_target="tpu_custom_call" | custom-call | flops 536870912 | bytes 2097152 | tf_op jit(solution)/shard_map/pool/pallas_call | solution.py:164
  14.5 3.9 %collective-permute-done.rest_0_ = bf16[32,2048]{1,0:T(8,128)(2,1)S(1)} collective-permute-done((bf16[32,2048]{1,0:T(8,128)(2,1)S(1)}, bf16[32,2048]{1,0:T(8,128)(2,1)S(1)}, u32[]{:S(2)}, u32[]{:S(2)}) %collective-permute-start) | collective-permute-done | bytes 131104 | tf_op jit(solution)/shard_map/ppermute | solution.py:225
  18.4 0.0 collective-permute-done.2.rest_1_
  18.4 0.0 collective-permute-done.3.rest_2_
  18.4 1.3 %collective-permute-done.5.rest_3_ = bf16[32,2048]{1,0:T(8,128)(2,1)S(1)} collective-permute-done((bf16[32,2048]{1,0:T(8,128)(2,1)S(1)}, bf16[32,2048]{1,0:T(8,128)(2,1)S(1)}, u32[]{:S(2)}, u32[]{:S(2)}) %collective-permute-start.5) | collective-permute-done | bytes 131104 | tf_op jit(solution)/shard_map/ppermute | solution.py:225
  19.8 0.9 %pool_last.1 = f32[4,8,8,128]{3,2,1,0:T(8,128)S(1)} custom-call(f32[8,8,128]{2,1,0:T(8,128)S(1)} %get-tuple-element.10.members_ref, f8e4m3fn[1024,2048]{1,0:T(32,128)(4,1)S(1)} %get-tuple-element.11.refs_ref, bf16[32,2048]{1,0:T(8,128)(2,1)S(1)} %collective-permute-done.rest_0_, bf16[32,2048]{1,0:T(8,128)(2,1)S(1)} %collective-permute-done.2.rest_1_, ...), custom_call_target="tpu_custom_call" | custom-call | flops 536870912 | bytes 2097152 | tf_op jit(solution)/shard_map/pool_last/pallas_call | solution.py:178
  20.7 12.1 %all_to_all.5.in_ref = f32[32,8,128]{2,1,0:T(8,128)S(1)} all-to-all(f32[32,8,128]{2,1,0:T(8,128)S(1)} %bitcast.3), channel_id=1, replica_groups=mesh['ref'=8,'win'=4] {'win','ref'}, dimensions={0} | all-to-all | bytes 262144 | tf_op jit(solution)/shard_map/all_to_all | solution.py:264
  32.8 0.8 %finish.1 = f32[4,8,32]{2,1,0:T(8,128)} custom-call(f32[10,8,128]{2,1,0:T(8,128)S(1)} %get-tuple-element.9.consts_ref, f32[32,8,128]{2,1,0:T(8,128)S(1)} %all_to_all.5.in_ref), custom_call_target="tpu_custom_call" | custom-call | tf_op jit(solution)/shard_map/finish/pallas_call | solution.py:215
Async XLA Ops:
  0.0 9.6 %collective-permute-start.1 = (bf16[32,2048]{1,0:T(8,128)(2,1)}, bf16[32,2048]{1,0:T(8,128)(2,1)S(1)}, u32[]{:S(2)}, u32[]{:S(2)}) collective-permute-start(bf16[32,2048]{1,0:T(8,128)(2,1)} %queries_ref.1), channel_id=1, source_target_pairs={{0,24},{4,28},{8,16},{12,20},{16,8},{20,12},{24,0},{28,4},{1,25},{... | collective-permute-start | bytes 393224 | tf_op jit(solution)/shard_map/ppermute | solution.py:225
  5.0 7.7 %collective-permute-start.4 = (bf16[32,2048]{1,0:T(8,128)(2,1)}, bf16[32,2048]{1,0:T(8,128)(2,1)S(1)}, u32[]{:S(2)}, u32[]{:S(2)}) collective-permute-start(bf16[32,2048]{1,0:T(8,128)(2,1)} %queries_ref.1), channel_id=1, source_target_pairs={{0,8},{4,12},{8,0},{12,4},{16,24},{20,28},{24,16},{28,20},{1,9},{5... | collective-permute-start | bytes 393224 | tf_op jit(solution)/shard_map/ppermute | solution.py:225
  5.1 8.5 %collective-permute-start.6 = (bf16[32,2048]{1,0:T(8,128)(2,1)}, bf16[32,2048]{1,0:T(8,128)(2,1)S(1)}, u32[]{:S(2)}, u32[]{:S(2)}) collective-permute-start(bf16[32,2048]{1,0:T(8,128)(2,1)} %queries_ref.1), channel_id=1, source_target_pairs={{0,4},{4,0},{8,12},{12,8},{16,20},{20,16},{24,28},{28,24},{1,5},{5... | collective-permute-start | bytes 393224 | tf_op jit(solution)/shard_map/ppermute | solution.py:225
  8.9 9.5 %collective-permute-start = (bf16[32,2048]{1,0:T(8,128)(2,1)S(1)}, bf16[32,2048]{1,0:T(8,128)(2,1)S(1)}, u32[]{:S(2)}, u32[]{:S(2)}) collective-permute-start(bf16[32,2048]{1,0:T(8,128)(2,1)S(1)} %get-tuple-element.12.rest_0_), channel_id=1, source_target_pairs={{0,20},{4,16},{8,28},{12,24},{16,4},{20,0},{24,12},{28,8},{1,21},{... | collective-permute-start | bytes 393224 | tf_op jit(solution)/shard_map/ppermute | solution.py:225
  9.6 8.8 %collective-permute-start.2 = (bf16[32,2048]{1,0:T(8,128)(2,1)S(1)}, bf16[32,2048]{1,0:T(8,128)(2,1)S(1)}, u32[]{:S(2)}, u32[]{:S(2)}) collective-permute-start(bf16[32,2048]{1,0:T(8,128)(2,1)S(1)} %collective-permute-done.1.rest_3_), channel_id=1, source_target_pairs={{0,4},{4,0},{8,12},{12,8},{16,20},{20,16},{24,28},{28,24},{1,5},{5... | collective-permute-start | bytes 393224 | tf_op jit(solution)/shard_map/ppermute | solution.py:225
  11.3 7.1 %collective-permute-start.3 = (bf16[32,2048]{1,0:T(8,128)(2,1)S(1)}, bf16[32,2048]{1,0:T(8,128)(2,1)S(1)}, u32[]{:S(2)}, u32[]{:S(2)}) collective-permute-start(bf16[32,2048]{1,0:T(8,128)(2,1)S(1)} %collective-permute-done.1.rest_3_), channel_id=1, source_target_pairs={{0,8},{4,12},{8,0},{12,4},{16,24},{20,28},{24,16},{28,20},{1,9},{5... | collective-permute-start | bytes 393224 | tf_op jit(solution)/shard_map/ppermute | solution.py:225
  12.8 7.0 %collective-permute-start.5 = (bf16[32,2048]{1,0:T(8,128)(2,1)S(1)}, bf16[32,2048]{1,0:T(8,128)(2,1)S(1)}, u32[]{:S(2)}, u32[]{:S(2)}) collective-permute-start(bf16[32,2048]{1,0:T(8,128)(2,1)S(1)} %collective-permute-done.4.rest_2_), channel_id=1, source_target_pairs={{0,4},{4,0},{8,12},{12,8},{16,20},{20,16},{24,28},{28,24},{1,5},{5... | collective-permute-start | bytes 393224 | tf_op jit(solution)/shard_map/ppermute | solution.py:225

commit v6 on v5

--- a/solution.py
+++ b/solution.py
@@ -233,7 +233,7 @@
     first = [0, 1, 2, near[-1]]
     early({k: blocks[k] for k in first})
     for k in near:
-        blocks[k ^ 3] = exchange(mine, k ^ 3, size)
+        blocks[k ^ 3] = exchange(queries, k ^ 3, size)
     for k in near:
         blocks[k | 1] = exchange(blocks[k], 1, size)
     for k in near:

time: 33.7 us -> 33.3 us (0.988)
  waiting for transfers between devices: 5.41 us -> 3.71 us
  starting transfers between devices: 11.1 us -> 12.6 us
    ppermute x7, waiting for transfers between devices: 5.41 us -> 3.71 us  [exchange(): return lax.ppermute(block, 'ref', [(i, i ^ offset) for i in range(size)])]
    ppermute x7, starting transfers between devices: 11.1 us -> 12.6 us  [exchange(): return lax.ppermute(block, 'ref', [(i, i ^ offset) for i in range(size)])]
  transfers between devices with their start and end apart: 7 -> 7, of which waited for: 3 -> 2; matrix products, arithmetic and copies ran while one was open for 0% -> 0% of each run, Pallas kernels for 10% -> 10%
where the time goes in v6:
time: 33.3 us; the launch traced here: 33.1 us
  starting transfers between devices  12.6 us (38%)
  blocking collectives  11.8 us (35%)
  Pallas kernels  5.02 us (15%)
  waiting for transfers between devices  3.71 us (11%)
    ppermute x7, starting transfers between devices, exchange(): return lax.ppermute(block, 'ref', [(i, i ^ offset) for i in range(size)])  12.6 us
    all_to_all x1, blocking collectives, per_device(): lax.all_to_all(sent, ('win', 'ref'), split_axis=0, concat_axis=0, tiled=T...  11.8 us
    ppermute x7, waiting for transfers between devices, exchange(): return lax.ppermute(block, 'ref', [(i, i ^ offset) for i in range(size)])  3.71 us
    pallas_call x1, Pallas kernels, stage(): pl.pallas_call(stage_body, out_shape=(pltpu.VMEM(references.shape, narrow...  2.38 us
    pallas_call x1, Pallas kernels, pool(): pl.pallas_call(pool_body, out_shape=pltpu.VMEM((len(queries), A, windows...  0.91 us
    pallas_call x1, Pallas kernels, pool_last(): pl.pallas_call(functools.partial(last_body, late, groups), out_shape=pltp...  0.91 us
    pallas_call x1, Pallas kernels, finish(): pl.pallas_call(functools.partial(finish_body, win, refs, windows), out_sh...  0.82 us
  transfers between devices with their start and end apart: 7, of which 2 were waited for; matrix products, arithmetic and copies ran while one was open for 0% of the time, Pallas kernels for 10%

profile of v6, /device:TPU:0, one launch (start us, length us, event | category | flops | bytes accessed | tf_op | source)
XLA Modules:
  0.0 33.1 jit_solution(7471924475923729708)
XLA Ops:
  0.0 5.0 %collective-permute-start.1 = (bf16[32,2048]{1,0:T(8,128)(2,1)}, bf16[32,2048]{1,0:T(8,128)(2,1)S(1)}, u32[]{:S(2)}, u32[]{:S(2)}) collective-permute-start(bf16[32,2048]{1,0:T(8,128)(2,1)} %queries_ref.1), channel_id=1, source_target_pairs={{0,24},{4,28},{8,16},{12,20},{16,8},{20,12},{24,0},{28,4},{1,25},{... | collective-permute-start | bytes 393224 | tf_op jit(solution)/shard_map/ppermute | solution.py:225
  5.0 0.0 collective-permute-start.4
  5.1 1.5 %collective-permute-start.6 = (bf16[32,2048]{1,0:T(8,128)(2,1)}, bf16[32,2048]{1,0:T(8,128)(2,1)S(1)}, u32[]{:S(2)}, u32[]{:S(2)}) collective-permute-start(bf16[32,2048]{1,0:T(8,128)(2,1)} %queries_ref.1), channel_id=1, source_target_pairs={{0,4},{4,0},{8,12},{12,8},{16,20},{20,16},{24,28},{28,24},{1,5},{5... | collective-permute-start | bytes 393224 | tf_op jit(solution)/shard_map/ppermute | solution.py:225
  6.5 0.5 %collective-permute-start = (bf16[32,2048]{1,0:T(8,128)(2,1)}, bf16[32,2048]{1,0:T(8,128)(2,1)S(1)}, u32[]{:S(2)}, u32[]{:S(2)}) collective-permute-start(bf16[32,2048]{1,0:T(8,128)(2,1)} %queries_ref.1), channel_id=1, source_target_pairs={{0,20},{4,16},{8,28},{12,24},{16,4},{20,0},{24,12},{28,8},{1,21},{... | collective-permute-start | bytes 393224 | tf_op jit(solution)/shard_map/ppermute | solution.py:225
  7.1 2.6 %collective-permute-done.1.rest_3_ = bf16[32,2048]{1,0:T(8,128)(2,1)S(1)} collective-permute-done((bf16[32,2048]{1,0:T(8,128)(2,1)}, bf16[32,2048]{1,0:T(8,128)(2,1)S(1)}, u32[]{:S(2)}, u32[]{:S(2)}) %collective-permute-start.1) | collective-permute-done | bytes 131104 | tf_op jit(solution)/shard_map/ppermute | solution.py:225
  9.6 1.7 %collective-permute-start.2 = (bf16[32,2048]{1,0:T(8,128)(2,1)S(1)}, bf16[32,2048]{1,0:T(8,128)(2,1)S(1)}, u32[]{:S(2)}, u32[]{:S(2)}) collective-permute-start(bf16[32,2048]{1,0:T(8,128)(2,1)S(1)} %collective-permute-done.1.rest_3_), channel_id=1, source_target_pairs={{0,4},{4,0},{8,12},{12,8},{16,20},{20,16},{24,28},{28,24},{1,5},{5... | collective-permute-start | bytes 393224 | tf_op jit(solution)/shard_map/ppermute | solution.py:225
  11.3 3.3 %collective-permute-start.3 = (bf16[32,2048]{1,0:T(8,128)(2,1)S(1)}, bf16[32,2048]{1,0:T(8,128)(2,1)S(1)}, u32[]{:S(2)}, u32[]{:S(2)}) collective-permute-start(bf16[32,2048]{1,0:T(8,128)(2,1)S(1)} %collective-permute-done.1.rest_3_), channel_id=1, source_target_pairs={{0,8},{4,12},{8,0},{12,4},{16,24},{20,28},{24,16},{28,20},{1,9},{5... | collective-permute-start | bytes 393224 | tf_op jit(solution)/shard_map/ppermute | solution.py:225
  14.6 0.0 collective-permute-done.4.rest_2_
  14.6 0.5 %collective-permute-start.5 = (bf16[32,2048]{1,0:T(8,128)(2,1)S(1)}, bf16[32,2048]{1,0:T(8,128)(2,1)S(1)}, u32[]{:S(2)}, u32[]{:S(2)}) collective-permute-start(bf16[32,2048]{1,0:T(8,128)(2,1)S(1)} %collective-permute-done.4.rest_2_), channel_id=1, source_target_pairs={{0,4},{4,0},{8,12},{12,8},{16,20},{20,16},{24,28},{28,24},{1,5},{5... | collective-permute-start | bytes 393224 | tf_op jit(solution)/shard_map/ppermute | solution.py:225
  15.1 2.4 %stage.1 = (f8e4m3fn[1024,2048]{1,0:T(32,128)(4,1)S(1)}, bf16[32,2048]{1,0:T(8,128)(2,1)S(1)}, f32[8,8,128]{2,1,0:T(8,128)S(1)}, f32[10,8,128]{2,1,0:T(8,128)S(1)}) custom-call(bf16[1024,2048]{1,0:T(8,128)(2,1)} %refs_ref.1, bf16[32,2048]{1,0:T(8,128)(2,1)} %queries_ref.1, s32[8]{0:T(128)} %labels_in.1, f32[8,9]{1,0:T(8,128)} %bitcast.4, f32[1,8]{1,0:T(1,128)} %bitcast.5), custom_call_target="tpu_custom_call" | custom-call | flops 2097152 | bytes 6291456 | tf_op jit(solution)/shard_map/stage/pallas_call | solution.py:80
  17.5 0.0 collective-permute-done.6.rest_1_
  17.5 0.9 %pool.1.rest_4_ = f32[4,8,128]{2,1,0:T(8,128)S(1)} custom-call(f32[8,8,128]{2,1,0:T(8,128)S(1)} %get-tuple-element.10.members_ref, f8e4m3fn[1024,2048]{1,0:T(32,128)(4,1)S(1)} %get-tuple-element.11.refs_ref, bf16[32,2048]{1,0:T(8,128)(2,1)S(1)} %get-tuple-element.12.rest_0_, bf16[32,2048]{1,0:T(8,128)(2,1)S(1)} %collective-permute-done.6.rest_1_, ...), custom_call_target="tpu_custom_call" | custom-call | flops 536870912 | bytes 2097152 | tf_op jit(solution)/shard_map/pool/pallas_call | solution.py:164
  18.4 0.0 collective-permute-done.rest_0_
  18.4 0.0 collective-permute-done.2.rest_1_
  18.4 0.0 collective-permute-done.3.rest_2_
  18.4 1.1 %collective-permute-done.5.rest_3_ = bf16[32,2048]{1,0:T(8,128)(2,1)S(1)} collective-permute-done((bf16[32,2048]{1,0:T(8,128)(2,1)S(1)}, bf16[32,2048]{1,0:T(8,128)(2,1)S(1)}, u32[]{:S(2)}, u32[]{:S(2)}) %collective-permute-start.5) | collective-permute-done | bytes 131104 | tf_op jit(solution)/shard_map/ppermute | solution.py:225
  19.6 0.9 %pool_last.1 = f32[4,8,8,128]{3,2,1,0:T(8,128)S(1)} custom-call(f32[8,8,128]{2,1,0:T(8,128)S(1)} %get-tuple-element.10.members_ref, f8e4m3fn[1024,2048]{1,0:T(32,128)(4,1)S(1)} %get-tuple-element.11.refs_ref, bf16[32,2048]{1,0:T(8,128)(2,1)S(1)} %collective-permute-done.rest_0_, bf16[32,2048]{1,0:T(8,128)(2,1)S(1)} %collective-permute-done.2.rest_1_, ...), custom_call_target="tpu_custom_call" | custom-call | flops 536870912 | bytes 2097152 | tf_op jit(solution)/shard_map/pool_last/pallas_call | solution.py:178
  20.5 11.8 %all_to_all.5.in_ref = f32[32,8,128]{2,1,0:T(8,128)S(1)} all-to-all(f32[32,8,128]{2,1,0:T(8,128)S(1)} %bitcast.3), channel_id=1, replica_groups=mesh['ref'=8,'win'=4] {'win','ref'}, dimensions={0} | all-to-all | bytes 262144 | tf_op jit(solution)/shard_map/all_to_all | solution.py:264
  32.3 0.8 %finish.1 = f32[4,8,32]{2,1,0:T(8,128)} custom-call(f32[10,8,128]{2,1,0:T(8,128)S(1)} %get-tuple-element.9.consts_ref, f32[32,8,128]{2,1,0:T(8,128)S(1)} %all_to_all.5.in_ref), custom_call_target="tpu_custom_call" | custom-call | tf_op jit(solution)/shard_map/finish/pallas_call | solution.py:215
Async XLA Ops:
  0.0 9.6 %collective-permute-start.1 = (bf16[32,2048]{1,0:T(8,128)(2,1)}, bf16[32,2048]{1,0:T(8,128)(2,1)S(1)}, u32[]{:S(2)}, u32[]{:S(2)}) collective-permute-start(bf16[32,2048]{1,0:T(8,128)(2,1)} %queries_ref.1), channel_id=1, source_target_pairs={{0,24},{4,28},{8,16},{12,20},{16,8},{20,12},{24,0},{28,4},{1,25},{... | collective-permute-start | bytes 393224 | tf_op jit(solution)/shard_map/ppermute | solution.py:225
  5.0 9.6 %collective-permute-start.4 = (bf16[32,2048]{1,0:T(8,128)(2,1)}, bf16[32,2048]{1,0:T(8,128)(2,1)S(1)}, u32[]{:S(2)}, u32[]{:S(2)}) collective-permute-start(bf16[32,2048]{1,0:T(8,128)(2,1)} %queries_ref.1), channel_id=1, source_target_pairs={{0,8},{4,12},{8,0},{12,4},{16,24},{20,28},{24,16},{28,20},{1,9},{5... | collective-permute-start | bytes 393224 | tf_op jit(solution)/shard_map/ppermute | solution.py:225
  5.1 12.4 %collective-permute-start.6 = (bf16[32,2048]{1,0:T(8,128)(2,1)}, bf16[32,2048]{1,0:T(8,128)(2,1)S(1)}, u32[]{:S(2)}, u32[]{:S(2)}) collective-permute-start(bf16[32,2048]{1,0:T(8,128)(2,1)} %queries_ref.1), channel_id=1, source_target_pairs={{0,4},{4,0},{8,12},{12,8},{16,20},{20,16},{24,28},{28,24},{1,5},{5... | collective-permute-start | bytes 393224 | tf_op jit(solution)/shard_map/ppermute | solution.py:225
  6.5 11.9 %collective-permute-start = (bf16[32,2048]{1,0:T(8,128)(2,1)}, bf16[32,2048]{1,0:T(8,128)(2,1)S(1)}, u32[]{:S(2)}, u32[]{:S(2)}) collective-permute-start(bf16[32,2048]{1,0:T(8,128)(2,1)} %queries_ref.1), channel_id=1, source_target_pairs={{0,20},{4,16},{8,28},{12,24},{16,4},{20,0},{24,12},{28,8},{1,21},{... | collective-permute-start | bytes 393224 | tf_op jit(solution)/shard_map/ppermute | solution.py:225
  9.6 8.8 %collective-permute-start.2 = (bf16[32,2048]{1,0:T(8,128)(2,1)S(1)}, bf16[32,2048]{1,0:T(8,128)(2,1)S(1)}, u32[]{:S(2)}, u32[]{:S(2)}) collective-permute-start(bf16[32,2048]{1,0:T(8,128)(2,1)S(1)} %collective-permute-done.1.rest_3_), channel_id=1, source_target_pairs={{0,4},{4,0},{8,12},{12,8},{16,20},{20,16},{24,28},{28,24},{1,5},{5... | collective-permute-start | bytes 393224 | tf_op jit(solution)/shard_map/ppermute | solution.py:225
  11.3 7.1 %collective-permute-start.3 = (bf16[32,2048]{1,0:T(8,128)(2,1)S(1)}, bf16[32,2048]{1,0:T(8,128)(2,1)S(1)}, u32[]{:S(2)}, u32[]{:S(2)}) collective-permute-start(bf16[32,2048]{1,0:T(8,128)(2,1)S(1)} %collective-permute-done.1.rest_3_), channel_id=1, source_target_pairs={{0,8},{4,12},{8,0},{12,4},{16,24},{20,28},{24,16},{28,20},{1,9},{5... | collective-permute-start | bytes 393224 | tf_op jit(solution)/shard_map/ppermute | solution.py:225
  14.6 5.0 %collective-permute-start.5 = (bf16[32,2048]{1,0:T(8,128)(2,1)S(1)}, bf16[32,2048]{1,0:T(8,128)(2,1)S(1)}, u32[]{:S(2)}, u32[]{:S(2)}) collective-permute-start(bf16[32,2048]{1,0:T(8,128)(2,1)S(1)} %collective-permute-done.4.rest_2_), channel_id=1, source_target_pairs={{0,4},{4,0},{8,12},{12,8},{16,20},{20,16},{24,28},{28,24},{1,5},{5... | collective-permute-start | bytes 393224 | tf_op jit(solution)/shard_map/ppermute | solution.py:225

commit v7 on v6

--- a/solution.py
+++ b/solution.py
@@ -13,6 +13,7 @@
 TAPS = 9
 HALF = TAPS // 2
 LAST = 4
+PART = 256
 
 LOG2E = 1.4426950408889634
 SCALE = 256.0 / S
@@ -24,11 +25,12 @@
 
 
 def pool_window(scores, members):
-    count = scores.shape[1]
-    blocks = scores.shape[0] // BLOCK
+    count = scores[0].shape[1]
+    per = scores[0].shape[0] // BLOCK
+    blocks = per * len(scores)
     peaks, totals = [], []
     for b in range(blocks):
-        part = scores[b * BLOCK : (b + 1) * BLOCK]
+        part = scores[b // per][b % per * BLOCK : (b % per + 1) * BLOCK]
         peak = jnp.max(part, axis=0, keepdims=True)
         totals.append(jnp.sum(jnp.exp2((part - peak) * (SCALE * LOG2E)), axis=0, keepdims=True))
         peaks.append(peak)
@@ -43,7 +45,7 @@
 
 
 def stage_body(
-    refs_ref, queries_ref, labels_in, taps_in, bias_in,
+    refs_ref, queries_ref, labels_in, taps_in, bias_in, _,
     out_ref, mine_ref, members_ref, consts_ref,
     chunks, labels_ref, taps_ref, bias_ref, sems,
 ):
@@ -73,7 +75,7 @@
         out_ref[c * step : (c + 1) * step] = chunks[c].astype(narrow)
 
 
-def stage(references, queries, labels, kernel, class_bias):
+def stage(references, queries, labels, kernel, class_bias, block):
     step = 128
     count = references.shape[0] // step
     operands = (references, queries, labels, kernel.T, class_bias[None, :])
@@ -85,7 +87,7 @@
             pltpu.VMEM((references.shape[0] // BLOCK, A, BLOCK), jnp.float32),
             pltpu.VMEM((TAPS + 1, A, BLOCK), jnp.float32),
         ),
-        in_specs=[anywhere] * len(operands),
+        in_specs=[anywhere] * (len(operands) + 1),
         out_specs=(vmem,) * 4,
         scratch_shapes=[
             pltpu.VMEM((count, step, references.shape[1]), references.dtype),
@@ -99,12 +101,16 @@
         ),
         compiler_params=pltpu.CompilerParams(vmem_limit_bytes=40 << 20),
         name="stage",
-    )(*(pltpu.with_memory_space_constraint(x, pltpu.HBM) for x in operands))
+    )(
+        *(pltpu.with_memory_space_constraint(x, pltpu.HBM) for x in operands),
+        pltpu.with_memory_space_constraint(block, pltpu.VMEM),
+    )
 
 
 def pool_tiles(members_ref, refs_ref, query_refs):
     windows = refs_ref.shape[1] // S
-    rows = query_refs[0].shape[0]
+    odd = lax.axis_index("win") % 2 == 1
+    rows = query_refs[0][0].shape[0]
     count = rows * len(query_refs)
     members = [members_ref[b] > 0.5 for b in range(members_ref.shape[0])]
     if count != BLOCK:
@@ -114,13 +120,21 @@
     pooled = []
     for window in range(windows):
         cols = slice(window * S, (window + 1) * S)
-        queries = jnp.concatenate([q[:, cols] for q in query_refs], axis=0)
-        scores = lax.dot_general(
-            refs_ref[:, cols],
-            queries.astype(narrow),
-            (((1,), (1,)), ((), ())),
-            preferred_element_type=jnp.float32,
+        queries = jnp.concatenate(
+            [q[0][:, cols] if len(q) == 1 else jnp.where(odd, q[1][:, cols], q[0][:, cols]) for q in query_refs],
+            axis=0,
         )
+        queries = queries.astype(narrow)
+        parts = refs_ref.shape[0] // PART
+        scores = [
+            lax.dot_general(
+                refs_ref[part * PART : (part + 1) * PART, cols],
+                queries,
+                (((1,), (1,)), ((), ())),
+                preferred_element_type=jnp.float32,
+            )
+            for part in range(parts)
+        ]
         pooled.append(pool_window(scores, members))
     return [
         jnp.concatenate([p[:, j * rows : (j + 1) * rows] for p in pooled], axis=1)
@@ -128,13 +142,18 @@
     ]
 
 
-def pool_body(members_ref, refs_ref, *rest):
+def grouped(refs, sizes):
+    refs = list(refs)
+    return [[refs.pop(0) for _ in range(size)] for size in sizes]
+
+
+def pool_body(sizes, members_ref, refs_ref, *rest):
     out_ref = rest[-1]
-    for j, tile in enumerate(pool_tiles(members_ref, refs_ref, rest[:-1])):
+    for j, tile in enumerate(pool_tiles(members_ref, refs_ref, grouped(rest[:-1], sizes))):
         out_ref[j] = tile
 
 
-def last_body(late, groups, members_ref, refs_ref, *rest):
+def last_body(late, groups, sizes, members_ref, refs_ref, *rest):
     out_ref = rest[-1]
     here = lax.axis_index("ref")
 
@@ -142,15 +161,15 @@
         for v in range(out_ref.shape[0]):
             out_ref[v, here ^ offset] = tile
 
-    for ref, offsets in zip(rest[len(late) : -1], groups, strict=True):
+    for ref, offsets in zip(rest[sum(sizes) : -1], groups, strict=True):
         for j, offset in enumerate(offsets):
             place(offset, ref[j])
-    for offset, tile in zip(late, pool_tiles(members_ref, refs_ref, rest[: len(late)]), strict=True):
+    for offset, tile in zip(late, pool_tiles(members_ref, refs_ref, grouped(rest[: sum(sizes)], sizes)), strict=True):
         place(offset, tile)
 
 
 def pool_cost(refs, queries):
-    count = sum(q.shape[0] for q in queries)
+    count = sum(q[0].shape[0] for q in queries)
     return pl.CostEstimate(
         flops=2 * refs.size * count,
         bytes_accessed=refs.size,
@@ -160,30 +179,32 @@
 
 def pool(members, refs, queries):
     windows = refs.shape[1] // S
-    rows = queries[0].shape[0]
+    rows = queries[0][0].shape[0]
+    sizes = [len(q) for q in queries]
     return pl.pallas_call(
-        pool_body,
+        functools.partial(pool_body, sizes),
         out_shape=pltpu.VMEM((len(queries), A, windows * rows), jnp.float32),
-        in_specs=[vmem] * (2 + len(queries)),
+        in_specs=[vmem] * (2 + sum(sizes)),
         out_specs=vmem,
         cost_estimate=pool_cost(refs, queries),
         compiler_params=pltpu.CompilerParams(vmem_limit_bytes=40 << 20),
         name="pool",
-    )(members, refs, *queries)
+    )(members, refs, *sum(map(list, queries), []))
 
 
 def pool_last(members, refs, queries, late, tiles, groups, win, count):
     windows = refs.shape[1] // S
-    rows = queries[0].shape[0]
+    rows = queries[0][0].shape[0]
+    sizes = [len(q) for q in queries]
     return pl.pallas_call(
-        functools.partial(last_body, late, groups),
+        functools.partial(last_body, late, groups, sizes),
         out_shape=pltpu.VMEM((win, count, A, windows * rows), jnp.float32),
-        in_specs=[vmem] * (2 + len(queries) + len(tiles)),
+        in_specs=[vmem] * (2 + sum(sizes) + len(tiles)),
         out_specs=vmem,
         cost_estimate=pool_cost(refs, queries),
         compiler_params=pltpu.CompilerParams(vmem_limit_bytes=40 << 20),
         name="pool_last",
-    )(members, refs, *queries, *tiles)
+    )(members, refs, *sum(map(list, queries), []), *tiles)
 
 
 def finish_body(win, refs, windows, consts_ref, in_ref, out_ref):
@@ -225,41 +246,54 @@
     return lax.ppermute(block, "ref", [(i, i ^ offset) for i in range(size)])
 
 
-def gather_queries(queries, mine, size, early):
+def exchange_some(block, offset, size, core):
+    wins = lax.axis_size("win")
+    pairs = [
+        (i * wins + w, (i ^ offset) * wins + w)
+        for w in range(core, wins, 2)
+        for i in range(size)
+    ]
+    return lax.ppermute(block, ("ref", "win"), pairs)
+
+
+def gather_queries(queries, size):
     near = [k for k in range(4, size, 2) if k & 2]
-    blocks = {0: mine}
+    blocks = {}
     for k in near + [2, 1]:
         blocks[k] = exchange(queries, k, size)
-    first = [0, 1, 2, near[-1]]
-    early({k: blocks[k] for k in first})
     for k in near:
-        blocks[k ^ 3] = exchange(queries, k ^ 3, size)
+        blocks[k ^ 3] = (
+            exchange_some(queries, k ^ 3, size, 0),
+            exchange_some(blocks[1], k ^ 2, size, 1),
+        )
     for k in near:
         blocks[k | 1] = exchange(blocks[k], 1, size)
     for k in near:
         blocks[k ^ 2] = exchange(blocks[k], 2, size)
     blocks[3] = exchange(blocks[2], 1, size)
-    rest = [k for k in blocks if k not in first]
-    for k in range(0, len(rest) - LAST, LAST):
-        early({j: blocks[j] for j in rest[k : k + LAST]})
     return blocks
+
+
+def as_tuple(block):
+    return block if isinstance(block, tuple) else (block,)
 
 
 def per_device(queries, references, labels, kernel, class_bias):
     refs, win = lax.axis_size("ref"), lax.axis_size("win")
     windows = references.shape[1] // S
     rows = queries.shape[0]
-    staged, mine, members, consts = stage(references, queries, labels, kernel, class_bias)
-    tiles, groups = [], []
-
-    def early(blocks):
-        groups.append(list(blocks))
-        tiles.append(pool(members, staged, list(blocks.values())))
-        return tiles[-1]
-
-    blocks = gather_queries(queries, mine, refs, early)
-    late = [k for k in blocks if k not in sum(groups, [])]
-    sent = pool_last(members, staged, [blocks[k] for k in late], late, tiles, groups, win, refs)
+    blocks = gather_queries(queries, refs)
+    staged, mine, members, consts = stage(
+        references, queries, labels, kernel, class_bias, blocks[2]
+    )
+    blocks[0] = mine
+    first = [0, 1, 2, refs - 2]
+    rest = [k for k in blocks if k not in first]
+    cut = len(rest) - LAST
+    groups = [first] + [rest[k : k + LAST] for k in range(0, cut, LAST)]
+    late = rest[cut:]
+    tiles = [pool(members, staged, [as_tuple(blocks[k]) for k in group]) for group in groups]
+    sent = pool_last(members, staged, [as_tuple(blocks[k]) for k in late], late, tiles, groups, win, refs)
     sent = sent.reshape((win * refs,) + sent.shape[2:])
     received = lax.all_to_all(sent, ("win", "ref"), split_axis=0, concat_axis=0, tiled=True)
     return finish(received, consts, win, refs, windows, rows)

time: 33.3 us -> 32.6 us (0.979)
  waiting for transfers between devices: 3.71 us -> 2.26 us
  starting transfers between devices: 12.6 us -> 13.3 us
    ppermute x0 -> x2, starting transfers between devices: none -> 3.09 us  [exchange_some(): return lax.ppermute(block, ('ref', 'win'), pairs)]
    ppermute x7 -> x6, starting transfers between devices: 12.6 us -> 10.2 us  [exchange(): return lax.ppermute(block, 'ref', [(i, i ^ offset) for i in range(size)])]
    ppermute x7 -> x6, waiting for transfers between devices: 3.71 us -> 2.25 us  [exchange(): return lax.ppermute(block, 'ref', [(i, i ^ offset) for i in range(size)])]
  transfers between devices with their start and end apart: 7 -> 8, of which waited for: 2 -> 2; matrix products, arithmetic and copies ran while one was open for 0% -> 0% of each run, Pallas kernels for 10% -> 10%
where the time goes in v7:
time: 32.6 us; the launch traced here: 32.4 us
  starting transfers between devices  13.3 us (41%)
  blocking collectives  11.9 us (37%)
  Pallas kernels  4.86 us (15%)
  waiting for transfers between devices  2.26 us (7%)
    all_to_all x1, blocking collectives, per_device(): lax.all_to_all(sent, ('win', 'ref'), split_axis=0, concat_axis=0, tiled=T...  11.9 us
    ppermute x6, starting transfers between devices, exchange(): return lax.ppermute(block, 'ref', [(i, i ^ offset) for i in range(size)])  10.2 us
    ppermute x2, starting transfers between devices, exchange_some(): return lax.ppermute(block, ('ref', 'win'), pairs)  3.09 us
    pallas_call x1, Pallas kernels, stage(): pl.pallas_call(stage_body, out_shape=(pltpu.VMEM(references.shape, narrow...  2.38 us
    ppermute x6, waiting for transfers between devices, exchange(): return lax.ppermute(block, 'ref', [(i, i ^ offset) for i in range(size)])  2.25 us
    pallas_call x1, Pallas kernels, pool_last(): pl.pallas_call(functools.partial(last_body, late, groups, sizes), out_sha...  0.84 us
    pallas_call x1, Pallas kernels, finish(): pl.pallas_call(functools.partial(finish_body, win, refs, windows), out_sh...  0.82 us
    pallas_call x1, Pallas kernels, pool(): pl.pallas_call(functools.partial(pool_body, sizes), out_shape=pltpu.VMEM(...  0.82 us
  transfers between devices with their start and end apart: 8, of which 2 were waited for; matrix products, arithmetic and copies ran while one was open for 0% of the time, Pallas kernels for 10%

profile of v7, /device:TPU:0, one launch (start us, length us, event | category | flops | bytes accessed | tf_op | source)
XLA Modules:
  0.0 32.4 jit_solution(15650171523169943771)
XLA Ops:
  0.0 5.0 %collective-permute-start.4 = (bf16[32,2048]{1,0:T(8,128)(2,1)}, bf16[32,2048]{1,0:T(8,128)(2,1)S(1)}, u32[]{:S(2)}, u32[]{:S(2)}) collective-permute-start(bf16[32,2048]{1,0:T(8,128)(2,1)} %queries_ref.1), channel_id=1, source_target_pairs={{0,24},{4,28},{8,16},{12,20},{16,8},{20,12},{24,0},{28,4},{1,25},{... | collective-permute-start | bytes 393224 | tf_op jit(solution)/shard_map/ppermute | solution.py:246
  5.0 0.0 collective-permute-start
  5.1 1.5 %collective-permute-start.2 = (bf16[32,2048]{1,0:T(8,128)(2,1)}, bf16[32,2048]{1,0:T(8,128)(2,1)S(1)}, u32[]{:S(2)}, u32[]{:S(2)}) collective-permute-start(bf16[32,2048]{1,0:T(8,128)(2,1)} %queries_ref.1), channel_id=1, source_target_pairs={{0,4},{4,0},{8,12},{12,8},{16,20},{20,16},{24,28},{28,24},{1,5},{5... | collective-permute-start | bytes 393224 | tf_op jit(solution)/shard_map/ppermute | solution.py:246
  6.5 2.4 %collective-permute-start.1 = (bf16[32,2048]{1,0:T(8,128)(2,1)}, bf16[32,2048]{1,0:T(8,128)(2,1)S(1)}, u32[]{:S(2)}, u32[]{:S(2)}) collective-permute-start(bf16[32,2048]{1,0:T(8,128)(2,1)} %queries_ref.1), channel_id=1, source_target_pairs={{0,20},{4,16},{8,28},{12,24},{16,4},{20,0},{24,12},{28,8},{2,22},{... | collective-permute-start | bytes 393224 | tf_op jit(solution)/shard_map/ppermute | solution.py:256
  9.0 0.6 %collective-permute-done.4.rest_3_ = bf16[32,2048]{1,0:T(8,128)(2,1)S(1)} collective-permute-done((bf16[32,2048]{1,0:T(8,128)(2,1)}, bf16[32,2048]{1,0:T(8,128)(2,1)S(1)}, u32[]{:S(2)}, u32[]{:S(2)}) %collective-permute-start.4) | collective-permute-done | bytes 131104 | tf_op jit(solution)/shard_map/ppermute | solution.py:246
  9.6 1.7 %collective-permute-start.5 = (bf16[32,2048]{1,0:T(8,128)(2,1)S(1)}, bf16[32,2048]{1,0:T(8,128)(2,1)S(1)}, u32[]{:S(2)}, u32[]{:S(2)}) collective-permute-start(bf16[32,2048]{1,0:T(8,128)(2,1)S(1)} %collective-permute-done.4.rest_3_), channel_id=1, source_target_pairs={{0,4},{4,0},{8,12},{12,8},{16,20},{20,16},{24,28},{28,24},{1,5},{5... | collective-permute-start | bytes 393224 | tf_op jit(solution)/shard_map/ppermute | solution.py:246
  11.3 1.4 %collective-permute-start.6 = (bf16[32,2048]{1,0:T(8,128)(2,1)S(1)}, bf16[32,2048]{1,0:T(8,128)(2,1)S(1)}, u32[]{:S(2)}, u32[]{:S(2)}) collective-permute-start(bf16[32,2048]{1,0:T(8,128)(2,1)S(1)} %collective-permute-done.4.rest_3_), channel_id=1, source_target_pairs={{0,8},{4,12},{8,0},{12,4},{16,24},{20,28},{24,16},{28,20},{1,9},{5... | collective-permute-start | bytes 393224 | tf_op jit(solution)/shard_map/ppermute | solution.py:246
  12.8 0.0 collective-permute-done._.rest_2_
  12.8 0.5 %collective-permute-start.7 = (bf16[32,2048]{1,0:T(8,128)(2,1)S(1)}, bf16[32,2048]{1,0:T(8,128)(2,1)S(1)}, u32[]{:S(2)}, u32[]{:S(2)}) collective-permute-start(bf16[32,2048]{1,0:T(8,128)(2,1)S(1)} %collective-permute-done._.rest_2_), channel_id=1, source_target_pairs={{0,4},{4,0},{8,12},{12,8},{16,20},{20,16},{24,28},{28,24},{1,5},{5... | collective-permute-start | bytes 393224 | tf_op jit(solution)/shard_map/ppermute | solution.py:246
  13.3 0.0 collective-permute-done.2.rest_1_
  13.3 0.7 %collective-permute-start.3 = (bf16[32,2048]{1,0:T(8,128)(2,1)S(1)}, bf16[32,2048]{1,0:T(8,128)(2,1)S(1)}, u32[]{:S(2)}, u32[]{:S(2)}) collective-permute-start(bf16[32,2048]{1,0:T(8,128)(2,1)S(1)} %collective-permute-done.2.rest_1_), channel_id=1, source_target_pairs={{1,17},{5,21},{9,25},{13,29},{17,1},{21,5},{25,9},{29,13},{3,19},{... | collective-permute-start | bytes 393224 | tf_op jit(solution)/shard_map/ppermute | solution.py:256
  14.0 2.4 %stage.1 = (f8e4m3fn[1024,2048]{1,0:T(32,128)(4,1)S(1)}, bf16[32,2048]{1,0:T(8,128)(2,1)S(1)}, f32[8,8,128]{2,1,0:T(8,128)S(1)}, f32[10,8,128]{2,1,0:T(8,128)S(1)}) custom-call(bf16[1024,2048]{1,0:T(8,128)(2,1)} %refs_ref.1, bf16[32,2048]{1,0:T(8,128)(2,1)} %queries_ref.1, s32[8]{0:T(128)} %labels_in.1, f32[8,9]{1,0:T(8,128)} %bitcast.4, f32[1,8]{1,0:T(1,128)} %bitcast.5, ...), custom_call_target="tpu_custom_call" | custom-call | flops 2097152 | bytes 6291456 | tf_op jit(solution)/shard_map/stage/pallas_call | solution.py:82
  16.4 0.8 %pool.1.rest_5_ = f32[4,8,128]{2,1,0:T(8,128)S(1)} custom-call(f32[8,8,128]{2,1,0:T(8,128)S(1)} %get-tuple-element.10.members_ref, f8e4m3fn[1024,2048]{1,0:T(32,128)(4,1)S(1)} %get-tuple-element.11.refs_ref, bf16[32,2048]{1,0:T(8,128)(2,1)S(1)} %get-tuple-element.12.rest_0_, bf16[32,2048]{1,0:T(8,128)(2,1)S(1)} %collective-permute-done.2.rest_1_, ...), custom_call_target="tpu_custom_call" | custom-call | flops 536870912 | bytes 2097152 | tf_op jit(solution)/shard_map/pool/pallas_call | solution.py:184
  17.2 0.0 collective-permute-done.1.rest_0_
  17.2 0.0 collective-permute-done.5.rest_2_
  17.2 0.0 collective-permute-done.6.rest_3_
  17.2 1.6 %collective-permute-done.7.rest_4_ = bf16[32,2048]{1,0:T(8,128)(2,1)S(1)} collective-permute-done((bf16[32,2048]{1,0:T(8,128)(2,1)S(1)}, bf16[32,2048]{1,0:T(8,128)(2,1)S(1)}, u32[]{:S(2)}, u32[]{:S(2)}) %collective-permute-start.7) | collective-permute-done | bytes 131104 | tf_op jit(solution)/shard_map/ppermute | solution.py:246
  18.8 0.0 collective-permute-done.3.rest_1_
  18.8 0.8 %pool_last.1 = f32[4,8,8,128]{3,2,1,0:T(8,128)S(1)} custom-call(f32[8,8,128]{2,1,0:T(8,128)S(1)} %get-tuple-element.10.members_ref, f8e4m3fn[1024,2048]{1,0:T(32,128)(4,1)S(1)} %get-tuple-element.11.refs_ref, bf16[32,2048]{1,0:T(8,128)(2,1)S(1)} %collective-permute-done.1.rest_0_, bf16[32,2048]{1,0:T(8,128)(2,1)S(1)} %collective-permute-done.3.rest_1_, ...), custom_call_target="tpu_custom_call" | custom-call | flops 536870912 | bytes 2097152 | tf_op jit(solution)/shard_map/pool_last/pallas_call | solution.py:199
  19.7 11.9 %all_to_all.5.in_ref = f32[32,8,128]{2,1,0:T(8,128)S(1)} all-to-all(f32[32,8,128]{2,1,0:T(8,128)S(1)} %bitcast.3), channel_id=1, replica_groups=mesh['ref'=8,'win'=4] {'win','ref'}, dimensions={0} | all-to-all | bytes 262144 | tf_op jit(solution)/shard_map/all_to_all | solution.py:298
  31.6 0.8 %finish.1 = f32[4,8,32]{2,1,0:T(8,128)} custom-call(f32[10,8,128]{2,1,0:T(8,128)S(1)} %get-tuple-element.9.consts_ref, f32[32,8,128]{2,1,0:T(8,128)S(1)} %all_to_all.5.in_ref), custom_call_target="tpu_custom_call" | custom-call | tf_op jit(solution)/shard_map/finish/pallas_call | solution.py:236
Async XLA Ops:
  0.0 9.6 %collective-permute-start.4 = (bf16[32,2048]{1,0:T(8,128)(2,1)}, bf16[32,2048]{1,0:T(8,128)(2,1)S(1)}, u32[]{:S(2)}, u32[]{:S(2)}) collective-permute-start(bf16[32,2048]{1,0:T(8,128)(2,1)} %queries_ref.1), channel_id=1, source_target_pairs={{0,24},{4,28},{8,16},{12,20},{16,8},{20,12},{24,0},{28,4},{1,25},{... | collective-permute-start | bytes 393224 | tf_op jit(solution)/shard_map/ppermute | solution.py:246
  5.0 7.7 %collective-permute-start = (bf16[32,2048]{1,0:T(8,128)(2,1)}, bf16[32,2048]{1,0:T(8,128)(2,1)S(1)}, u32[]{:S(2)}, u32[]{:S(2)}) collective-permute-start(bf16[32,2048]{1,0:T(8,128)(2,1)} %queries_ref.1), channel_id=1, source_target_pairs={{0,8},{4,12},{8,0},{12,4},{16,24},{20,28},{24,16},{28,20},{1,9},{5... | collective-permute-start | bytes 393224 | tf_op jit(solution)/shard_map/ppermute | solution.py:246
  5.1 8.3 %collective-permute-start.2 = (bf16[32,2048]{1,0:T(8,128)(2,1)}, bf16[32,2048]{1,0:T(8,128)(2,1)S(1)}, u32[]{:S(2)}, u32[]{:S(2)}) collective-permute-start(bf16[32,2048]{1,0:T(8,128)(2,1)} %queries_ref.1), channel_id=1, source_target_pairs={{0,4},{4,0},{8,12},{12,8},{16,20},{20,16},{24,28},{28,24},{1,5},{5... | collective-permute-start | bytes 393224 | tf_op jit(solution)/shard_map/ppermute | solution.py:246
  6.5 10.7 %collective-permute-start.1 = (bf16[32,2048]{1,0:T(8,128)(2,1)}, bf16[32,2048]{1,0:T(8,128)(2,1)S(1)}, u32[]{:S(2)}, u32[]{:S(2)}) collective-permute-start(bf16[32,2048]{1,0:T(8,128)(2,1)} %queries_ref.1), channel_id=1, source_target_pairs={{0,20},{4,16},{8,28},{12,24},{16,4},{20,0},{24,12},{28,8},{2,22},{... | collective-permute-start | bytes 393224 | tf_op jit(solution)/shard_map/ppermute | solution.py:256
  9.6 7.6 %collective-permute-start.5 = (bf16[32,2048]{1,0:T(8,128)(2,1)S(1)}, bf16[32,2048]{1,0:T(8,128)(2,1)S(1)}, u32[]{:S(2)}, u32[]{:S(2)}) collective-permute-start(bf16[32,2048]{1,0:T(8,128)(2,1)S(1)} %collective-permute-done.4.rest_3_), channel_id=1, source_target_pairs={{0,4},{4,0},{8,12},{12,8},{16,20},{20,16},{24,28},{28,24},{1,5},{5... | collective-permute-start | bytes 393224 | tf_op jit(solution)/shard_map/ppermute | solution.py:246
  11.3 5.9 %collective-permute-start.6 = (bf16[32,2048]{1,0:T(8,128)(2,1)S(1)}, bf16[32,2048]{1,0:T(8,128)(2,1)S(1)}, u32[]{:S(2)}, u32[]{:S(2)}) collective-permute-start(bf16[32,2048]{1,0:T(8,128)(2,1)S(1)} %collective-permute-done.4.rest_3_), channel_id=1, source_target_pairs={{0,8},{4,12},{8,0},{12,4},{16,24},{20,28},{24,16},{28,20},{1,9},{5... | collective-permute-start | bytes 393224 | tf_op jit(solution)/shard_map/ppermute | solution.py:246
  12.8 6.0 %collective-permute-start.7 = (bf16[32,2048]{1,0:T(8,128)(2,1)S(1)}, bf16[32,2048]{1,0:T(8,128)(2,1)S(1)}, u32[]{:S(2)}, u32[]{:S(2)}) collective-permute-start(bf16[32,2048]{1,0:T(8,128)(2,1)S(1)} %collective-permute-done._.rest_2_), channel_id=1, source_target_pairs={{0,4},{4,0},{8,12},{12,8},{16,20},{20,16},{24,28},{28,24},{1,5},{5... | collective-permute-start | bytes 393224 | tf_op jit(solution)/shard_map/ppermute | solution.py:246
  13.3 5.5 %collective-permute-start.3 = (bf16[32,2048]{1,0:T(8,128)(2,1)S(1)}, bf16[32,2048]{1,0:T(8,128)(2,1)S(1)}, u32[]{:S(2)}, u32[]{:S(2)}) collective-permute-start(bf16[32,2048]{1,0:T(8,128)(2,1)S(1)} %collective-permute-done.2.rest_1_), channel_id=1, source_target_pairs={{1,17},{5,21},{9,25},{13,29},{17,1},{21,5},{25,9},{29,13},{3,19},{... | collective-permute-start | bytes 393224 | tf_op jit(solution)/shard_map/ppermute | solution.py:256

commit v8 on v7

--- a/solution.py
+++ b/solution.py
@@ -219,12 +219,19 @@
 
     before = jnp.where(here > 0, centered(jnp.maximum(here - 1, 0)), 0.0)
     after = jnp.where(here < win - 1, centered(jnp.minimum(here + 1, win - 1)), 0.0)
-    padded = jnp.concatenate([before, centered(here), after], axis=1)
+    now = centered(here)
     width = windows * rows
-    total = jnp.zeros((A, width), jnp.float32)
-    for tap in range(TAPS):
-        start = width + (tap - HALF) * rows
-        total = total + consts_ref[tap][:, :width] * padded[:, start : start + width]
+    lane = lax.broadcasted_iota(jnp.int32, (A, width), 1)
+    total = consts_ref[HALF][:, :width] * now
+    for step in range(1, HALF + 1):
+        moved = step * rows
+        if moved == width:
+            low, high = before, after
+        else:
+            low = pltpu.roll(jnp.where(lane < width - moved, now, before), moved, 1)
+            high = pltpu.roll(jnp.where(lane >= moved, now, after), width - moved, 1)
+        total = total + consts_ref[HALF - step][:, :width] * low
+        total = total + consts_ref[HALF + step][:, :width] * high
     logits = total + consts_ref[TAPS][:, :width]
     shifted = logits - jnp.max(logits, axis=0, keepdims=True)
     result = shifted - jnp.log(jnp.sum(jnp.exp(shifted), axis=0, keepdims=True))

time: 32.6 us -> 32.6 us (level)
  no operation moved by 1% of the time
where the time goes in v8:
time: 32.6 us; the launch traced here: 32.4 us
  starting transfers between devices  13.3 us (41%)
  blocking collectives  11.9 us (37%)
  Pallas kernels  4.87 us (15%)
  waiting for transfers between devices  2.26 us (7%)
    all_to_all x1, blocking collectives, per_device(): lax.all_to_all(sent, ('win', 'ref'), split_axis=0, concat_axis=0, tiled=T...  11.9 us
    ppermute x6, starting transfers between devices, exchange(): return lax.ppermute(block, 'ref', [(i, i ^ offset) for i in range(size)])  10.2 us
    ppermute x2, starting transfers between devices, exchange_some(): return lax.ppermute(block, ('ref', 'win'), pairs)  3.09 us
    pallas_call x1, Pallas kernels, stage(): pl.pallas_call(stage_body, out_shape=(pltpu.VMEM(references.shape, narrow...  2.38 us
    ppermute x6, waiting for transfers between devices, exchange(): return lax.ppermute(block, 'ref', [(i, i ^ offset) for i in range(size)])  2.25 us
    pallas_call x1, Pallas kernels, pool_last(): pl.pallas_call(functools.partial(last_body, late, groups, sizes), out_sha...  0.84 us
    pallas_call x1, Pallas kernels, finish(): pl.pallas_call(functools.partial(finish_body, win, refs, windows), out_sh...  0.83 us
    pallas_call x1, Pallas kernels, pool(): pl.pallas_call(functools.partial(pool_body, sizes), out_shape=pltpu.VMEM(...  0.82 us
  transfers between devices with their start and end apart: 8, of which 2 were waited for; matrix products, arithmetic and copies ran while one was open for 0% of the time, Pallas kernels for 10%

profile of v8, /device:TPU:0, one launch (start us, length us, event | category | flops | bytes accessed | tf_op | source)
XLA Modules:
  0.0 32.4 jit_solution(3205962139663597260)
XLA Ops:
  0.0 5.0 %collective-permute-start.4 = (bf16[32,2048]{1,0:T(8,128)(2,1)}, bf16[32,2048]{1,0:T(8,128)(2,1)S(1)}, u32[]{:S(2)}, u32[]{:S(2)}) collective-permute-start(bf16[32,2048]{1,0:T(8,128)(2,1)} %queries_ref.1), channel_id=1, source_target_pairs={{0,24},{4,28},{8,16},{12,20},{16,8},{20,12},{24,0},{28,4},{1,25},{... | collective-permute-start | bytes 393224 | tf_op jit(solution)/shard_map/ppermute | solution.py:253
  5.0 0.0 collective-permute-start
  5.1 1.5 %collective-permute-start.2 = (bf16[32,2048]{1,0:T(8,128)(2,1)}, bf16[32,2048]{1,0:T(8,128)(2,1)S(1)}, u32[]{:S(2)}, u32[]{:S(2)}) collective-permute-start(bf16[32,2048]{1,0:T(8,128)(2,1)} %queries_ref.1), channel_id=1, source_target_pairs={{0,4},{4,0},{8,12},{12,8},{16,20},{20,16},{24,28},{28,24},{1,5},{5... | collective-permute-start | bytes 393224 | tf_op jit(solution)/shard_map/ppermute | solution.py:253
  6.5 2.4 %collective-permute-start.1 = (bf16[32,2048]{1,0:T(8,128)(2,1)}, bf16[32,2048]{1,0:T(8,128)(2,1)S(1)}, u32[]{:S(2)}, u32[]{:S(2)}) collective-permute-start(bf16[32,2048]{1,0:T(8,128)(2,1)} %queries_ref.1), channel_id=1, source_target_pairs={{0,20},{4,16},{8,28},{12,24},{16,4},{20,0},{24,12},{28,8},{2,22},{... | collective-permute-start | bytes 393224 | tf_op jit(solution)/shard_map/ppermute | solution.py:263
  9.0 0.6 %collective-permute-done.4.rest_3_ = bf16[32,2048]{1,0:T(8,128)(2,1)S(1)} collective-permute-done((bf16[32,2048]{1,0:T(8,128)(2,1)}, bf16[32,2048]{1,0:T(8,128)(2,1)S(1)}, u32[]{:S(2)}, u32[]{:S(2)}) %collective-permute-start.4) | collective-permute-done | bytes 131104 | tf_op jit(solution)/shard_map/ppermute | solution.py:253
  9.6 1.7 %collective-permute-start.5 = (bf16[32,2048]{1,0:T(8,128)(2,1)S(1)}, bf16[32,2048]{1,0:T(8,128)(2,1)S(1)}, u32[]{:S(2)}, u32[]{:S(2)}) collective-permute-start(bf16[32,2048]{1,0:T(8,128)(2,1)S(1)} %collective-permute-done.4.rest_3_), channel_id=1, source_target_pairs={{0,4},{4,0},{8,12},{12,8},{16,20},{20,16},{24,28},{28,24},{1,5},{5... | collective-permute-start | bytes 393224 | tf_op jit(solution)/shard_map/ppermute | solution.py:253
  11.3 1.4 %collective-permute-start.6 = (bf16[32,2048]{1,0:T(8,128)(2,1)S(1)}, bf16[32,2048]{1,0:T(8,128)(2,1)S(1)}, u32[]{:S(2)}, u32[]{:S(2)}) collective-permute-start(bf16[32,2048]{1,0:T(8,128)(2,1)S(1)} %collective-permute-done.4.rest_3_), channel_id=1, source_target_pairs={{0,8},{4,12},{8,0},{12,4},{16,24},{20,28},{24,16},{28,20},{1,9},{5... | collective-permute-start | bytes 393224 | tf_op jit(solution)/shard_map/ppermute | solution.py:253
  12.8 0.0 collective-permute-done._.rest_2_
  12.8 0.5 %collective-permute-start.7 = (bf16[32,2048]{1,0:T(8,128)(2,1)S(1)}, bf16[32,2048]{1,0:T(8,128)(2,1)S(1)}, u32[]{:S(2)}, u32[]{:S(2)}) collective-permute-start(bf16[32,2048]{1,0:T(8,128)(2,1)S(1)} %collective-permute-done._.rest_2_), channel_id=1, source_target_pairs={{0,4},{4,0},{8,12},{12,8},{16,20},{20,16},{24,28},{28,24},{1,5},{5... | collective-permute-start | bytes 393224 | tf_op jit(solution)/shard_map/ppermute | solution.py:253
  13.3 0.0 collective-permute-done.2.rest_1_
  13.3 0.7 %collective-permute-start.3 = (bf16[32,2048]{1,0:T(8,128)(2,1)S(1)}, bf16[32,2048]{1,0:T(8,128)(2,1)S(1)}, u32[]{:S(2)}, u32[]{:S(2)}) collective-permute-start(bf16[32,2048]{1,0:T(8,128)(2,1)S(1)} %collective-permute-done.2.rest_1_), channel_id=1, source_target_pairs={{1,17},{5,21},{9,25},{13,29},{17,1},{21,5},{25,9},{29,13},{3,19},{... | collective-permute-start | bytes 393224 | tf_op jit(solution)/shard_map/ppermute | solution.py:263
  14.0 2.4 %stage.1 = (f8e4m3fn[1024,2048]{1,0:T(32,128)(4,1)S(1)}, bf16[32,2048]{1,0:T(8,128)(2,1)S(1)}, f32[8,8,128]{2,1,0:T(8,128)S(1)}, f32[10,8,128]{2,1,0:T(8,128)S(1)}) custom-call(bf16[1024,2048]{1,0:T(8,128)(2,1)} %refs_ref.1, bf16[32,2048]{1,0:T(8,128)(2,1)} %queries_ref.1, s32[8]{0:T(128)} %labels_in.1, f32[8,9]{1,0:T(8,128)} %bitcast.4, f32[1,8]{1,0:T(1,128)} %bitcast.5, ...), custom_call_target="tpu_custom_call" | custom-call | flops 2097152 | bytes 6291456 | tf_op jit(solution)/shard_map/stage/pallas_call | solution.py:82
  16.4 0.8 %pool.1.rest_5_ = f32[4,8,128]{2,1,0:T(8,128)S(1)} custom-call(f32[8,8,128]{2,1,0:T(8,128)S(1)} %get-tuple-element.10.members_ref, f8e4m3fn[1024,2048]{1,0:T(32,128)(4,1)S(1)} %get-tuple-element.11.refs_ref, bf16[32,2048]{1,0:T(8,128)(2,1)S(1)} %get-tuple-element.12.rest_0_, bf16[32,2048]{1,0:T(8,128)(2,1)S(1)} %collective-permute-done.2.rest_1_, ...), custom_call_target="tpu_custom_call" | custom-call | flops 536870912 | bytes 2097152 | tf_op jit(solution)/shard_map/pool/pallas_call | solution.py:184
  17.2 0.0 collective-permute-done.1.rest_0_
  17.2 0.0 collective-permute-done.5.rest_2_
  17.2 0.0 collective-permute-done.6.rest_3_
  17.2 1.6 %collective-permute-done.7.rest_4_ = bf16[32,2048]{1,0:T(8,128)(2,1)S(1)} collective-permute-done((bf16[32,2048]{1,0:T(8,128)(2,1)S(1)}, bf16[32,2048]{1,0:T(8,128)(2,1)S(1)}, u32[]{:S(2)}, u32[]{:S(2)}) %collective-permute-start.7) | collective-permute-done | bytes 131104 | tf_op jit(solution)/shard_map/ppermute | solution.py:253
  18.8 0.0 collective-permute-done.3.rest_1_
  18.8 0.8 %pool_last.1 = f32[4,8,8,128]{3,2,1,0:T(8,128)S(1)} custom-call(f32[8,8,128]{2,1,0:T(8,128)S(1)} %get-tuple-element.10.members_ref, f8e4m3fn[1024,2048]{1,0:T(32,128)(4,1)S(1)} %get-tuple-element.11.refs_ref, bf16[32,2048]{1,0:T(8,128)(2,1)S(1)} %collective-permute-done.1.rest_0_, bf16[32,2048]{1,0:T(8,128)(2,1)S(1)} %collective-permute-done.3.rest_1_, ...), custom_call_target="tpu_custom_call" | custom-call | flops 536870912 | bytes 2097152 | tf_op jit(solution)/shard_map/pool_last/pallas_call | solution.py:199
  19.7 11.9 %all_to_all.5.in_ref = f32[32,8,128]{2,1,0:T(8,128)S(1)} all-to-all(f32[32,8,128]{2,1,0:T(8,128)S(1)} %bitcast.3), channel_id=1, replica_groups=mesh['ref'=8,'win'=4] {'win','ref'}, dimensions={0} | all-to-all | bytes 262144 | tf_op jit(solution)/shard_map/all_to_all | solution.py:305
  31.6 0.8 %finish.1 = f32[4,8,32]{2,1,0:T(8,128)} custom-call(f32[10,8,128]{2,1,0:T(8,128)S(1)} %get-tuple-element.9.consts_ref, f32[32,8,128]{2,1,0:T(8,128)S(1)} %all_to_all.5.in_ref), custom_call_target="tpu_custom_call" | custom-call | tf_op jit(solution)/shard_map/finish/pallas_call | solution.py:243
Async XLA Ops:
  0.0 9.6 %collective-permute-start.4 = (bf16[32,2048]{1,0:T(8,128)(2,1)}, bf16[32,2048]{1,0:T(8,128)(2,1)S(1)}, u32[]{:S(2)}, u32[]{:S(2)}) collective-permute-start(bf16[32,2048]{1,0:T(8,128)(2,1)} %queries_ref.1), channel_id=1, source_target_pairs={{0,24},{4,28},{8,16},{12,20},{16,8},{20,12},{24,0},{28,4},{1,25},{... | collective-permute-start | bytes 393224 | tf_op jit(solution)/shard_map/ppermute | solution.py:253
  5.0 7.7 %collective-permute-start = (bf16[32,2048]{1,0:T(8,128)(2,1)}, bf16[32,2048]{1,0:T(8,128)(2,1)S(1)}, u32[]{:S(2)}, u32[]{:S(2)}) collective-permute-start(bf16[32,2048]{1,0:T(8,128)(2,1)} %queries_ref.1), channel_id=1, source_target_pairs={{0,8},{4,12},{8,0},{12,4},{16,24},{20,28},{24,16},{28,20},{1,9},{5... | collective-permute-start | bytes 393224 | tf_op jit(solution)/shard_map/ppermute | solution.py:253
  5.1 8.3 %collective-permute-start.2 = (bf16[32,2048]{1,0:T(8,128)(2,1)}, bf16[32,2048]{1,0:T(8,128)(2,1)S(1)}, u32[]{:S(2)}, u32[]{:S(2)}) collective-permute-start(bf16[32,2048]{1,0:T(8,128)(2,1)} %queries_ref.1), channel_id=1, source_target_pairs={{0,4},{4,0},{8,12},{12,8},{16,20},{20,16},{24,28},{28,24},{1,5},{5... | collective-permute-start | bytes 393224 | tf_op jit(solution)/shard_map/ppermute | solution.py:253
  6.5 10.7 %collective-permute-start.1 = (bf16[32,2048]{1,0:T(8,128)(2,1)}, bf16[32,2048]{1,0:T(8,128)(2,1)S(1)}, u32[]{:S(2)}, u32[]{:S(2)}) collective-permute-start(bf16[32,2048]{1,0:T(8,128)(2,1)} %queries_ref.1), channel_id=1, source_target_pairs={{0,20},{4,16},{8,28},{12,24},{16,4},{20,0},{24,12},{28,8},{2,22},{... | collective-permute-start | bytes 393224 | tf_op jit(solution)/shard_map/ppermute | solution.py:263
  9.6 7.6 %collective-permute-start.5 = (bf16[32,2048]{1,0:T(8,128)(2,1)S(1)}, bf16[32,2048]{1,0:T(8,128)(2,1)S(1)}, u32[]{:S(2)}, u32[]{:S(2)}) collective-permute-start(bf16[32,2048]{1,0:T(8,128)(2,1)S(1)} %collective-permute-done.4.rest_3_), channel_id=1, source_target_pairs={{0,4},{4,0},{8,12},{12,8},{16,20},{20,16},{24,28},{28,24},{1,5},{5... | collective-permute-start | bytes 393224 | tf_op jit(solution)/shard_map/ppermute | solution.py:253
  11.3 5.9 %collective-permute-start.6 = (bf16[32,2048]{1,0:T(8,128)(2,1)S(1)}, bf16[32,2048]{1,0:T(8,128)(2,1)S(1)}, u32[]{:S(2)}, u32[]{:S(2)}) collective-permute-start(bf16[32,2048]{1,0:T(8,128)(2,1)S(1)} %collective-permute-done.4.rest_3_), channel_id=1, source_target_pairs={{0,8},{4,12},{8,0},{12,4},{16,24},{20,28},{24,16},{28,20},{1,9},{5... | collective-permute-start | bytes 393224 | tf_op jit(solution)/shard_map/ppermute | solution.py:253
  12.8 6.0 %collective-permute-start.7 = (bf16[32,2048]{1,0:T(8,128)(2,1)S(1)}, bf16[32,2048]{1,0:T(8,128)(2,1)S(1)}, u32[]{:S(2)}, u32[]{:S(2)}) collective-permute-start(bf16[32,2048]{1,0:T(8,128)(2,1)S(1)} %collective-permute-done._.rest_2_), channel_id=1, source_target_pairs={{0,4},{4,0},{8,12},{12,8},{16,20},{20,16},{24,28},{28,24},{1,5},{5... | collective-permute-start | bytes 393224 | tf_op jit(solution)/shard_map/ppermute | solution.py:253
  13.3 5.5 %collective-permute-start.3 = (bf16[32,2048]{1,0:T(8,128)(2,1)S(1)}, bf16[32,2048]{1,0:T(8,128)(2,1)S(1)}, u32[]{:S(2)}, u32[]{:S(2)}) collective-permute-start(bf16[32,2048]{1,0:T(8,128)(2,1)S(1)} %collective-permute-done.2.rest_1_), channel_id=1, source_target_pairs={{1,17},{5,21},{9,25},{13,29},{17,1},{21,5},{25,9},{29,13},{3,19},{... | collective-permute-start | bytes 393224 | tf_op jit(solution)/shard_map/ppermute | solution.py:263

commit v9 on v8

--- a/solution.py
+++ b/solution.py
@@ -294,7 +294,7 @@
         references, queries, labels, kernel, class_bias, blocks[2]
     )
     blocks[0] = mine
-    first = [0, 1, 2, refs - 2]
+    first = [1, 0, 2, refs - 2]
     rest = [k for k in blocks if k not in first]
     cut = len(rest) - LAST
     groups = [first] + [rest[k : k + LAST] for k in range(0, cut, LAST)]

time: 32.6 us -> 32.6 us (level)
  no operation moved by 1% of the time
where the time goes in v9:
time: 32.6 us; the launch traced here: 32.4 us
  starting transfers between devices  13.3 us (41%)
  blocking collectives  11.9 us (37%)
  Pallas kernels  4.87 us (15%)
  waiting for transfers between devices  2.26 us (7%)
    all_to_all x1, blocking collectives, per_device(): lax.all_to_all(sent, ('win', 'ref'), split_axis=0, concat_axis=0, tiled=T...  11.9 us
    ppermute x6, starting transfers between devices, exchange(): return lax.ppermute(block, 'ref', [(i, i ^ offset) for i in range(size)])  10.2 us
    ppermute x2, starting transfers between devices, exchange_some(): return lax.ppermute(block, ('ref', 'win'), pairs)  3.09 us
    pallas_call x1, Pallas kernels, stage(): pl.pallas_call(stage_body, out_shape=(pltpu.VMEM(references.shape, narrow...  2.38 us
    ppermute x6, waiting for transfers between devices, exchange(): return lax.ppermute(block, 'ref', [(i, i ^ offset) for i in range(size)])  2.25 us
    pallas_call x1, Pallas kernels, pool_last(): pl.pallas_call(functools.partial(last_body, late, groups, sizes), out_sha...  0.84 us
    pallas_call x1, Pallas kernels, finish(): pl.pallas_call(functools.partial(finish_body, win, refs, windows), out_sh...  0.83 us
    pallas_call x1, Pallas kernels, pool(): pl.pallas_call(functools.partial(pool_body, sizes), out_shape=pltpu.VMEM(...  0.82 us
  transfers between devices with their start and end apart: 8, of which 2 were waited for; matrix products, arithmetic and copies ran while one was open for 0% of the time, Pallas kernels for 10%

profile of v9, /device:TPU:0, one launch (start us, length us, event | category | flops | bytes accessed | tf_op | source)
XLA Modules:
  0.0 32.4 jit_solution(8979264724132916033)
XLA Ops:
  0.0 5.0 %collective-permute-start.4 = (bf16[32,2048]{1,0:T(8,128)(2,1)}, bf16[32,2048]{1,0:T(8,128)(2,1)S(1)}, u32[]{:S(2)}, u32[]{:S(2)}) collective-permute-start(bf16[32,2048]{1,0:T(8,128)(2,1)} %queries_ref.1), channel_id=1, source_target_pairs={{0,24},{4,28},{8,16},{12,20},{16,8},{20,12},{24,0},{28,4},{1,25},{... | collective-permute-start | bytes 393224 | tf_op jit(solution)/shard_map/ppermute | solution.py:253
  5.0 0.0 collective-permute-start
  5.1 1.5 %collective-permute-start.2 = (bf16[32,2048]{1,0:T(8,128)(2,1)}, bf16[32,2048]{1,0:T(8,128)(2,1)S(1)}, u32[]{:S(2)}, u32[]{:S(2)}) collective-permute-start(bf16[32,2048]{1,0:T(8,128)(2,1)} %queries_ref.1), channel_id=1, source_target_pairs={{0,4},{4,0},{8,12},{12,8},{16,20},{20,16},{24,28},{28,24},{1,5},{5... | collective-permute-start | bytes 393224 | tf_op jit(solution)/shard_map/ppermute | solution.py:253
  6.5 2.4 %collective-permute-start.1 = (bf16[32,2048]{1,0:T(8,128)(2,1)}, bf16[32,2048]{1,0:T(8,128)(2,1)S(1)}, u32[]{:S(2)}, u32[]{:S(2)}) collective-permute-start(bf16[32,2048]{1,0:T(8,128)(2,1)} %queries_ref.1), channel_id=1, source_target_pairs={{0,20},{4,16},{8,28},{12,24},{16,4},{20,0},{24,12},{28,8},{2,22},{... | collective-permute-start | bytes 393224 | tf_op jit(solution)/shard_map/ppermute | solution.py:263
  9.0 0.6 %collective-permute-done.4.rest_3_ = bf16[32,2048]{1,0:T(8,128)(2,1)S(1)} collective-permute-done((bf16[32,2048]{1,0:T(8,128)(2,1)}, bf16[32,2048]{1,0:T(8,128)(2,1)S(1)}, u32[]{:S(2)}, u32[]{:S(2)}) %collective-permute-start.4) | collective-permute-done | bytes 131104 | tf_op jit(solution)/shard_map/ppermute | solution.py:253
  9.6 1.7 %collective-permute-start.5 = (bf16[32,2048]{1,0:T(8,128)(2,1)S(1)}, bf16[32,2048]{1,0:T(8,128)(2,1)S(1)}, u32[]{:S(2)}, u32[]{:S(2)}) collective-permute-start(bf16[32,2048]{1,0:T(8,128)(2,1)S(1)} %collective-permute-done.4.rest_3_), channel_id=1, source_target_pairs={{0,4},{4,0},{8,12},{12,8},{16,20},{20,16},{24,28},{28,24},{1,5},{5... | collective-permute-start | bytes 393224 | tf_op jit(solution)/shard_map/ppermute | solution.py:253
  11.3 1.4 %collective-permute-start.6 = (bf16[32,2048]{1,0:T(8,128)(2,1)S(1)}, bf16[32,2048]{1,0:T(8,128)(2,1)S(1)}, u32[]{:S(2)}, u32[]{:S(2)}) collective-permute-start(bf16[32,2048]{1,0:T(8,128)(2,1)S(1)} %collective-permute-done.4.rest_3_), channel_id=1, source_target_pairs={{0,8},{4,12},{8,0},{12,4},{16,24},{20,28},{24,16},{28,20},{1,9},{5... | collective-permute-start | bytes 393224 | tf_op jit(solution)/shard_map/ppermute | solution.py:253
  12.8 0.0 collective-permute-done._.rest_2_
  12.8 0.5 %collective-permute-start.7 = (bf16[32,2048]{1,0:T(8,128)(2,1)S(1)}, bf16[32,2048]{1,0:T(8,128)(2,1)S(1)}, u32[]{:S(2)}, u32[]{:S(2)}) collective-permute-start(bf16[32,2048]{1,0:T(8,128)(2,1)S(1)} %collective-permute-done._.rest_2_), channel_id=1, source_target_pairs={{0,4},{4,0},{8,12},{12,8},{16,20},{20,16},{24,28},{28,24},{1,5},{5... | collective-permute-start | bytes 393224 | tf_op jit(solution)/shard_map/ppermute | solution.py:253
  13.3 0.0 collective-permute-done.2.rest_0_
  13.3 0.7 %collective-permute-start.3 = (bf16[32,2048]{1,0:T(8,128)(2,1)S(1)}, bf16[32,2048]{1,0:T(8,128)(2,1)S(1)}, u32[]{:S(2)}, u32[]{:S(2)}) collective-permute-start(bf16[32,2048]{1,0:T(8,128)(2,1)S(1)} %collective-permute-done.2.rest_0_), channel_id=1, source_target_pairs={{1,17},{5,21},{9,25},{13,29},{17,1},{21,5},{25,9},{29,13},{3,19},{... | collective-permute-start | bytes 393224 | tf_op jit(solution)/shard_map/ppermute | solution.py:263
  14.0 2.4 %stage.1 = (f8e4m3fn[1024,2048]{1,0:T(32,128)(4,1)S(1)}, bf16[32,2048]{1,0:T(8,128)(2,1)S(1)}, f32[8,8,128]{2,1,0:T(8,128)S(1)}, f32[10,8,128]{2,1,0:T(8,128)S(1)}) custom-call(bf16[1024,2048]{1,0:T(8,128)(2,1)} %refs_ref.1, bf16[32,2048]{1,0:T(8,128)(2,1)} %queries_ref.1, s32[8]{0:T(128)} %labels_in.1, f32[8,9]{1,0:T(8,128)} %bitcast.4, f32[1,8]{1,0:T(1,128)} %bitcast.5, ...), custom_call_target="tpu_custom_call" | custom-call | flops 2097152 | bytes 6291456 | tf_op jit(solution)/shard_map/stage/pallas_call | solution.py:82
  16.4 0.8 %pool.1.rest_5_ = f32[4,8,128]{2,1,0:T(8,128)S(1)} custom-call(f32[8,8,128]{2,1,0:T(8,128)S(1)} %get-tuple-element.10.members_ref, f8e4m3fn[1024,2048]{1,0:T(32,128)(4,1)S(1)} %get-tuple-element.11.refs_ref, bf16[32,2048]{1,0:T(8,128)(2,1)S(1)} %collective-permute-done.2.rest_0_, bf16[32,2048]{1,0:T(8,128)(2,1)S(1)} %get-tuple-element.12.rest_1_, ...), custom_call_target="tpu_custom_call" | custom-call | flops 536870912 | bytes 2097152 | tf_op jit(solution)/shard_map/pool/pallas_call | solution.py:184
  17.2 0.0 collective-permute-done.1.rest_0_
  17.2 0.0 collective-permute-done.5.rest_2_
  17.2 0.0 collective-permute-done.6.rest_3_
  17.2 1.6 %collective-permute-done.7.rest_4_ = bf16[32,2048]{1,0:T(8,128)(2,1)S(1)} collective-permute-done((bf16[32,2048]{1,0:T(8,128)(2,1)S(1)}, bf16[32,2048]{1,0:T(8,128)(2,1)S(1)}, u32[]{:S(2)}, u32[]{:S(2)}) %collective-permute-start.7) | collective-permute-done | bytes 131104 | tf_op jit(solution)/shard_map/ppermute | solution.py:253
  18.8 0.0 collective-permute-done.3.rest_1_
  18.8 0.8 %pool_last.1 = f32[4,8,8,128]{3,2,1,0:T(8,128)S(1)} custom-call(f32[8,8,128]{2,1,0:T(8,128)S(1)} %get-tuple-element.10.members_ref, f8e4m3fn[1024,2048]{1,0:T(32,128)(4,1)S(1)} %get-tuple-element.11.refs_ref, bf16[32,2048]{1,0:T(8,128)(2,1)S(1)} %collective-permute-done.1.rest_0_, bf16[32,2048]{1,0:T(8,128)(2,1)S(1)} %collective-permute-done.3.rest_1_, ...), custom_call_target="tpu_custom_call" | custom-call | flops 536870912 | bytes 2097152 | tf_op jit(solution)/shard_map/pool_last/pallas_call | solution.py:199
  19.7 11.9 %all_to_all.5.in_ref = f32[32,8,128]{2,1,0:T(8,128)S(1)} all-to-all(f32[32,8,128]{2,1,0:T(8,128)S(1)} %bitcast.3), channel_id=1, replica_groups=mesh['ref'=8,'win'=4] {'win','ref'}, dimensions={0} | all-to-all | bytes 262144 | tf_op jit(solution)/shard_map/all_to_all | solution.py:305
  31.6 0.8 %finish.1 = f32[4,8,32]{2,1,0:T(8,128)} custom-call(f32[10,8,128]{2,1,0:T(8,128)S(1)} %get-tuple-element.9.consts_ref, f32[32,8,128]{2,1,0:T(8,128)S(1)} %all_to_all.5.in_ref), custom_call_target="tpu_custom_call" | custom-call | tf_op jit(solution)/shard_map/finish/pallas_call | solution.py:243
Async XLA Ops:
  0.0 9.6 %collective-permute-start.4 = (bf16[32,2048]{1,0:T(8,128)(2,1)}, bf16[32,2048]{1,0:T(8,128)(2,1)S(1)}, u32[]{:S(2)}, u32[]{:S(2)}) collective-permute-start(bf16[32,2048]{1,0:T(8,128)(2,1)} %queries_ref.1), channel_id=1, source_target_pairs={{0,24},{4,28},{8,16},{12,20},{16,8},{20,12},{24,0},{28,4},{1,25},{... | collective-permute-start | bytes 393224 | tf_op jit(solution)/shard_map/ppermute | solution.py:253
  5.0 7.7 %collective-permute-start = (bf16[32,2048]{1,0:T(8,128)(2,1)}, bf16[32,2048]{1,0:T(8,128)(2,1)S(1)}, u32[]{:S(2)}, u32[]{:S(2)}) collective-permute-start(bf16[32,2048]{1,0:T(8,128)(2,1)} %queries_ref.1), channel_id=1, source_target_pairs={{0,8},{4,12},{8,0},{12,4},{16,24},{20,28},{24,16},{28,20},{1,9},{5... | collective-permute-start | bytes 393224 | tf_op jit(solution)/shard_map/ppermute | solution.py:253
  5.1 8.3 %collective-permute-start.2 = (bf16[32,2048]{1,0:T(8,128)(2,1)}, bf16[32,2048]{1,0:T(8,128)(2,1)S(1)}, u32[]{:S(2)}, u32[]{:S(2)}) collective-permute-start(bf16[32,2048]{1,0:T(8,128)(2,1)} %queries_ref.1), channel_id=1, source_target_pairs={{0,4},{4,0},{8,12},{12,8},{16,20},{20,16},{24,28},{28,24},{1,5},{5... | collective-permute-start | bytes 393224 | tf_op jit(solution)/shard_map/ppermute | solution.py:253
  6.5 10.7 %collective-permute-start.1 = (bf16[32,2048]{1,0:T(8,128)(2,1)}, bf16[32,2048]{1,0:T(8,128)(2,1)S(1)}, u32[]{:S(2)}, u32[]{:S(2)}) collective-permute-start(bf16[32,2048]{1,0:T(8,128)(2,1)} %queries_ref.1), channel_id=1, source_target_pairs={{0,20},{4,16},{8,28},{12,24},{16,4},{20,0},{24,12},{28,8},{2,22},{... | collective-permute-start | bytes 393224 | tf_op jit(solution)/shard_map/ppermute | solution.py:263
  9.6 7.6 %collective-permute-start.5 = (bf16[32,2048]{1,0:T(8,128)(2,1)S(1)}, bf16[32,2048]{1,0:T(8,128)(2,1)S(1)}, u32[]{:S(2)}, u32[]{:S(2)}) collective-permute-start(bf16[32,2048]{1,0:T(8,128)(2,1)S(1)} %collective-permute-done.4.rest_3_), channel_id=1, source_target_pairs={{0,4},{4,0},{8,12},{12,8},{16,20},{20,16},{24,28},{28,24},{1,5},{5... | collective-permute-start | bytes 393224 | tf_op jit(solution)/shard_map/ppermute | solution.py:253
  11.3 5.9 %collective-permute-start.6 = (bf16[32,2048]{1,0:T(8,128)(2,1)S(1)}, bf16[32,2048]{1,0:T(8,128)(2,1)S(1)}, u32[]{:S(2)}, u32[]{:S(2)}) collective-permute-start(bf16[32,2048]{1,0:T(8,128)(2,1)S(1)} %collective-permute-done.4.rest_3_), channel_id=1, source_target_pairs={{0,8},{4,12},{8,0},{12,4},{16,24},{20,28},{24,16},{28,20},{1,9},{5... | collective-permute-start | bytes 393224 | tf_op jit(solution)/shard_map/ppermute | solution.py:253
  12.8 6.0 %collective-permute-start.7 = (bf16[32,2048]{1,0:T(8,128)(2,1)S(1)}, bf16[32,2048]{1,0:T(8,128)(2,1)S(1)}, u32[]{:S(2)}, u32[]{:S(2)}) collective-permute-start(bf16[32,2048]{1,0:T(8,128)(2,1)S(1)} %collective-permute-done._.rest_2_), channel_id=1, source_target_pairs={{0,4},{4,0},{8,12},{12,8},{16,20},{20,16},{24,28},{28,24},{1,5},{5... | collective-permute-start | bytes 393224 | tf_op jit(solution)/shard_map/ppermute | solution.py:253
  13.3 5.5 %collective-permute-start.3 = (bf16[32,2048]{1,0:T(8,128)(2,1)S(1)}, bf16[32,2048]{1,0:T(8,128)(2,1)S(1)}, u32[]{:S(2)}, u32[]{:S(2)}) collective-permute-start(bf16[32,2048]{1,0:T(8,128)(2,1)S(1)} %collective-permute-done.2.rest_0_), channel_id=1, source_target_pairs={{1,17},{5,21},{9,25},{13,29},{17,1},{21,5},{25,9},{29,13},{3,19},{... | collective-permute-start | bytes 393224 | tf_op jit(solution)/shard_map/ppermute | solution.py:263
